TPU v7x, 32 devices: a whole 2x2x4 slice. The times are simulated.
32 devices in a mesh: sector: 4 (over z), dir: 8 (over y, x, core).
Axes of the slice: x: 2, y: 2, z: 4, core: 2. Of those that a mesh axis runs over, the one named last changes fastest.
Arguments:
- fields: bfloat16 [1024, 128, 128], P(('sector', 'dir')), may hold values from -6 to 6
- aggregation: bfloat16 [64, 256], replicated, may hold values from -0.375 to 0.375
- operators: bfloat16 [64, 64, 64, 128], P(None, 'dir'), may hold values from -0.09375 to 0.09375
- disaggregation: bfloat16 [128, 128], replicated, may hold values from -0.5 to 0.5
- near_tile: int32 [16, 16], P('sector'), may hold values from 0 to 3
- near_operator: int32 [16, 16], P('sector'), may hold values from 0 to 63
- far_slot: int32 [16, 16], P('sector'), may hold values from 0 to 7, as said below
- far_operator: int32 [16, 16], P('sector'), may hold values from 0 to 63
- send_tiles: int32 [4, 4, 2], replicated, may hold values from 0 to 3, as said below
Outputs:
- scattered: bfloat16 [1024, 128, 128], P(('sector', 'dir'))
Inputs may be any that keep to these rules, and one draw needn't show every extreme that they name: `send_tiles`: for every source and target sector the 2 entries are distinct tile numbers within the source sector. `far_slot`: entry c * 2 + j names slot j of the list that sector c keeps for the target tile's sector; c is never the target tile's own sector.
All inputs are finite; a program needn't handle non-finite values.
Results may differ from a plain program's by a relative error of at most 0.0058.
Values may be sent and summed in bfloat16 or wider, within the bound.
No kernel may reach another device: no remote copies, remote signals or barrier semaphores. Data moves between devices by JAX's collectives and lax.ppermute only.
A program may use at most 128 MiB of HBM per device.

v0:
```python
import jax
import jax.numpy as jnp
from jax import lax
from jax.sharding import PartitionSpec as P


def combine(first, second):
    halfway = first.shape[-1] // 2
    real_part = first[..., :halfway] - second[..., halfway:]
    imag_part = first[..., halfway:] + second[..., :halfway]
    return jnp.concatenate([real_part, imag_part], axis=-1)


def local(
    fields,
    aggregation,
    operators,
    disaggregation,
    near_tile,
    near_operator,
    far_slot,
    far_operator,
    send_tiles,
):
    dirs_here = operators.shape[1]
    tile_rows = operators.shape[2]
    tiles_here = near_tile.shape[0]
    columns = fields.shape[2]
    unknowns = aggregation.shape[1] // 2
    all_dirs = disaggregation.shape[1] // 2
    first = jnp.einsum(
        "kq,bqc->kbc", aggregation[:, :unknowns], fields, preferred_element_type=jnp.float32
    )
    second = jnp.einsum(
        "kq,bqc->kbc", aggregation[:, unknowns:], fields, preferred_element_type=jnp.float32
    )
    outgoing = combine(first, second).astype(jnp.bfloat16)
    slab = lax.all_to_all(outgoing, "dir", split_axis=0, concat_axis=1, tiled=True)
    own_tiles = slab.reshape(dirs_here, tiles_here, tile_rows, columns)
    sector_now = lax.axis_index("sector")
    listing = lax.dynamic_index_in_dim(send_tiles, sector_now, 0, keepdims=False)
    leaving = own_tiles[:, listing.reshape(-1)]
    far_pool = lax.all_to_all(leaving, "sector", split_axis=1, concat_axis=1, tiled=True)

    def apply_ops(op_here, pool_here, tile_index, op_index):
        sources = pool_here[tile_index]
        blocks = op_here[op_index]
        blocks = blocks.reshape(blocks.shape[0], blocks.shape[1], tile_rows, 2, tile_rows)
        return jnp.einsum("tlarb,tlbc->rtac", blocks, sources, preferred_element_type=jnp.float32)

    def per_direction(direction):
        op_here = lax.dynamic_index_in_dim(operators, direction, 1, keepdims=False)
        own_here = lax.dynamic_index_in_dim(own_tiles, direction, 0, keepdims=False)
        far_here = lax.dynamic_index_in_dim(far_pool, direction, 0, keepdims=False)
        total = apply_ops(op_here, own_here, near_tile, near_operator) + apply_ops(
            op_here, far_here, far_slot, far_operator
        )
        return combine(total[0], total[1]).astype(jnp.bfloat16)

    incoming = lax.map(per_direction, jnp.arange(dirs_here, dtype=jnp.int32))
    returned = lax.all_to_all(
        incoming.reshape(dirs_here, tiles_here * tile_rows, columns),
        "dir",
        split_axis=1,
        concat_axis=0,
        tiled=True,
    )
    first_back = jnp.einsum(
        "qk,kbc->bqc", disaggregation[:, :all_dirs], returned, preferred_element_type=jnp.float32
    )
    second_back = jnp.einsum(
        "qk,kbc->bqc", disaggregation[:, all_dirs:], returned, preferred_element_type=jnp.float32
    )
    return combine(first_back, second_back).astype(jnp.bfloat16)


def solution(mesh):
    placed = (
        P(("sector", "dir"), None, None),
        P(),
        P(None, "dir", None, None),
        P(),
        P("sector", None),
        P("sector", None),
        P("sector", None),
        P("sector", None),
        P(),
    )
    return jax.shard_map(
        local,
        mesh=mesh,
        in_specs=placed,
        out_specs=P(("sector", "dir"), None, None),
        check_vma=False,
    )
```

profile of v0, /device:TPU:0, one launch (start us, length us, event | category | flops | bytes accessed | tf_op | source)
XLA Modules:
  0.0 225.6 jit_solution(10468016917287568439)
XLA Ops:
  4.6 5.2 %all-to-all-start = ((bf16[64,32,128]{2,1,0:T(8,128)(2,1)}), bf16[64,32,128]{2,1,0:T(8,128)(2,1)S(1)}, u32[]{:S(2)}, u32[]{:S(2)}) async-start(bf16[64,32,128]{2,1,0:T(8,128)(2,1)} %copy.29), calls=%async_computation | async-start | bytes 1048576 | tf_op jit(solution)/shard_map/all_to_all | solution.py:38
  10.7 8.9 %all-to-all-done = bf16[64,32,128]{2,1,0:T(8,128)(2,1)S(1)} async-done(((bf16[64,32,128]{2,1,0:T(8,128)(2,1)}), bf16[64,32,128]{2,1,0:T(8,128)(2,1)S(1)}, u32[]{:S(2)}, u32[]{:S(2)}) %all-to-all-start) | async-done | bytes 524320 | tf_op jit(solution)/shard_map/all_to_all | solution.py:38
  20.4 2.7 %gather_fusion.4 = bf16[8,8,64,128]{3,2,1,0:T(8,128)(2,1)} fusion(bf16[8,4,64,128]{3,2,1,0:T(8,128)(2,1)} %bitcast.27, s32[1024]{0:T(1024)S(1)} %pad_clamp_fusion.4), kind=kCustom, calls=%fused_computation.4 | custom fusion | bytes 2097184 | tf_op jit(solution)/shard_map/gather | solution.py:42
  23.1 4.9 %all-to-all-start.1 = ((bf16[8,8,64,128]{3,2,0,1:T(8,128)(2,1)}), bf16[8,8,64,128]{3,2,0,1:T(8,128)(2,1)}, u32[]{:S(2)}, u32[]{:S(2)}) async-start(bf16[8,8,64,128]{3,2,0,1:T(8,128)(2,1)} %bitcast.30), calls=%async_computation.1 | async-start | bytes 2097152 | tf_op jit(solution)/shard_map/all_to_all | solution.py:43
  28.0 23.5 %all-to-all-done.1 = bf16[8,8,64,128]{3,2,0,1:T(8,128)(2,1)} async-done(((bf16[8,8,64,128]{3,2,0,1:T(8,128)(2,1)}), bf16[8,8,64,128]{3,2,0,1:T(8,128)(2,1)}, u32[]{:S(2)}, u32[]{:S(2)}) %all-to-all-start.1) | async-done | bytes 1048608 | tf_op jit(solution)/shard_map/all_to_all | solution.py:43
  51.5 155.9 %while.10 = (s32[]{:T(128)}, bf16[8,4,64,128]{3,2,1,0:T(8,128)(2,1)}, s32[8]{0:T(128)S(1)}, bf16[8,4,64,128]{3,2,1,0:T(8,128)(2,1)}, s32[4,16]{1,0:T(4,128)S(1)}...) while((s32[]{:T(128)}, ...), condition=%wide.region_1.2_spmd, body=%wide.region_0.1_spmd.sunk | while | flops 268702464 | bytes 25254612 | solution.py:60
  56.2 1.9 reshape.217
  59.8 2.9 %fusion.54 = f32[4,128,64,2]{1,2,3,0:T(8,128)} fusion(bf16[4,16,64,128,1]{3,2,1,4,0:T(8,128)(2,1)S(1)} %bitcast.126, bf16[4,16,64,2,64]{4,3,2,1,0:T(2,128)(2,1)} %reshape.217), kind=kOutput, calls=%fused_computation.9.clone.1 | convolution fusion | flops 134217728 | bytes 2359296 | tf_op jit(solution)/shard_map/while/body/eval_jaxpr/tlarb,tlbc->rtac/dot_general | solution.py:49
  63.5 1.9 reshape.220
  66.6 1.7 gather_fusion.2
  68.2 1.9 fusion.55
  75.7 1.9 reshape.217
  79.2 2.9 %fusion.54 = f32[4,128,64,2]{1,2,3,0:T(8,128)} fusion(bf16[4,16,64,128,1]{3,2,1,4,0:T(8,128)(2,1)S(1)} %bitcast.126, bf16[4,16,64,2,64]{4,3,2,1,0:T(2,128)(2,1)} %reshape.217), kind=kOutput, calls=%fused_computation.9.clone.1 | convolution fusion | flops 134217728 | bytes 2359296 | tf_op jit(solution)/shard_map/while/body/eval_jaxpr/tlarb,tlbc->rtac/dot_general | solution.py:49
  83.0 1.9 reshape.220
  86.0 1.7 gather_fusion.2
  87.7 1.9 fusion.55
  95.2 1.9 reshape.217
  98.7 2.9 %fusion.54 = f32[4,128,64,2]{1,2,3,0:T(8,128)} fusion(bf16[4,16,64,128,1]{3,2,1,4,0:T(8,128)(2,1)S(1)} %bitcast.126, bf16[4,16,64,2,64]{4,3,2,1,0:T(2,128)(2,1)} %reshape.217), kind=kOutput, calls=%fused_computation.9.clone.1 | convolution fusion | flops 134217728 | bytes 2359296 | tf_op jit(solution)/shard_map/while/body/eval_jaxpr/tlarb,tlbc->rtac/dot_general | solution.py:49
  102.5 1.9 reshape.220
  105.5 1.7 gather_fusion.2
  107.2 1.9 fusion.55
  114.7 1.9 reshape.217
  118.2 2.9 %fusion.54 = f32[4,128,64,2]{1,2,3,0:T(8,128)} fusion(bf16[4,16,64,128,1]{3,2,1,4,0:T(8,128)(2,1)S(1)} %bitcast.126, bf16[4,16,64,2,64]{4,3,2,1,0:T(2,128)(2,1)} %reshape.217), kind=kOutput, calls=%fused_computation.9.clone.1 | convolution fusion | flops 134217728 | bytes 2359296 | tf_op jit(solution)/shard_map/while/body/eval_jaxpr/tlarb,tlbc->rtac/dot_general | solution.py:49
  122.0 1.9 reshape.220
  125.0 1.7 gather_fusion.2
  126.7 1.9 fusion.55
  134.2 1.9 reshape.217
  137.7 2.9 %fusion.54 = f32[4,128,64,2]{1,2,3,0:T(8,128)} fusion(bf16[4,16,64,128,1]{3,2,1,4,0:T(8,128)(2,1)S(1)} %bitcast.126, bf16[4,16,64,2,64]{4,3,2,1,0:T(2,128)(2,1)} %reshape.217), kind=kOutput, calls=%fused_computation.9.clone.1 | convolution fusion | flops 134217728 | bytes 2359296 | tf_op jit(solution)/shard_map/while/body/eval_jaxpr/tlarb,tlbc->rtac/dot_general | solution.py:49
  141.5 1.9 reshape.220
  144.5 1.7 gather_fusion.2
  146.2 1.9 fusion.55
  153.6 1.9 reshape.217
  157.2 2.9 %fusion.54 = f32[4,128,64,2]{1,2,3,0:T(8,128)} fusion(bf16[4,16,64,128,1]{3,2,1,4,0:T(8,128)(2,1)S(1)} %bitcast.126, bf16[4,16,64,2,64]{4,3,2,1,0:T(2,128)(2,1)} %reshape.217), kind=kOutput, calls=%fused_computation.9.clone.1 | convolution fusion | flops 134217728 | bytes 2359296 | tf_op jit(solution)/shard_map/while/body/eval_jaxpr/tlarb,tlbc->rtac/dot_general | solution.py:49
  161.0 1.9 reshape.220
  164.0 1.7 gather_fusion.2
  165.6 1.9 fusion.55
  173.1 1.9 reshape.217
  176.7 2.9 %fusion.54 = f32[4,128,64,2]{1,2,3,0:T(8,128)} fusion(bf16[4,16,64,128,1]{3,2,1,4,0:T(8,128)(2,1)S(1)} %bitcast.126, bf16[4,16,64,2,64]{4,3,2,1,0:T(2,128)(2,1)} %reshape.217), kind=kOutput, calls=%fused_computation.9.clone.1 | convolution fusion | flops 134217728 | bytes 2359296 | tf_op jit(solution)/shard_map/while/body/eval_jaxpr/tlarb,tlbc->rtac/dot_general | solution.py:49
  180.5 1.9 reshape.220
  183.5 1.7 gather_fusion.2
  185.1 1.9 fusion.55
  192.6 1.9 reshape.217
  196.2 2.9 %fusion.54 = f32[4,128,64,2]{1,2,3,0:T(8,128)} fusion(bf16[4,16,64,128,1]{3,2,1,4,0:T(8,128)(2,1)S(1)} %bitcast.126, bf16[4,16,64,2,64]{4,3,2,1,0:T(2,128)(2,1)} %reshape.217), kind=kOutput, calls=%fused_computation.9.clone.1 | convolution fusion | flops 134217728 | bytes 2359296 | tf_op jit(solution)/shard_map/while/body/eval_jaxpr/tlarb,tlbc->rtac/dot_general | solution.py:49
  199.9 1.9 reshape.220
  202.9 1.7 gather_fusion.2
  204.6 1.9 fusion.55
  207.4 1.4 copy.33
  208.8 14.0 %all_to_all.38 = bf16[8,256,128]{2,0,1:T(8,128)(2,1)S(1)} all-to-all(bf16[8,256,128]{2,0,1:T(8,128)(2,1)S(1)} %bitcast.130), channel_id=1, replica_groups=mesh['sector'=4,'dir'=8] {'dir'}, dimensions={1} | all-to-all | bytes 1048576 | tf_op jit(solution)/shard_map/all_to_all | solution.py:61
  (208 shorter events, 67.6 us)
Async XLA Ops:
  0.0 1.2 copy-start
  0.0 2.2 copy-start.7
  4.6 14.9 %all-to-all-start = ((bf16[64,32,128]{2,1,0:T(8,128)(2,1)}), bf16[64,32,128]{2,1,0:T(8,128)(2,1)S(1)}, u32[]{:S(2)}, u32[]{:S(2)}) async-start(bf16[64,32,128]{2,1,0:T(8,128)(2,1)} %copy.29), calls=%async_computation | async-start | bytes 1048576 | tf_op jit(solution)/shard_map/all_to_all | solution.py:38
  20.4 31.1 %copy-start.3 = (s32[4,16]{1,0:T(4,128)S(1)}, s32[4,16]{1,0:T(4,128)}, u32[]{:S(2)}) copy-start(s32[4,16]{1,0:T(4,128)} %param.15) | copy-start | bytes 772
  20.4 31.1 %copy-start.4 = (s32[4,16]{1,0:T(4,128)S(1)}, s32[4,16]{1,0:T(4,128)}, u32[]{:S(2)}) copy-start(s32[4,16]{1,0:T(4,128)} %param.16) | copy-start | bytes 772
  20.4 31.1 %copy-start.5 = (s32[4,16]{1,0:T(4,128)S(1)}, s32[4,16]{1,0:T(4,128)}, u32[]{:S(2)}) copy-start(s32[4,16]{1,0:T(4,128)} %param.17) | copy-start | bytes 772
  20.4 31.1 %copy-start.6 = (s32[4,16]{1,0:T(4,128)S(1)}, s32[4,16]{1,0:T(4,128)}, u32[]{:S(2)}) copy-start(s32[4,16]{1,0:T(4,128)} %param.18) | copy-start | bytes 772
  23.1 28.4 %all-to-all-start.1 = ((bf16[8,8,64,128]{3,2,0,1:T(8,128)(2,1)}), bf16[8,8,64,128]{3,2,0,1:T(8,128)(2,1)}, u32[]{:S(2)}, u32[]{:S(2)}) async-start(bf16[8,8,64,128]{3,2,0,1:T(8,128)(2,1)} %bitcast.30), calls=%async_computation.1 | async-start | bytes 2097152 | tf_op jit(solution)/shard_map/all_to_all | solution.py:43
  65.4 2.8 %copy-start.1 = (bf16[4,16,64,2,64]{4,3,2,1,0:T(2,128)(2,1)S(1)}, bf16[4,16,64,2,64]{4,3,2,1,0:T(2,128)(2,1)}, u32[]{:S(2)}) copy-start(bf16[4,16,64,2,64]{4,3,2,1,0:T(2,128)(2,1)} %reshape.220) | copy-start | bytes 3145732 | tf_op jit(solution)/shard_map/while
  84.9 2.8 %copy-start.1 = (bf16[4,16,64,2,64]{4,3,2,1,0:T(2,128)(2,1)S(1)}, bf16[4,16,64,2,64]{4,3,2,1,0:T(2,128)(2,1)}, u32[]{:S(2)}) copy-start(bf16[4,16,64,2,64]{4,3,2,1,0:T(2,128)(2,1)} %reshape.220) | copy-start | bytes 3145732 | tf_op jit(solution)/shard_map/while
  104.4 2.8 %copy-start.1 = (bf16[4,16,64,2,64]{4,3,2,1,0:T(2,128)(2,1)S(1)}, bf16[4,16,64,2,64]{4,3,2,1,0:T(2,128)(2,1)}, u32[]{:S(2)}) copy-start(bf16[4,16,64,2,64]{4,3,2,1,0:T(2,128)(2,1)} %reshape.220) | copy-start | bytes 3145732 | tf_op jit(solution)/shard_map/while
  123.9 2.8 %copy-start.1 = (bf16[4,16,64,2,64]{4,3,2,1,0:T(2,128)(2,1)S(1)}, bf16[4,16,64,2,64]{4,3,2,1,0:T(2,128)(2,1)}, u32[]{:S(2)}) copy-start(bf16[4,16,64,2,64]{4,3,2,1,0:T(2,128)(2,1)} %reshape.220) | copy-start | bytes 3145732 | tf_op jit(solution)/shard_map/while
  143.4 2.8 %copy-start.1 = (bf16[4,16,64,2,64]{4,3,2,1,0:T(2,128)(2,1)S(1)}, bf16[4,16,64,2,64]{4,3,2,1,0:T(2,128)(2,1)}, u32[]{:S(2)}) copy-start(bf16[4,16,64,2,64]{4,3,2,1,0:T(2,128)(2,1)} %reshape.220) | copy-start | bytes 3145732 | tf_op jit(solution)/shard_map/while
  162.8 2.8 %copy-start.1 = (bf16[4,16,64,2,64]{4,3,2,1,0:T(2,128)(2,1)S(1)}, bf16[4,16,64,2,64]{4,3,2,1,0:T(2,128)(2,1)}, u32[]{:S(2)}) copy-start(bf16[4,16,64,2,64]{4,3,2,1,0:T(2,128)(2,1)} %reshape.220) | copy-start | bytes 3145732 | tf_op jit(solution)/shard_map/while
  182.3 2.8 %copy-start.1 = (bf16[4,16,64,2,64]{4,3,2,1,0:T(2,128)(2,1)S(1)}, bf16[4,16,64,2,64]{4,3,2,1,0:T(2,128)(2,1)}, u32[]{:S(2)}) copy-start(bf16[4,16,64,2,64]{4,3,2,1,0:T(2,128)(2,1)} %reshape.220) | copy-start | bytes 3145732 | tf_op jit(solution)/shard_map/while
  201.8 2.8 %copy-start.1 = (bf16[4,16,64,2,64]{4,3,2,1,0:T(2,128)(2,1)S(1)}, bf16[4,16,64,2,64]{4,3,2,1,0:T(2,128)(2,1)}, u32[]{:S(2)}) copy-start(bf16[4,16,64,2,64]{4,3,2,1,0:T(2,128)(2,1)} %reshape.220) | copy-start | bytes 3145732 | tf_op jit(solution)/shard_map/while
  207.4 15.4 %copy-start.2 = (bf16[128,128]{1,0:T(8,128)(2,1)S(1)}, bf16[128,128]{1,0:T(8,128)(2,1)}, u32[]{:S(2)}) copy-start(bf16[128,128]{1,0:T(8,128)(2,1)} %param.14) | copy-start | bytes 98308
where the time goes:
time: 228 us; the launch traced here: 226 us
  local copies, waits for them, and re-layouts  104 us (46%)
  matrix products  40.8 us (18%)
  waiting for transfers between devices  32.3 us (14%)
  loops' own time  16.1 us (7%)
  blocking collectives  14 us (6%)
  starting transfers between devices  10 us (4%)
  other arithmetic  8.65 us (4%)
    dot_general x16, matrix products, apply_ops(): jnp.einsum('tlarb,tlbc->rtac', blocks, sources, preferred_element_type=jn...  38.5 us
    reshape x16, local copies, waits for them, and re-layouts, apply_ops(): blocks.reshape(blocks.shape[0], blocks.shape[1], tile_rows, 2, tile_rows)  29.7 us
    all_to_all x1, waiting for transfers between devices, local(): lax.all_to_all(leaving, 'sector', split_axis=1, concat_axis=1, tiled=True)  23.5 us
    gather x16, local copies, waits for them, and re-layouts, apply_ops(): sources = pool_here[tile_index]  19.2 us
    another operation x1, loops' own time, local(): incoming = lax.map(per_direction, jnp.arange(dirs_here, dtype=jnp.int32))  16.1 us
    all_to_all x1, blocking collectives, local(): lax.all_to_all(incoming.reshape(dirs_here, tiles_here * tile_rows, column...  14 us
    gather x16, local copies, waits for them, and re-layouts, apply_ops(): blocks = op_here[op_index]  12 us
    squeeze x8, local copies, waits for them, and re-layouts, per_direction(): op_here = lax.dynamic_index_in_dim(operators, direction, 1, keepdims=False)  10.5 us
  transfers between devices with their start and end apart: 2, of which 2 were waited for; matrix products, arithmetic and copies ran while one was open for 0% of the time, Pallas kernels for 0%

commit v1 on v0

v1 whole, which is shorter than its diff:
```python
import jax
import jax.numpy as jnp
from jax import lax
from jax.experimental import pallas as pl
from jax.experimental.pallas import tpu as pltpu
from jax.sharding import PartitionSpec as P

CHUNKS = 1
MIB = 1024 * 1024


def turned(values):
    half = values.shape[-1] // 2
    lane = lax.broadcasted_iota(jnp.int32, values.shape, values.ndim - 1)
    moved = pltpu.roll(values, half, values.ndim - 1)
    return jnp.where(lane < half, -moved, moved)


def stack_rows(values):
    wide = values.astype(jnp.float32)
    return jnp.concatenate([wide, turned(wide)], axis=0).astype(jnp.bfloat16)


def vmem(count):
    return [pl.BlockSpec(memory_space=pltpu.VMEM)] * count


def smem(count):
    return [pl.BlockSpec(memory_space=pltpu.SMEM)] * count


def aggregate(fields, aggregation, devices, chunks):
    boxes, unknowns, columns = fields.shape
    all_dirs = aggregation.shape[0]
    part = all_dirs // devices // chunks

    def kernel(fields_ref, agg_ref, *refs):
        outs, scratch = refs[:chunks], refs[chunks]
        matrix = jnp.concatenate([agg_ref[:, :unknowns], agg_ref[:, unknowns:]], axis=0)
        for box in range(boxes):
            both = jnp.dot(matrix, fields_ref[box], preferred_element_type=jnp.float32)
            scratch[box * all_dirs : (box + 1) * all_dirs, :] = both[:all_dirs] + turned(both[all_dirs:])
        for direction in range(all_dirs):
            device, place = divmod(direction, part * chunks)
            chunk, inner = divmod(place, part)
            rows = scratch[pl.ds(direction, boxes, stride=all_dirs), :]
            outs[chunk][device, inner] = rows.astype(jnp.bfloat16)

    return pl.pallas_call(
        kernel,
        out_shape=[jax.ShapeDtypeStruct((devices, part, boxes, columns), jnp.bfloat16)] * chunks,
        in_specs=vmem(2),
        out_specs=vmem(chunks),
        scratch_shapes=[pltpu.VMEM((boxes * all_dirs, columns), jnp.float32)],
        name="aggregate",
    )(fields, aggregation)


def pick(slab, listing, where, partners, cap, per_tile):
    devices, part, boxes, columns = slab.shape

    def kernel(listing_ref, where_ref, slab_ref, *outs):
        for index in range(partners):
            other = where_ref[0] ^ (index + 1)
            for slot in range(cap):
                tile = listing_ref[where_ref[0], other, slot]
                outs[index][slot] = slab_ref[pl.ds(tile * per_tile, per_tile)]

    shape = jax.ShapeDtypeStruct((cap, per_tile, part, boxes, columns), jnp.bfloat16)
    return pl.pallas_call(
        kernel,
        out_shape=[shape] * partners,
        in_specs=smem(2) + vmem(1),
        out_specs=vmem(partners),
        name="pick",
    )(listing, where, slab)


def build(operators, near_tile, near_operator, far_slot, far_operator, where, partners, cap):
    count, dirs, rows, wide = operators.shape
    tiles, entries = near_tile.shape
    far_entries = far_slot.shape[1]
    slots = partners * cap
    group = min(4, tiles)

    def kernel(near_tile_ref, near_op_ref, far_slot_ref, far_op_ref, where_ref, op_ref, near_out, far_out, *scratch):
        near_sum, far_sum = scratch[:group], scratch[group:]
        for base in range(0, tiles, group):
            for ref in scratch:
                ref[...] = jnp.zeros_like(ref)

            def add(entry, _):
                for t in range(group):
                    source = near_tile_ref[base + t, entry]
                    block = op_ref[near_op_ref[base + t, entry]]
                    near_sum[t][source] += block.astype(jnp.float32)
                return 0

            def add_far(entry, _):
                for t in range(group):
                    place = far_slot_ref[base + t, entry]
                    sector = (place // cap) ^ where_ref[0]
                    slot = (sector - 1) * cap + place % cap
                    block = op_ref[far_op_ref[base + t, entry]]
                    far_sum[t][slot] += block.astype(jnp.float32)
                return 0

            lax.fori_loop(0, entries, add, 0)
            lax.fori_loop(0, far_entries, add_far, 0)
            for t in range(group):
                at = pl.ds((base + t) * rows, rows)
                near_out[:, at, :] = near_sum[t][...].astype(jnp.bfloat16)
                far_out[:, at, :] = far_sum[t][...].astype(jnp.bfloat16)

    return pl.pallas_call(
        kernel,
        grid=(dirs,),
        out_shape=[
            jax.ShapeDtypeStruct((dirs, tiles, tiles * rows, wide), jnp.bfloat16),
            jax.ShapeDtypeStruct((dirs, slots, tiles * rows, wide), jnp.bfloat16),
        ],
        in_specs=smem(5) + [pl.BlockSpec((count, None, rows, wide), lambda k: (0, k, 0, 0))],
        out_specs=[
            pl.BlockSpec((None, tiles, tiles * rows, wide), lambda k: (k, 0, 0, 0)),
            pl.BlockSpec((None, slots, tiles * rows, wide), lambda k: (k, 0, 0, 0)),
        ],
        scratch_shapes=[pltpu.VMEM((tiles, rows, wide), jnp.float32)] * group
        + [pltpu.VMEM((slots, rows, wide), jnp.float32)] * group,
        compiler_params=pltpu.CompilerParams(vmem_limit_bytes=40 * MIB),
        cost_estimate=pl.CostEstimate(
            flops=20 * dirs * tiles * (entries + far_entries) * rows * wide,
            bytes_accessed=2 * operators.size + 2 * dirs * (tiles + slots) * tiles * rows * wide,
            transcendentals=0,
        ),
        name="build",
    )(near_tile, near_operator, far_slot, far_operator, where, operators)


def wide_block(block_ref, slots):
    return jnp.concatenate([block_ref[slot] for slot in range(slots)], axis=1)


def near_product(blocks, slab, first, per_tile):
    _, tiles, rows, wide = blocks.shape
    devices, part, boxes, columns = slab.shape

    def kernel(block_ref, slab_ref, out_ref):
        sources = []
        for tile in range(tiles):
            pieces = [slab_ref[tile * per_tile + piece] for piece in range(per_tile)]
            sources.append(stack_rows(jnp.concatenate(pieces, axis=0)))
        out_ref[...] = jnp.dot(
            wide_block(block_ref, tiles), jnp.concatenate(sources, axis=0), preferred_element_type=jnp.float32
        )

    return pl.pallas_call(
        kernel,
        grid=(part,),
        out_shape=jax.ShapeDtypeStruct((part, rows, columns), jnp.float32),
        in_specs=[
            pl.BlockSpec((None, tiles, rows, wide), lambda k: (first + k, 0, 0, 0)),
            pl.BlockSpec((devices, None, boxes, columns), lambda k: (0, k, 0, 0)),
        ],
        out_specs=pl.BlockSpec((None, rows, columns), lambda k: (k, 0, 0)),
        compiler_params=pltpu.CompilerParams(vmem_limit_bytes=40 * MIB),
        cost_estimate=pl.CostEstimate(
            flops=8 * part * rows * tiles * wide * columns,
            bytes_accessed=2 * blocks.size // blocks.shape[0] * part + 2 * slab.size,
            transcendentals=0,
        ),
        name="near_product",
    )(blocks, slab)


def far_product(blocks, arrived, near, first, devices, per_tile):
    _, slots, rows, wide = blocks.shape
    cap, _, part, boxes, columns = arrived[0].shape
    partners = len(arrived)

    def kernel(block_ref, near_ref, *refs):
        out_ref = refs[partners]
        sources = []
        for index in range(partners):
            for slot in range(cap):
                pieces = [refs[index][slot, piece] for piece in range(per_tile)]
                sources.append(stack_rows(jnp.concatenate(pieces, axis=0)))
        total = near_ref[...] + jnp.dot(
            wide_block(block_ref, slots), jnp.concatenate(sources, axis=0), preferred_element_type=jnp.float32
        )
        total = total.astype(jnp.bfloat16)
        for device in range(devices):
            out_ref[device] = total[device * boxes : (device + 1) * boxes]

    return pl.pallas_call(
        kernel,
        grid=(part,),
        out_shape=jax.ShapeDtypeStruct((devices, part, boxes, columns), jnp.bfloat16),
        in_specs=[
            pl.BlockSpec((None, slots, rows, wide), lambda k: (first + k, 0, 0, 0)),
            pl.BlockSpec((None, rows, columns), lambda k: (k, 0, 0)),
        ]
        + [pl.BlockSpec((cap, per_tile, None, boxes, columns), lambda k: (0, 0, k, 0, 0))] * partners,
        out_specs=pl.BlockSpec((devices, None, boxes, columns), lambda k: (0, k, 0, 0)),
        compiler_params=pltpu.CompilerParams(vmem_limit_bytes=40 * MIB),
        name="far_product",
    )(blocks, near, *arrived)


def disaggregate(returned, disaggregation):
    devices, part, boxes, columns = returned[0].shape
    chunks = len(returned)
    unknowns = disaggregation.shape[0]
    all_dirs = disaggregation.shape[1] // 2

    def kernel(dis_ref, *refs):
        out_ref, scratch = refs[chunks], refs[chunks + 1]
        for direction in range(all_dirs):
            device, place = divmod(direction, part * chunks)
            chunk, inner = divmod(place, part)
            scratch[direction * boxes : (direction + 1) * boxes, :] = refs[chunk][device, inner].astype(jnp.float32)
        matrix = dis_ref[...]
        for box in range(boxes):
            rows = stack_rows(scratch[pl.ds(box, all_dirs, stride=boxes), :])
            out_ref[box] = jnp.dot(matrix, rows, preferred_element_type=jnp.float32).astype(jnp.bfloat16)

    return pl.pallas_call(
        kernel,
        out_shape=jax.ShapeDtypeStruct((boxes, unknowns, columns), jnp.bfloat16),
        in_specs=vmem(1 + chunks),
        out_specs=pl.BlockSpec(memory_space=pltpu.VMEM),
        scratch_shapes=[pltpu.VMEM((all_dirs * boxes, columns), jnp.float32)],
        name="disaggregate",
    )(disaggregation, *returned)


def make_local(sectors, devices):
    def local(
        fields,
        aggregation,
        operators,
        disaggregation,
        near_tile,
        near_operator,
        far_slot,
        far_operator,
        send_tiles,
    ):
        dirs_here = operators.shape[1]
        per_tile = operators.shape[2] // fields.shape[0]
        cap = send_tiles.shape[2]
        chunks = min(CHUNKS, dirs_here)
        part = dirs_here // chunks
        where = lax.axis_index("sector").astype(jnp.int32).reshape(1)
        outgoing = aggregate(fields, aggregation, devices, chunks)
        near_blocks, far_blocks = build(
            operators, near_tile, near_operator, far_slot, far_operator, where, sectors - 1, cap
        )
        returned = []
        for chunk in range(chunks):
            slab = lax.all_to_all(outgoing[chunk], "dir", 0, 0, tiled=True)
            leaving = pick(slab, send_tiles, where, sectors - 1, cap, per_tile)
            arrived = [
                lax.ppermute(leaving[index], "sector", [(i, i ^ (index + 1)) for i in range(sectors)])
                for index in range(sectors - 1)
            ]
            near = near_product(near_blocks, slab, chunk * part, per_tile)
            incoming = far_product(far_blocks, arrived, near, chunk * part, devices, per_tile)
            returned.append(lax.all_to_all(incoming, "dir", 0, 0, tiled=True))
        return disaggregate(returned, disaggregation)

    return local


def solution(mesh):
    placed = (
        P(("sector", "dir"), None, None),
        P(),
        P(None, "dir", None, None),
        P(),
        P("sector", None),
        P("sector", None),
        P("sector", None),
        P("sector", None),
        P(),
    )
    return jax.shard_map(
        make_local(mesh.shape["sector"], mesh.shape["dir"]),
        mesh=mesh,
        in_specs=placed,
        out_specs=P(("sector", "dir"), None, None),
        check_vma=False,
    )
```

time: 228 us -> 63.8 us (0.28)
  the two profiles are of different devices: /device:TPU:0 before, /device:TPU:16 now
where the time goes in v1:
time: 63.8 us; the launch traced here: 63.4 us
  Pallas kernels  23.4 us (37%)
  blocking collectives  14.1 us (22%)
  waiting for transfers between devices  13.1 us (21%)
  starting transfers between devices  7.21 us (11%)
  local copies, waits for them, and re-layouts  5.58 us (9%)
    all_to_all x1, blocking collectives, local(): returned.append(lax.all_to_all(incoming, 'dir', 0, 0, tiled=True))  14.1 us
    pallas_call x1, Pallas kernels, build(): pl.pallas_call(kernel, grid=(dirs,), out_shape=[jax.ShapeDtypeStruct((dir...  9.88 us
    all_to_all x1, waiting for transfers between devices, local(): slab = lax.all_to_all(outgoing[chunk], 'dir', 0, 0, tiled=True)  8.36 us
    unnamed x15, local copies, waits for them, and re-layouts  5.58 us
    ppermute x3, waiting for transfers between devices, local(): lax.ppermute(leaving[index], 'sector', [(i, i ^ index + 1) for i in range...  4.78 us
    all_to_all x1, starting transfers between devices, local(): slab = lax.all_to_all(outgoing[chunk], 'dir', 0, 0, tiled=True)  3.72 us
    ppermute x3, starting transfers between devices, local(): lax.ppermute(leaving[index], 'sector', [(i, i ^ index + 1) for i in range...  3.49 us
    pallas_call x1, Pallas kernels, aggregate(): pl.pallas_call(kernel, out_shape=[jax.ShapeDtypeStruct((devices, part, bo...  3.27 us
  transfers between devices with their start and end apart: 4, of which 2 were waited for; matrix products, arithmetic and copies ran while one was open for 2% of the time, Pallas kernels for 19%

profile of v1, /device:TPU:16, one launch (start us, length us, event | category | flops | bytes accessed | tf_op | source)
XLA Modules:
  0.0 63.4 jit_solution(137667189451894215)
XLA Ops:
  0.0 0.0 copy-start.3
  0.0 0.0 copy-start.4
  0.0 0.0 copy-start.5
  0.0 0.0 copy-start.6
  0.0 3.3 %aggregate.1 = bf16[8,8,32,128]{3,2,1,0:T(8,128)(2,1)} custom-call(bf16[32,128,128]{2,1,0:T(8,128)(2,1)} %fields_ref.1, bf16[64,256]{1,0:T(8,128)(2,1)} %agg_ref.1), custom_call_target="tpu_custom_call" | custom-call | tf_op jit(solution)/shard_map/aggregate/pallas_call | solution.py:49
  3.3 3.7 %all-to-all-start = ((bf16[8,8,32,128]{3,2,1,0:T(8,128)(2,1)}), bf16[8,8,32,128]{3,2,1,0:T(8,128)(2,1)S(1)}, u32[]{:S(2)}, u32[]{:S(2)}) async-start(bf16[8,8,32,128]{3,2,1,0:T(8,128)(2,1)} %aggregate.1), calls=%async_computation | async-start | bytes 1048576 | tf_op jit(solution)/shard_map/all_to_all | solution.py:260
  7.0 1.4 %copy.10.listing_ref = s32[4,4,2]{2,1,0:T(4,128)} copy(s32[4,4,2]{1,2,0:T(2,128)} %param.17) | data formatting | bytes 256 | tf_op args[8]
  8.4 8.4 %all-to-all-done.slab_ref = bf16[8,8,32,128]{3,2,1,0:T(8,128)(2,1)S(1)} async-done(((bf16[8,8,32,128]{3,2,1,0:T(8,128)(2,1)}), bf16[8,8,32,128]{3,2,1,0:T(8,128)(2,1)S(1)}, u32[]{:S(2)}, u32[]{:S(2)}) %all-to-all-start) | async-done | bytes 524320 | tf_op jit(solution)/shard_map/all_to_all | solution.py:260
  16.8 0.0 copy-start.1
  16.8 0.8 %copy-done.1 = bf16[8,8,32,128]{3,2,1,0:T(8,128)(2,1)} copy-done((bf16[8,8,32,128]{3,2,1,0:T(8,128)(2,1)}, bf16[8,8,32,128]{3,2,1,0:T(8,128)(2,1)S(1)}, u32[]{:S(2)}) %copy-start.1) | copy-done | bytes 524312
  17.6 2.0 %pick.1 = (bf16[2,2,8,32,128]{4,3,2,1,0:T(8,128)(2,1)}, bf16[2,2,8,32,128]{4,3,2,1,0:T(8,128)(2,1)}, bf16[2,2,8,32,128]{4,3,2,1,0:T(8,128)(2,1)}) custom-call(s32[4,4,2]{2,1,0:T(4,128)} %copy.10.listing_ref, s32[1]{0:T(128)} %bitcast.where_ref, bf16[8,8,32,128]{3,2,1,0:T(8,128)(2,1)} %copy-done.1), custom_call_target="tpu_custom_call" | custom-call | tf_op jit(solution)/shard_map/pick/pallas_call | solution.py:70
  19.5 1.6 %collective-permute-start = (bf16[2,2,8,32,128]{4,3,2,1,0:T(8,128)(2,1)}, bf16[2,2,8,32,128]{4,3,2,1,0:T(8,128)(2,1)S(1)}, u32[]{:S(2)}, u32[]{:S(2)}) collective-permute-start(bf16[2,2,8,32,128]{4,3,2,1,0:T(8,128)(2,1)} %get-tuple-element.12), channel_id=1, source_target_pairs={{0,8},{8,0},{16,24},{24,16},{1,9},{9,1},{17,25},{25,17},{2,10},{10... | collective-permute-start | bytes 786440 | tf_op jit(solution)/shard_map/ppermute | solution.py:263
  21.1 0.3 collective-permute-start.1
  21.5 1.6 %collective-permute-start.2 = (bf16[2,2,8,32,128]{4,3,2,1,0:T(8,128)(2,1)}, bf16[2,2,8,32,128]{4,3,2,1,0:T(8,128)(2,1)S(1)}, u32[]{:S(2)}, u32[]{:S(2)}) collective-permute-start(bf16[2,2,8,32,128]{4,3,2,1,0:T(8,128)(2,1)} %get-tuple-element.14), channel_id=1, source_target_pairs={{0,24},{8,16},{16,8},{24,0},{1,25},{9,17},{17,9},{25,1},{2,26},{10... | collective-permute-start | bytes 786440 | tf_op jit(solution)/shard_map/ppermute | solution.py:263
  23.0 0.0 copy-done.3
  23.0 0.0 copy-done.4
  23.0 0.0 copy-done.5
  23.0 0.0 copy-done.6
  23.0 0.0 copy-start
  23.1 3.4 %copy-done = bf16[64,8,64,128]{3,2,1,0:T(8,128)(2,1)S(1)} copy-done((bf16[64,8,64,128]{3,2,1,0:T(8,128)(2,1)S(1)}, bf16[64,8,64,128]{3,2,1,0:T(8,128)(2,1)}, u32[]{:S(2)}) %copy-start) | copy-done | bytes 8388632
  26.4 0.0 copy-start.2
  26.4 9.9 %build.1 = (bf16[8,4,256,128]{3,2,1,0:T(8,128)(2,1)S(1)}, bf16[8,6,256,128]{3,2,1,0:T(8,128)(2,1)S(1)}) custom-call(s32[4,16]{1,0:T(4,128)S(1)} %copy-done.3, s32[4,16]{1,0:T(4,128)S(1)} %copy-done.4, s32[4,16]{1,0:T(4,128)S(1)} %copy-done.5, s32[4,16]{1,0:T(4,128)S(1)} %copy-done.6, s32[1]{0:T(128)} %bitcast.where_ref, bf16[64,8,64,128]{3,2,1,0:T(8,128)(2,1)S(1)} %copy-done), custom_call_target="tpu_custom_call" | custom-call | flops 167772160 | bytes 13631488 | tf_op jit(solution)/shard_map/build/pallas_call | solution.py:115
  36.3 0.0 copy-done.2
  36.3 2.4 %near_product.1.near_ref = f32[8,256,128]{2,1,0:T(8,128)S(1)} custom-call(bf16[8,4,256,128]{3,2,1,0:T(8,128)(2,1)S(1)} %get-tuple-element.11.block_ref, bf16[8,8,32,128]{3,2,1,0:T(8,128)(2,1)S(1)} %copy-done.2), custom_call_target="tpu_custom_call" | custom-call | flops 1073741824 | bytes 2621440 | tf_op jit(solution)/shard_map/near_product/pallas_call | solution.py:156
  38.7 0.0 collective-permute-done.refs_0_
  38.8 0.0 collective-permute-done.1.refs_1_
  38.8 4.7 %collective-permute-done.2.refs_2_ = bf16[2,2,8,32,128]{4,3,2,1,0:T(8,128)(2,1)S(1)} collective-permute-done((bf16[2,2,8,32,128]{4,3,2,1,0:T(8,128)(2,1)}, bf16[2,2,8,32,128]{4,3,2,1,0:T(8,128)(2,1)S(1)}, u32[]{:S(2)}, u32[]{:S(2)}) %collective-permute-start.2) | collective-permute-done | bytes 262176 | tf_op jit(solution)/shard_map/ppermute | solution.py:263
  43.5 2.7 %far_product.1 = bf16[8,8,32,128]{3,2,1,0:T(8,128)(2,1)S(1)} custom-call(bf16[8,6,256,128]{3,2,1,0:T(8,128)(2,1)S(1)} %get-tuple-element.10.block_ref, f32[8,256,128]{2,1,0:T(8,128)S(1)} %near_product.1.near_ref, bf16[2,2,8,32,128]{4,3,2,1,0:T(8,128)(2,1)S(1)} %collective-permute-done.refs_0_, ...), custom_call_target="tpu_custom_call" | custom-call | tf_op jit(solution)/shard_map/far_product/pallas_call | solution.py:194
  46.3 14.1 %all_to_all.10.refs_0_ = bf16[8,8,32,128]{3,2,1,0:T(8,128)(2,1)} all-to-all(bf16[8,8,32,128]{3,2,1,0:T(8,128)(2,1)S(1)} %far_product.1), channel_id=1, replica_groups=mesh['sector'=4,'dir'=8] {'dir'}, dimensions={0} | all-to-all | bytes 1048576 | tf_op jit(solution)/shard_map/all_to_all | solution.py:268
  60.4 3.1 %disaggregate.1 = bf16[32,128,128]{2,1,0:T(8,128)(2,1)} custom-call(bf16[128,128]{1,0:T(8,128)(2,1)} %dis_ref.1, bf16[8,8,32,128]{3,2,1,0:T(8,128)(2,1)} %all_to_all.10.refs_0_), custom_call_target="tpu_custom_call" | custom-call | tf_op jit(solution)/shard_map/disaggregate/pallas_call | solution.py:226
Async XLA Ops:
  0.0 23.0 %copy-start.3 = (s32[4,16]{1,0:T(4,128)S(1)}, s32[4,16]{1,0:T(4,128)}, u32[]{:S(2)}) copy-start(s32[4,16]{1,0:T(4,128)} %near_tile_ref.1) | copy-start | bytes 772
  0.0 23.0 %copy-start.4 = (s32[4,16]{1,0:T(4,128)S(1)}, s32[4,16]{1,0:T(4,128)}, u32[]{:S(2)}) copy-start(s32[4,16]{1,0:T(4,128)} %near_op_ref.1) | copy-start | bytes 772
  0.0 23.0 %copy-start.5 = (s32[4,16]{1,0:T(4,128)S(1)}, s32[4,16]{1,0:T(4,128)}, u32[]{:S(2)}) copy-start(s32[4,16]{1,0:T(4,128)} %far_slot_ref.1) | copy-start | bytes 772
  0.0 23.0 %copy-start.6 = (s32[4,16]{1,0:T(4,128)S(1)}, s32[4,16]{1,0:T(4,128)}, u32[]{:S(2)}) copy-start(s32[4,16]{1,0:T(4,128)} %far_op_ref.1) | copy-start | bytes 772
  3.3 13.5 %all-to-all-start = ((bf16[8,8,32,128]{3,2,1,0:T(8,128)(2,1)}), bf16[8,8,32,128]{3,2,1,0:T(8,128)(2,1)S(1)}, u32[]{:S(2)}, u32[]{:S(2)}) async-start(bf16[8,8,32,128]{3,2,1,0:T(8,128)(2,1)} %aggregate.1), calls=%async_computation | async-start | bytes 1048576 | tf_op jit(solution)/shard_map/all_to_all | solution.py:260
  16.8 0.8 %copy-start.1 = (bf16[8,8,32,128]{3,2,1,0:T(8,128)(2,1)}, bf16[8,8,32,128]{3,2,1,0:T(8,128)(2,1)S(1)}, u32[]{:S(2)}) copy-start(bf16[8,8,32,128]{3,2,1,0:T(8,128)(2,1)S(1)} %all-to-all-done.slab_ref) | copy-start | bytes 1572868
  19.5 19.2 %collective-permute-start = (bf16[2,2,8,32,128]{4,3,2,1,0:T(8,128)(2,1)}, bf16[2,2,8,32,128]{4,3,2,1,0:T(8,128)(2,1)S(1)}, u32[]{:S(2)}, u32[]{:S(2)}) collective-permute-start(bf16[2,2,8,32,128]{4,3,2,1,0:T(8,128)(2,1)} %get-tuple-element.12), channel_id=1, source_target_pairs={{0,8},{8,0},{16,24},{24,16},{1,9},{9,1},{17,25},{25,17},{2,10},{10... | collective-permute-start | bytes 786440 | tf_op jit(solution)/shard_map/ppermute | solution.py:263
  21.1 17.7 %collective-permute-start.1 = (bf16[2,2,8,32,128]{4,3,2,1,0:T(8,128)(2,1)}, bf16[2,2,8,32,128]{4,3,2,1,0:T(8,128)(2,1)S(1)}, u32[]{:S(2)}, u32[]{:S(2)}) collective-permute-start(bf16[2,2,8,32,128]{4,3,2,1,0:T(8,128)(2,1)} %get-tuple-element.13), channel_id=1, source_target_pairs={{0,16},{8,24},{16,0},{24,8},{1,17},{9,25},{17,1},{25,9},{2,18},{10... | collective-permute-start | bytes 786440 | tf_op jit(solution)/shard_map/ppermute | solution.py:263
  21.5 22.1 %collective-permute-start.2 = (bf16[2,2,8,32,128]{4,3,2,1,0:T(8,128)(2,1)}, bf16[2,2,8,32,128]{4,3,2,1,0:T(8,128)(2,1)S(1)}, u32[]{:S(2)}, u32[]{:S(2)}) collective-permute-start(bf16[2,2,8,32,128]{4,3,2,1,0:T(8,128)(2,1)} %get-tuple-element.14), channel_id=1, source_target_pairs={{0,24},{8,16},{16,8},{24,0},{1,25},{9,17},{17,9},{25,1},{2,26},{10... | collective-permute-start | bytes 786440 | tf_op jit(solution)/shard_map/ppermute | solution.py:263
  23.0 3.4 %copy-start = (bf16[64,8,64,128]{3,2,1,0:T(8,128)(2,1)S(1)}, bf16[64,8,64,128]{3,2,1,0:T(8,128)(2,1)}, u32[]{:S(2)}) copy-start(bf16[64,8,64,128]{3,2,1,0:T(8,128)(2,1)} %op_ref.1) | copy-start | bytes 25165828
  26.4 9.9 %copy-start.2 = (bf16[8,8,32,128]{3,2,1,0:T(8,128)(2,1)S(1)}, bf16[8,8,32,128]{3,2,1,0:T(8,128)(2,1)}, u32[]{:S(2)}) copy-start(bf16[8,8,32,128]{3,2,1,0:T(8,128)(2,1)} %copy-done.1) | copy-start | bytes 1572868

commit v2 on v1

v2 whole, which is shorter than its diff:
```python
import jax
import jax.numpy as jnp
from jax import lax
from jax.experimental import pallas as pl
from jax.experimental.pallas import tpu as pltpu
from jax.sharding import PartitionSpec as P

MIB = 1024 * 1024
STEP_DIRS = 2
AGG_MIB = 20
OP_CUTS = 4
LITTLE = pl.CostEstimate(flops=1, bytes_accessed=1, transcendentals=0)


def turned(values):
    half = values.shape[-1] // 2
    lane = lax.broadcasted_iota(jnp.int32, values.shape, values.ndim - 1)
    moved = pltpu.roll(values, half, values.ndim - 1)
    return jnp.where(lane < half, -moved, moved)


def stack_rows(values):
    wide = values.astype(jnp.float32)
    return jnp.concatenate([wide, turned(wide)], axis=0).astype(jnp.bfloat16)


def vmem(count):
    return [pl.BlockSpec(memory_space=pltpu.VMEM)] * count


def smem(count):
    return [pl.BlockSpec(memory_space=pltpu.SMEM)] * count


def aggregate(fields, aggregation, place, devices):
    boxes, unknowns, columns = fields.shape
    all_dirs = aggregation.shape[0]
    part = all_dirs // devices

    def kernel(place_ref, fields_ref, agg_ref, *refs):
        outs, scratch = refs[:devices], refs[devices]
        matrix = jnp.concatenate([agg_ref[:, :unknowns], agg_ref[:, unknowns:]], axis=0)
        for box in range(boxes):
            both = jnp.dot(matrix, fields_ref[box], preferred_element_type=jnp.float32)
            scratch[box * all_dirs : (box + 1) * all_dirs, :] = both[:all_dirs] + turned(both[all_dirs:])
        for step in range(devices):
            first = (place_ref[0] ^ step) * part
            for inner in range(part):
                rows = scratch[pl.ds(first + inner, boxes, stride=all_dirs), :]
                outs[step][inner] = rows.astype(jnp.bfloat16)

    return pl.pallas_call(
        kernel,
        out_shape=[jax.ShapeDtypeStruct((part, boxes, columns), jnp.bfloat16)] * devices,
        in_specs=smem(1) + vmem(2),
        out_specs=vmem(devices),
        scratch_shapes=[pltpu.VMEM((boxes * all_dirs, columns), jnp.float32)],
        compiler_params=pltpu.CompilerParams(vmem_limit_bytes=AGG_MIB * MIB),
        cost_estimate=LITTLE,
        name="aggregate",
    )(place, fields, aggregation)


def pick(pieces, listing, where, place, partners, per_tile):
    devices = len(pieces)
    dirs, boxes, columns = pieces[0].shape
    cap = listing.shape[1]

    def kernel(listing_ref, where_ref, place_ref, *refs):
        slab_ref, outs = refs[devices], refs[devices + 1 :]
        for step in range(devices):
            slab_ref[place_ref[0] ^ step] = refs[step][...]
        for index in range(partners):
            other = where_ref[0] ^ (index + 1)
            for slot in range(cap):
                tile = listing_ref[where_ref[0], slot, other]
                outs[index][slot] = slab_ref[pl.ds(tile * per_tile, per_tile)]

    shapes = [(devices, dirs, boxes, columns)] + [(cap, per_tile, dirs, boxes, columns)] * partners
    outs = pl.pallas_call(
        kernel,
        grid=(1,),
        out_shape=[jax.ShapeDtypeStruct(shape, jnp.bfloat16) for shape in shapes],
        in_specs=smem(3) + [pl.BlockSpec(piece.shape, lambda i: (0, 0, 0)) for piece in pieces],
        out_specs=[pl.BlockSpec(shape, lambda i, n=len(shape): (0,) * n) for shape in shapes],
        compiler_params=pltpu.CompilerParams(vmem_limit_bytes=20 * MIB),
        cost_estimate=LITTLE,
        name="pick",
    )(listing, where, place, *pieces)
    return outs[0], outs[1:]


def build(operators, near_tile, near_operator, far_slot, far_operator, where, partners, cap):
    count, dirs, rows, wide = operators.shape
    tiles, entries = near_tile.shape
    far_entries = far_slot.shape[1]
    slots = partners * cap
    group = min(4, tiles)
    total = entries + far_entries
    cuts = OP_CUTS if count % OP_CUTS == 0 else 1
    size = count // cuts
    tables = (near_tile, near_operator, far_slot, far_operator)

    def kernel(where_ref, *refs):
        sources, op_hbm, near_out, far_out = refs[:4], refs[4], refs[5], refs[6]
        listed, slot_table, op_table, ops, table_sem, op_sem = refs[7:11], refs[11], refs[12], refs[13], refs[14], refs[15]
        sums = refs[16:]
        near_sum, far_sum = sums[:group], sums[group:]
        now = pl.program_id(0)

        def table_copy(index):
            return pltpu.make_async_copy(sources[index], listed[index], table_sem.at[index])

        def op_copy(direction, cut):
            at = pl.ds(cut * size, size)
            return pltpu.make_async_copy(op_hbm.at[at, direction], ops.at[direction, at], op_sem.at[direction, cut])

        @pl.when(now == 0)
        def _():
            for index in range(4):
                table_copy(index).start()
            for direction in range(dirs):
                for cut in range(cuts):
                    op_copy(direction, cut).start()
            for index in range(4):
                table_copy(index).wait()
            for tile in range(tiles):

                def fill(entry, _):
                    slot_table[tile * total + entry] = listed[0][tile, entry]
                    op_table[tile * total + entry] = listed[1][tile, entry]
                    return 0

                def fill_far(entry, _):
                    place = listed[2][tile, entry]
                    sector = lax.div(place, cap)
                    slot = ((sector ^ where_ref[0]) - 1) * cap + place - sector * cap
                    slot_table[tile * total + entries + entry] = slot
                    op_table[tile * total + entries + entry] = listed[3][tile, entry]
                    return 0

                lax.fori_loop(0, entries, fill, 0, unroll=4)
                lax.fori_loop(0, far_entries, fill_far, 0, unroll=4)

        for cut in range(cuts):
            op_copy(now, cut).wait()
        for base in range(0, tiles, group):
            for ref in sums:
                ref[...] = jnp.zeros_like(ref)
            for entry in range(total):
                for t in range(group):
                    at = (base + t) * total + entry
                    kept = near_sum[t] if entry < entries else far_sum[t]
                    kept[slot_table[at]] += ops[now, op_table[at]].astype(jnp.float32)
            for t in range(group):
                at = pl.ds((base + t) * rows, rows)
                near_out[:, at, :] = near_sum[t][...].astype(jnp.bfloat16)
                far_out[:, at, :] = far_sum[t][...].astype(jnp.bfloat16)

    need = 2 * operators.size + 4 * group * (tiles + slots) * rows * wide + 8 * (tiles + slots) * tiles * rows * wide
    return pl.pallas_call(
        kernel,
        grid=(dirs,),
        out_shape=[
            jax.ShapeDtypeStruct((dirs, tiles, tiles * rows, wide), jnp.bfloat16),
            jax.ShapeDtypeStruct((dirs, slots, tiles * rows, wide), jnp.bfloat16),
        ],
        in_specs=smem(1) + [pl.BlockSpec(memory_space=pltpu.HBM)] * 5,
        out_specs=[
            pl.BlockSpec((None, tiles, tiles * rows, wide), lambda k: (k, 0, 0, 0)),
            pl.BlockSpec((None, slots, tiles * rows, wide), lambda k: (k, 0, 0, 0)),
        ],
        scratch_shapes=[pltpu.SMEM(table.shape, jnp.int32) for table in tables]
        + [pltpu.SMEM((tiles * total,), jnp.int32)] * 2
        + [
            pltpu.VMEM((dirs, count, rows, wide), jnp.bfloat16),
            pltpu.SemaphoreType.DMA((4,)),
            pltpu.SemaphoreType.DMA((dirs, cuts)),
        ]
        + [pltpu.VMEM((tiles, rows, wide), jnp.float32)] * group
        + [pltpu.VMEM((slots, rows, wide), jnp.float32)] * group,
        compiler_params=pltpu.CompilerParams(vmem_limit_bytes=need + 4 * MIB),
        cost_estimate=LITTLE,
        name="build",
    )(where, *tables, operators)


def wide_block(block_ref, slots):
    return jnp.concatenate([block_ref[slot] for slot in range(slots)], axis=1)


def near_product(blocks, slab, per_tile):
    dirs, tiles, rows, wide = blocks.shape
    devices, _, boxes, columns = slab.shape
    group = STEP_DIRS if dirs % STEP_DIRS == 0 else 1

    def kernel(block_ref, slab_ref, out_ref):
        for inner in range(group):
            sources = []
            for tile in range(tiles):
                pieces = [slab_ref[tile * per_tile + piece, inner] for piece in range(per_tile)]
                sources.append(stack_rows(jnp.concatenate(pieces, axis=0)))
            out_ref[inner] = jnp.dot(
                wide_block(block_ref.at[inner], tiles),
                jnp.concatenate(sources, axis=0),
                preferred_element_type=jnp.float32,
            )

    return pl.pallas_call(
        kernel,
        grid=(dirs // group,),
        out_shape=jax.ShapeDtypeStruct((dirs, rows, columns), jnp.float32),
        in_specs=[
            pl.BlockSpec((group, tiles, rows, wide), lambda k: (k, 0, 0, 0)),
            pl.BlockSpec((devices, group, boxes, columns), lambda k: (0, k, 0, 0)),
        ],
        out_specs=pl.BlockSpec((group, rows, columns), lambda k: (k, 0, 0)),
        compiler_params=pltpu.CompilerParams(vmem_limit_bytes=40 * MIB),
        cost_estimate=LITTLE,
        name="near_product",
    )(blocks, slab)


def far_product(blocks, arrived, first, before, place, devices, per_tile):
    dirs, _, rows, wide = blocks.shape
    cap, _, _, boxes, columns = arrived[0].shape
    count = len(arrived)
    slots = count * cap
    last = place is not None
    group = STEP_DIRS if dirs % STEP_DIRS == 0 else 1

    def kernel(block_ref, before_ref, *refs):
        taken, outs = refs[:count], refs[count:]
        step = pl.program_id(0)
        for inner in range(group):
            sources = []
            for index in range(count):
                for slot in range(cap):
                    pieces = [taken[index][slot, piece, inner] for piece in range(per_tile)]
                    sources.append(stack_rows(jnp.concatenate(pieces, axis=0)))
            total = before_ref[inner] + jnp.dot(
                wide_block(block_ref.at[inner], slots),
                jnp.concatenate(sources, axis=0),
                preferred_element_type=jnp.float32,
            )
            if last:
                total_ref = outs[-1]
                total_ref[inner] = total
                for index in range(devices):
                    at = pl.multiple_of((outs[-2][0] ^ index) * boxes, boxes)
                    outs[index][step * group + inner] = total_ref[inner, pl.ds(at, boxes), :].astype(jnp.bfloat16)
            else:
                outs[0][inner] = total

    def kernel_last(place_ref, block_ref, before_ref, *refs):
        kernel(block_ref, before_ref, *refs[: count + devices], place_ref, refs[count + devices])

    in_specs = [
        pl.BlockSpec((group, slots, rows, wide), lambda k: (k, first, 0, 0)),
        pl.BlockSpec((group, rows, columns), lambda k: (k, 0, 0)),
    ] + [pl.BlockSpec((cap, per_tile, group, boxes, columns), lambda k: (0, 0, k, 0, 0))] * count
    operands = [blocks, before, *arrived]
    if last:
        in_specs = smem(1) + in_specs
        operands = [place] + operands
        out_shape = [jax.ShapeDtypeStruct((dirs, boxes, columns), jnp.bfloat16)] * devices
        out_specs = [pl.BlockSpec((dirs, boxes, columns), lambda k: (0, 0, 0))] * devices
        scratch = [pltpu.VMEM((group, rows, columns), jnp.float32)]
    else:
        out_shape = [jax.ShapeDtypeStruct((dirs, rows, columns), jnp.float32)]
        out_specs = [pl.BlockSpec((group, rows, columns), lambda k: (k, 0, 0))]
        scratch = []
    return pl.pallas_call(
        kernel_last if last else kernel,
        grid=(dirs // group,),
        out_shape=out_shape,
        in_specs=in_specs,
        out_specs=out_specs,
        scratch_shapes=scratch,
        compiler_params=pltpu.CompilerParams(vmem_limit_bytes=40 * MIB),
        cost_estimate=LITTLE,
        name="far_last" if last else "far_first",
    )(*operands)


def disaggregate(returned, disaggregation, place):
    dirs, boxes, columns = returned[0].shape
    devices = len(returned)
    unknowns = disaggregation.shape[0]
    all_dirs = disaggregation.shape[1] // 2
    step = boxes // 2

    def kernel(place_ref, dis_ref, *refs):
        out_ref, scratch = refs[devices], refs[devices + 1]
        for index in range(devices):
            first = (place_ref[0] ^ index) * dirs
            for inner in range(dirs):
                at = pl.multiple_of((first + inner) * step, step)
                scratch[pl.ds(at, step), :] = refs[index][inner].astype(jnp.float32)
        matrix = dis_ref[...]
        for box in range(step):
            rows = stack_rows(scratch[pl.ds(box, all_dirs, stride=step), :])
            out_ref[box] = jnp.dot(matrix, rows, preferred_element_type=jnp.float32).astype(jnp.bfloat16)

    return pl.pallas_call(
        kernel,
        grid=(boxes // step,),
        out_shape=jax.ShapeDtypeStruct((boxes, unknowns, columns), jnp.bfloat16),
        in_specs=smem(1)
        + [pl.BlockSpec(disaggregation.shape, lambda i: (0, 0))]
        + [pl.BlockSpec((dirs, step, columns), lambda i: (0, i, 0))] * devices,
        out_specs=pl.BlockSpec((step, unknowns, columns), lambda i: (i, 0, 0)),
        scratch_shapes=[pltpu.VMEM((all_dirs * step, columns), jnp.float32)],
        compiler_params=pltpu.CompilerParams(vmem_limit_bytes=20 * MIB),
        cost_estimate=LITTLE,
        name="disaggregate",
    )(place, disaggregation, *returned)


def crossed(pieces, axis):
    count = len(pieces)
    moved = [lax.ppermute(pieces[step], axis, [(i, i ^ step) for i in range(count)]) for step in range(1, count)]
    return [pieces[0]] + moved


def make_local(sectors, devices):
    partners = sectors - 1
    barrier = lax.optimization_barrier

    def local(
        fields,
        aggregation,
        operators,
        disaggregation,
        near_tile,
        near_operator,
        far_slot,
        far_operator,
        send_tiles,
    ):
        per_tile = operators.shape[2] // fields.shape[0]
        cap = send_tiles.shape[2]
        where = lax.axis_index("sector").astype(jnp.int32).reshape(1)
        place = lax.axis_index("dir").astype(jnp.int32).reshape(1)
        listing = jnp.swapaxes(send_tiles, 1, 2)
        outgoing = aggregate(fields, aggregation, place, devices)
        pieces = crossed(outgoing, "dir")
        slab, leaving = pick(pieces, listing, where, place, partners, per_tile)
        leaving, tile_index = barrier((leaving, near_tile))
        arrived = crossed([leaving[0], *leaving], "sector")[1:]
        near_blocks, far_blocks = build(
            operators, tile_index, near_operator, far_slot, far_operator, where, partners, cap
        )
        total = near_product(near_blocks, slab, per_tile)
        total = far_product(far_blocks, arrived[:-1], 0, total, None, devices, per_tile)[0]
        incoming = far_product(far_blocks, arrived[-1:], partners - 1, total, place, devices, per_tile)
        returned = crossed(incoming, "dir")
        return disaggregate(returned, disaggregation, place)

    return local


def solution(mesh):
    placed = (
        P(("sector", "dir"), None, None),
        P(),
        P(None, "dir", None, None),
        P(),
        P("sector", None),
        P("sector", None),
        P("sector", None),
        P("sector", None),
        P(),
    )
    return jax.shard_map(
        make_local(mesh.shape["sector"], mesh.shape["dir"]),
        mesh=mesh,
        in_specs=placed,
        out_specs=P(("sector", "dir"), None, None),
        check_vma=False,
    )
```

time: 63.8 us -> 56.1 us (0.88)
  blocking collectives: 14.1 us -> 0 us
  Pallas kernels: 23.4 us -> 13.8 us
  starting transfers between devices: 7.21 us -> 16.2 us
  waiting for transfers between devices: 13.1 us -> 16.5 us
  local copies, waits for them, and re-layouts: 5.58 us -> 8.78 us
    all_to_all x1 -> x0, blocking collectives: 14.1 us -> none  [local(): returned.append(lax.all_to_all(incoming, 'dir', 0, 0, tiled=True))]
    ppermute x3 -> x17, starting transfers between devices: 3.49 us -> 16.2 us  [crossed(): lax.ppermute(pieces[step], axis, [(i, i ^ step) for i in range(count)])]
    ppermute x3 -> x17, waiting for transfers between devices: 4.78 us -> 16.5 us  [crossed(): lax.ppermute(pieces[step], axis, [(i, i ^ step) for i in range(count)])]
    all_to_all x1 -> x0, waiting for transfers between devices: 8.36 us -> none  [local(): slab = lax.all_to_all(outgoing[chunk], 'dir', 0, 0, tiled=True)]
    pallas_call x5 -> x6, Pallas kernels: 13.5 us -> 8.09 us  [the longest x2 3.07 us: far_product(): pl.pallas_call(kernel_last if last else kernel, grid=(dirs // group,), ou...]
    pallas_call x1, Pallas kernels: 9.88 us -> 5.76 us  [build(): pl.pallas_call(kernel, grid=(dirs,), out_shape=[jax.ShapeDtypeStruct((dir...]
    all_to_all x1 -> x0, starting transfers between devices: 3.72 us -> none  [local(): slab = lax.all_to_all(outgoing[chunk], 'dir', 0, 0, tiled=True)]
    unnamed x15 -> x18, local copies, waits for them, and re-layouts: 5.58 us -> 8.78 us
  transfers between devices with their start and end apart: 4 -> 17, of which waited for: 2 -> 9; matrix products, arithmetic and copies ran while one was open for 2% -> 0% of each run, Pallas kernels for 19% -> 16%
where the time goes in v2:
time: 56.1 us; the launch traced here: 55.4 us
  waiting for transfers between devices  16.5 us (29%)
  starting transfers between devices  16.2 us (29%)
  Pallas kernels  13.8 us (25%)
  local copies, waits for them, and re-layouts  8.78 us (16%)
    ppermute x17, waiting for transfers between devices, crossed(): lax.ppermute(pieces[step], axis, [(i, i ^ step) for i in range(count)])  16.5 us
    ppermute x17, starting transfers between devices, crossed(): lax.ppermute(pieces[step], axis, [(i, i ^ step) for i in range(count)])  16.2 us
    unnamed x18, local copies, waits for them, and re-layouts  8.78 us
    pallas_call x1, Pallas kernels, build(): pl.pallas_call(kernel, grid=(dirs,), out_shape=[jax.ShapeDtypeStruct((dir...  5.76 us
    pallas_call x2, Pallas kernels, far_product(): pl.pallas_call(kernel_last if last else kernel, grid=(dirs // group,), ou...  3.07 us
    pallas_call x1, Pallas kernels, disaggregate(): pl.pallas_call(kernel, grid=(boxes // step,), out_shape=jax.ShapeDtypeStr...  1.72 us
    pallas_call x1, Pallas kernels, near_product(): pl.pallas_call(kernel, grid=(dirs // group,), out_shape=jax.ShapeDtypeStr...  1.53 us
  transfers between devices with their start and end apart: 17, of which 9 were waited for; matrix products, arithmetic and copies ran while one was open for 0% of the time, Pallas kernels for 16%

profile of v2, /device:TPU:16, one launch (start us, length us, event | category | flops | bytes accessed | tf_op | source)
XLA Modules:
  0.0 55.4 jit_solution(4705905402623967000)
XLA Ops:
  0.0 1.2 %copy-done.1 = bf16[32,128,128]{2,1,0:T(8,128)(2,1)S(1)} copy-done((bf16[32,128,128]{2,1,0:T(8,128)(2,1)S(1)}, bf16[32,128,128]{2,1,0:T(8,128)(2,1)}, u32[]{:S(2)}) %copy-start.1) | copy-done | bytes 1048600
  1.2 0.8 %copy-done.2 = bf16[64,256]{1,0:T(8,128)(2,1)S(1)} copy-done((bf16[64,256]{1,0:T(8,128)(2,1)S(1)}, bf16[64,256]{1,0:T(8,128)(2,1)}, u32[]{:S(2)}) %copy-start.2) | copy-done | bytes 32792
  2.0 1.1 %aggregate.1 = (bf16[8,32,128]{2,1,0:T(8,128)(2,1)S(1)}, bf16[8,32,128]{2,1,0:T(8,128)(2,1)S(1)}, bf16[8,32,128]{2,1,0:T(8,128)(2,1)S(1)}, bf16[8,32,128]{2,1,0:...) custom-call(s32[1]{0:T(128)} %bitcast.place_ref, ...), custom_call_target="tpu_custom_call" | custom-call | flops 1 | bytes 1 | tf_op jit(solution)/shard_map/aggregate/pallas_call | solution.py:52
  3.1 0.1 collective-permute-start
  3.2 1.6 %collective-permute-start.1 = (bf16[8,32,128]{2,1,0:T(8,128)(2,1)S(1)}, bf16[8,32,128]{2,1,0:T(8,128)(2,1)S(1)}, u32[]{:S(2)}, u32[]{:S(2)}) collective-permute-start(bf16[8,32,128]{2,1,0:T(8,128)(2,1)S(1)} %get-tuple-element.33), channel_id=1, source_target_pairs={{0,2},{1,3},{2,0},{3,1},{4,6},{5,7},{6,4},{7,5},{8,10},{9,11},{10,... | collective-permute-start | bytes 196616 | tf_op jit(solution)/shard_map/ppermute | solution.py:322
  4.7 0.3 collective-permute-start.2
  5.0 1.5 %collective-permute-start.3 = (bf16[8,32,128]{2,1,0:T(8,128)(2,1)S(1)}, bf16[8,32,128]{2,1,0:T(8,128)(2,1)S(1)}, u32[]{:S(2)}, u32[]{:S(2)}) collective-permute-start(bf16[8,32,128]{2,1,0:T(8,128)(2,1)S(1)} %get-tuple-element.35), channel_id=1, source_target_pairs={{0,4},{1,5},{2,6},{3,7},{4,0},{5,1},{6,2},{7,3},{8,12},{9,13},{10,... | collective-permute-start | bytes 196616 | tf_op jit(solution)/shard_map/ppermute | solution.py:322
  6.5 0.2 collective-permute-start.4
  6.7 0.0 collective-permute-done.refs_1_
  6.7 2.4 %collective-permute-start.5 = (bf16[8,32,128]{2,1,0:T(8,128)(2,1)S(1)}, bf16[8,32,128]{2,1,0:T(8,128)(2,1)S(1)}, u32[]{:S(2)}, u32[]{:S(2)}) collective-permute-start(bf16[8,32,128]{2,1,0:T(8,128)(2,1)S(1)} %get-tuple-element.37), channel_id=1, source_target_pairs={{0,6},{1,7},{2,4},{3,5},{4,2},{5,3},{6,0},{7,1},{8,14},{9,15},{10,... | collective-permute-start | bytes 196616 | tf_op jit(solution)/shard_map/ppermute | solution.py:322
  9.2 0.0 collective-permute-done.1.refs_2_
  9.2 0.3 collective-permute-start.6
  9.4 0.0 collective-permute-done.2.refs_3_
  9.4 0.0 collective-permute-done.3.refs_4_
  9.4 1.3 %collective-permute-done.4.refs_5_ = bf16[8,32,128]{2,1,0:T(8,128)(2,1)S(1)} collective-permute-done((bf16[8,32,128]{2,1,0:T(8,128)(2,1)S(1)}, bf16[8,32,128]{2,1,0:T(8,128)(2,1)S(1)}, u32[]{:S(2)}, u32[]{:S(2)}) %collective-permute-start.4) | collective-permute-done | bytes 65568 | tf_op jit(solution)/shard_map/ppermute | solution.py:322
  10.7 1.5 %collective-permute-done.5.refs_6_ = bf16[8,32,128]{2,1,0:T(8,128)(2,1)S(1)} collective-permute-done((bf16[8,32,128]{2,1,0:T(8,128)(2,1)S(1)}, bf16[8,32,128]{2,1,0:T(8,128)(2,1)S(1)}, u32[]{:S(2)}, u32[]{:S(2)}) %collective-permute-start.5) | collective-permute-done | bytes 65568 | tf_op jit(solution)/shard_map/ppermute | solution.py:322
  12.2 1.9 %collective-permute-done.6.refs_7_ = bf16[8,32,128]{2,1,0:T(8,128)(2,1)S(1)} collective-permute-done((bf16[8,32,128]{2,1,0:T(8,128)(2,1)S(1)}, bf16[8,32,128]{2,1,0:T(8,128)(2,1)S(1)}, u32[]{:S(2)}, u32[]{:S(2)}) %collective-permute-start.6) | collective-permute-done | bytes 65568 | tf_op jit(solution)/shard_map/ppermute | solution.py:322
  14.1 0.7 %copy-done.4 = s32[4,4,2]{1,2,0:T(2,128)S(1)} copy-done((s32[4,4,2]{1,2,0:T(2,128)S(1)}, s32[4,4,2]{1,2,0:T(2,128)}, u32[]{:S(2)}) %copy-start.4) | copy-done | bytes 152
  14.8 0.7 %pick.1 = (bf16[8,8,32,128]{3,2,1,0:T(8,128)(2,1)S(1)}, bf16[2,2,8,32,128]{4,3,2,1,0:T(8,128)(2,1)S(1)}, bf16[2,2,8,32,128]{4,3,2,1,0:T(8,128)(2,1)S(1)}, bf16[2,2,8,32,128]{4,3,2,1,0:T(8,128)(2,1)S(1)}) custom-call(s32[4,2,4]{2,1,0:T(2,128)S(1)} %bitcast.3, s32[1]{0:T(128)} %bitcast.1.where_ref, s32[1]{0:T(128)} %bitcast.place_ref, ...), custom_call_target="tpu_custom_call" | custom-call | flops 1 | bytes 1 | tf_op jit(solution)/shard_map/pick/pallas_call | solution.py:80
  15.5 1.6 %collective-permute-start.7 = (bf16[2,2,8,32,128]{4,3,2,1,0:T(8,128)(2,1)S(1)}, bf16[2,2,8,32,128]{4,3,2,1,0:T(8,128)(2,1)S(1)}, u32[]{:S(2)}, u32[]{:S(2)}) collective-permute-start(bf16[2,2,8,32,128]{4,3,2,1,0:T(8,128)(2,1)S(1)} %get-tuple-element.46), channel_id=1, source_target_pairs={{0,8},{8,0},{16,24},{24,16},{1,9},{9,1},{17,25},{25,17},{2,10},{10... | collective-permute-start | bytes 786440 | tf_op jit(solution)/shard_map/ppermute | solution.py:322
  17.1 0.3 collective-permute-start.8
  17.5 1.6 %collective-permute-start.9 = (bf16[2,2,8,32,128]{4,3,2,1,0:T(8,128)(2,1)S(1)}, bf16[2,2,8,32,128]{4,3,2,1,0:T(8,128)(2,1)S(1)}, u32[]{:S(2)}, u32[]{:S(2)}) collective-permute-start(bf16[2,2,8,32,128]{4,3,2,1,0:T(8,128)(2,1)S(1)} %get-tuple-element.48), channel_id=1, source_target_pairs={{0,24},{8,16},{16,8},{24,0},{1,25},{9,17},{17,9},{25,1},{2,26},{10... | collective-permute-start | bytes 786440 | tf_op jit(solution)/shard_map/ppermute | solution.py:322
  19.1 3.4 %copy-done = bf16[64,8,64,128]{3,2,1,0:T(8,128)(2,1)S(1)} copy-done((bf16[64,8,64,128]{3,2,1,0:T(8,128)(2,1)S(1)}, bf16[64,8,64,128]{3,2,1,0:T(8,128)(2,1)}, u32[]{:S(2)}) %copy-start) | copy-done | bytes 8388632
  22.4 0.7 %copy-done.5 = s32[4,16]{1,0:T(4,128)S(1)} copy-done((s32[4,16]{1,0:T(4,128)S(1)}, s32[4,16]{1,0:T(4,128)}, u32[]{:S(2)}) %copy-start.5) | copy-done | bytes 280
  23.1 0.7 %copy-done.6 = s32[4,16]{1,0:T(4,128)S(1)} copy-done((s32[4,16]{1,0:T(4,128)S(1)}, s32[4,16]{1,0:T(4,128)}, u32[]{:S(2)}) %copy-start.6) | copy-done | bytes 280
  23.8 0.7 %copy-done.7 = s32[4,16]{1,0:T(4,128)S(1)} copy-done((s32[4,16]{1,0:T(4,128)S(1)}, s32[4,16]{1,0:T(4,128)}, u32[]{:S(2)}) %copy-start.7) | copy-done | bytes 280
  24.5 0.7 %copy-done.8 = s32[4,16]{1,0:T(4,128)S(1)} copy-done((s32[4,16]{1,0:T(4,128)S(1)}, s32[4,16]{1,0:T(4,128)}, u32[]{:S(2)}) %copy-start.8) | copy-done | bytes 280
  25.2 5.8 %build.1 = (bf16[8,4,256,128]{3,2,1,0:T(8,128)(2,1)S(1)}, bf16[8,6,256,128]{3,2,1,0:T(8,128)(2,1)S(1)}) custom-call(s32[1]{0:T(128)} %bitcast.1.where_ref, s32[4,16]{1,0:T(4,128)S(1)} %copy-done.5, s32[4,16]{1,0:T(4,128)S(1)} %copy-done.6, s32[4,16]{1,0:T(4,128)S(1)} %copy-done.7, s32[4,16]{1,0:T(4,128)S(1)} %copy-done.8, bf16[64,8,64,128]{3,2,1,0:T(8,128)(2,1)S(1)} %copy-done), custom_call_target="tpu_custom_call" | custom-call | flops 1 | bytes 1 | tf_op jit(solution)/shard_map/build/pallas_call | solution.py:161
  30.9 1.5 %near_product.1.before_ref = f32[8,256,128]{2,1,0:T(8,128)S(1)} custom-call(bf16[8,4,256,128]{3,2,1,0:T(8,128)(2,1)S(1)} %get-tuple-element.44.block_ref, bf16[8,8,32,128]{3,2,1,0:T(8,128)(2,1)S(1)} %get-tuple-element.45.slab_ref), custom_call_target="tpu_custom_call" | custom-call | flops 1 | bytes 1 | tf_op jit(solution)/shard_map/near_product/pallas_call | solution.py:209
  32.5 0.0 collective-permute-done.7.refs_0_
  32.5 2.9 %collective-permute-done.8.refs_1_ = bf16[2,2,8,32,128]{4,3,2,1,0:T(8,128)(2,1)S(1)} collective-permute-done((bf16[2,2,8,32,128]{4,3,2,1,0:T(8,128)(2,1)S(1)}, bf16[2,2,8,32,128]{4,3,2,1,0:T(8,128)(2,1)S(1)}, u32[]{:S(2)}, u32[]{:S(2)}) %collective-permute-start.8) | collective-permute-done | bytes 262176 | tf_op jit(solution)/shard_map/ppermute | solution.py:322
  35.4 1.7 %far_first.1.before_ref = f32[8,256,128]{2,1,0:T(8,128)S(1)} custom-call(bf16[8,6,256,128]{3,2,1,0:T(8,128)(2,1)S(1)} %get-tuple-element.43.block_ref, f32[8,256,128]{2,1,0:T(8,128)S(1)} %near_product.1.before_ref, bf16[2,2,8,32,128]{4,3,2,1,0:T(8,128)(2,1)S(1)} %collective-permute-done.7.refs_0_, bf16[2,2,8,32,128]{4,3,2,1,0:T(8,128)(2,1)S(1)} %collective-permute-done.8.refs_1_), custom_call_target="tpu_custom_call" | custom-call | flops 1 | bytes 1 | tf_op jit(solution)/shard_map/far_first/pallas_call | solution.py:273
  37.1 0.0 copy-start.3
  37.1 4.9 %collective-permute-done.9.refs_0_ = bf16[2,2,8,32,128]{4,3,2,1,0:T(8,128)(2,1)S(1)} collective-permute-done((bf16[2,2,8,32,128]{4,3,2,1,0:T(8,128)(2,1)S(1)}, bf16[2,2,8,32,128]{4,3,2,1,0:T(8,128)(2,1)S(1)}, u32[]{:S(2)}, u32[]{:S(2)}) %collective-permute-start.9) | collective-permute-done | bytes 262176 | tf_op jit(solution)/shard_map/ppermute | solution.py:322
  42.0 1.4 %far_last.1 = (bf16[8,32,128]{2,1,0:T(8,128)(2,1)S(1)}, bf16[8,32,128]{2,1,0:T(8,128)(2,1)S(1)}, bf16[8,32,128]{2,1,0:T(8,128)(2,1)S(1)}, bf16[8,32,128]{2,1,0:T...) custom-call(s32[1]{0:T(128)} %bitcast.place_ref, ...), custom_call_target="tpu_custom_call" | custom-call | flops 1 | bytes 1 | tf_op jit(solution)/shard_map/far_last/pallas_call | solution.py:273
  43.4 0.1 collective-permute-start.10
  43.5 0.8 %collective-permute-start.11 = (bf16[8,32,128]{2,1,0:T(8,128)(2,1)S(1)}, bf16[8,32,128]{2,1,0:T(8,128)(2,1)S(1)}, u32[]{:S(2)}, u32[]{:S(2)}) collective-permute-start(bf16[8,32,128]{2,1,0:T(8,128)(2,1)S(1)} %get-tuple-element.51), channel_id=1, source_target_pairs={{0,2},{1,3},{2,0},{3,1},{4,6},{5,7},{6,4},{7,5},{8,10},{9,11},{10,... | collective-permute-start | bytes 196616 | tf_op jit(solution)/shard_map/ppermute | solution.py:322
  44.3 1.0 %collective-permute-start.12 = (bf16[8,32,128]{2,1,0:T(8,128)(2,1)S(1)}, bf16[8,32,128]{2,1,0:T(8,128)(2,1)S(1)}, u32[]{:S(2)}, u32[]{:S(2)}) collective-permute-start(bf16[8,32,128]{2,1,0:T(8,128)(2,1)S(1)} %get-tuple-element.52), channel_id=1, source_target_pairs={{0,3},{1,2},{2,1},{3,0},{4,7},{5,6},{6,5},{7,4},{8,11},{9,10},{10,... | collective-permute-start | bytes 196616 | tf_op jit(solution)/shard_map/ppermute | solution.py:322
  45.4 0.6 %collective-permute-start.13 = (bf16[8,32,128]{2,1,0:T(8,128)(2,1)S(1)}, bf16[8,32,128]{2,1,0:T(8,128)(2,1)S(1)}, u32[]{:S(2)}, u32[]{:S(2)}) collective-permute-start(bf16[8,32,128]{2,1,0:T(8,128)(2,1)S(1)} %get-tuple-element.53), channel_id=1, source_target_pairs={{0,4},{1,5},{2,6},{3,7},{4,0},{5,1},{6,2},{7,3},{8,12},{9,13},{10,... | collective-permute-start | bytes 196616 | tf_op jit(solution)/shard_map/ppermute | solution.py:322
  46.0 1.1 %collective-permute-start.14 = (bf16[8,32,128]{2,1,0:T(8,128)(2,1)S(1)}, bf16[8,32,128]{2,1,0:T(8,128)(2,1)S(1)}, u32[]{:S(2)}, u32[]{:S(2)}) collective-permute-start(bf16[8,32,128]{2,1,0:T(8,128)(2,1)S(1)} %get-tuple-element.54), channel_id=1, source_target_pairs={{0,5},{1,4},{2,7},{3,6},{4,1},{5,0},{6,3},{7,2},{8,13},{9,12},{10,... | collective-permute-start | bytes 196616 | tf_op jit(solution)/shard_map/ppermute | solution.py:322
  47.1 1.7 %collective-permute-start.15 = (bf16[8,32,128]{2,1,0:T(8,128)(2,1)S(1)}, bf16[8,32,128]{2,1,0:T(8,128)(2,1)S(1)}, u32[]{:S(2)}, u32[]{:S(2)}) collective-permute-start(bf16[8,32,128]{2,1,0:T(8,128)(2,1)S(1)} %get-tuple-element.55), channel_id=1, source_target_pairs={{0,6},{1,7},{2,4},{3,5},{4,2},{5,3},{6,0},{7,1},{8,14},{9,15},{10,... | collective-permute-start | bytes 196616 | tf_op jit(solution)/shard_map/ppermute | solution.py:322
  48.7 1.0 %collective-permute-start.16 = (bf16[8,32,128]{2,1,0:T(8,128)(2,1)S(1)}, bf16[8,32,128]{2,1,0:T(8,128)(2,1)S(1)}, u32[]{:S(2)}, u32[]{:S(2)}) collective-permute-start(bf16[8,32,128]{2,1,0:T(8,128)(2,1)S(1)} %get-tuple-element.56), channel_id=1, source_target_pairs={{0,7},{1,6},{2,5},{3,4},{4,3},{5,2},{6,1},{7,0},{8,15},{9,14},{10,... | collective-permute-start | bytes 196616 | tf_op jit(solution)/shard_map/ppermute | solution.py:322
  49.8 0.0 collective-permute-done.12.refs_3_
  49.8 0.5 collective-permute-done.13.refs_4_
  50.3 0.3 collective-permute-done.14.refs_5_
  50.5 2.0 %collective-permute-done.15.refs_6_ = bf16[8,32,128]{2,1,0:T(8,128)(2,1)S(1)} collective-permute-done((bf16[8,32,128]{2,1,0:T(8,128)(2,1)S(1)}, bf16[8,32,128]{2,1,0:T(8,128)(2,1)S(1)}, u32[]{:S(2)}, u32[]{:S(2)}) %collective-permute-start.15) | collective-permute-done | bytes 65568 | tf_op jit(solution)/shard_map/ppermute | solution.py:322
  52.5 1.2 %collective-permute-done.16.refs_7_ = bf16[8,32,128]{2,1,0:T(8,128)(2,1)S(1)} collective-permute-done((bf16[8,32,128]{2,1,0:T(8,128)(2,1)S(1)}, bf16[8,32,128]{2,1,0:T(8,128)(2,1)S(1)}, u32[]{:S(2)}, u32[]{:S(2)}) %collective-permute-start.16) | collective-permute-done | bytes 65568 | tf_op jit(solution)/shard_map/ppermute | solution.py:322
  53.7 1.7 %disaggregate.1 = bf16[32,128,128]{2,1,0:T(8,128)(2,1)} custom-call(s32[1]{0:T(128)} %bitcast.place_ref, bf16[128,128]{1,0:T(8,128)(2,1)S(1)} %copy-done.3, bf16[8,32,128]{2,1,0:T(8,128)(2,1)S(1)} %get-tuple-element.49.refs_0_, bf16[8,32,128]{2,1,0:T(8,128)(2,1)S(1)} %collective-permute-done.10.refs_1_, ...), custom_call_target="tpu_custom_call" | custom-call | flops 1 | bytes 1 | tf_op jit(solution)/shard_map/disaggregate/pallas_call | solution.py:305
  (11 shorter events, 0.0 us)
Async XLA Ops:
  0.0 1.2 %copy-start.1 = (bf16[32,128,128]{2,1,0:T(8,128)(2,1)S(1)}, bf16[32,128,128]{2,1,0:T(8,128)(2,1)}, u32[]{:S(2)}) copy-start(bf16[32,128,128]{2,1,0:T(8,128)(2,1)} %fields_ref.1) | copy-start | bytes 3145732
  1.2 0.8 %copy-start.2 = (bf16[64,256]{1,0:T(8,128)(2,1)S(1)}, bf16[64,256]{1,0:T(8,128)(2,1)}, u32[]{:S(2)}) copy-start(bf16[64,256]{1,0:T(8,128)(2,1)} %agg_ref.1) | copy-start | bytes 98308
  3.1 3.6 %collective-permute-start = (bf16[8,32,128]{2,1,0:T(8,128)(2,1)S(1)}, bf16[8,32,128]{2,1,0:T(8,128)(2,1)S(1)}, u32[]{:S(2)}, u32[]{:S(2)}) collective-permute-start(bf16[8,32,128]{2,1,0:T(8,128)(2,1)S(1)} %get-tuple-element.32), channel_id=1, source_target_pairs={{0,1},{1,0},{2,3},{3,2},{4,5},{5,4},{6,7},{7,6},{8,9},{9,8},{10,11... | collective-permute-start | bytes 196616 | tf_op jit(solution)/shard_map/ppermute | solution.py:322
  3.2 6.0 %collective-permute-start.1 = (bf16[8,32,128]{2,1,0:T(8,128)(2,1)S(1)}, bf16[8,32,128]{2,1,0:T(8,128)(2,1)S(1)}, u32[]{:S(2)}, u32[]{:S(2)}) collective-permute-start(bf16[8,32,128]{2,1,0:T(8,128)(2,1)S(1)} %get-tuple-element.33), channel_id=1, source_target_pairs={{0,2},{1,3},{2,0},{3,1},{4,6},{5,7},{6,4},{7,5},{8,10},{9,11},{10,... | collective-permute-start | bytes 196616 | tf_op jit(solution)/shard_map/ppermute | solution.py:322
  4.7 4.7 %collective-permute-start.2 = (bf16[8,32,128]{2,1,0:T(8,128)(2,1)S(1)}, bf16[8,32,128]{2,1,0:T(8,128)(2,1)S(1)}, u32[]{:S(2)}, u32[]{:S(2)}) collective-permute-start(bf16[8,32,128]{2,1,0:T(8,128)(2,1)S(1)} %get-tuple-element.34), channel_id=1, source_target_pairs={{0,3},{1,2},{2,1},{3,0},{4,7},{5,6},{6,5},{7,4},{8,11},{9,10},{10,... | collective-permute-start | bytes 196616 | tf_op jit(solution)/shard_map/ppermute | solution.py:322
  5.0 4.4 %collective-permute-start.3 = (bf16[8,32,128]{2,1,0:T(8,128)(2,1)S(1)}, bf16[8,32,128]{2,1,0:T(8,128)(2,1)S(1)}, u32[]{:S(2)}, u32[]{:S(2)}) collective-permute-start(bf16[8,32,128]{2,1,0:T(8,128)(2,1)S(1)} %get-tuple-element.35), channel_id=1, source_target_pairs={{0,4},{1,5},{2,6},{3,7},{4,0},{5,1},{6,2},{7,3},{8,12},{9,13},{10,... | collective-permute-start | bytes 196616 | tf_op jit(solution)/shard_map/ppermute | solution.py:322
  6.5 4.2 %collective-permute-start.4 = (bf16[8,32,128]{2,1,0:T(8,128)(2,1)S(1)}, bf16[8,32,128]{2,1,0:T(8,128)(2,1)S(1)}, u32[]{:S(2)}, u32[]{:S(2)}) collective-permute-start(bf16[8,32,128]{2,1,0:T(8,128)(2,1)S(1)} %get-tuple-element.36), channel_id=1, source_target_pairs={{0,5},{1,4},{2,7},{3,6},{4,1},{5,0},{6,3},{7,2},{8,13},{9,12},{10,... | collective-permute-start | bytes 196616 | tf_op jit(solution)/shard_map/ppermute | solution.py:322
  6.7 5.4 %collective-permute-start.5 = (bf16[8,32,128]{2,1,0:T(8,128)(2,1)S(1)}, bf16[8,32,128]{2,1,0:T(8,128)(2,1)S(1)}, u32[]{:S(2)}, u32[]{:S(2)}) collective-permute-start(bf16[8,32,128]{2,1,0:T(8,128)(2,1)S(1)} %get-tuple-element.37), channel_id=1, source_target_pairs={{0,6},{1,7},{2,4},{3,5},{4,2},{5,3},{6,0},{7,1},{8,14},{9,15},{10,... | collective-permute-start | bytes 196616 | tf_op jit(solution)/shard_map/ppermute | solution.py:322
  9.2 4.9 %collective-permute-start.6 = (bf16[8,32,128]{2,1,0:T(8,128)(2,1)S(1)}, bf16[8,32,128]{2,1,0:T(8,128)(2,1)S(1)}, u32[]{:S(2)}, u32[]{:S(2)}) collective-permute-start(bf16[8,32,128]{2,1,0:T(8,128)(2,1)S(1)} %get-tuple-element.38), channel_id=1, source_target_pairs={{0,7},{1,6},{2,5},{3,4},{4,3},{5,2},{6,1},{7,0},{8,15},{9,14},{10,... | collective-permute-start | bytes 196616 | tf_op jit(solution)/shard_map/ppermute | solution.py:322
  14.1 0.7 %copy-start.4 = (s32[4,4,2]{1,2,0:T(2,128)S(1)}, s32[4,4,2]{1,2,0:T(2,128)}, u32[]{:S(2)}) copy-start(s32[4,4,2]{1,2,0:T(2,128)} %param.17) | copy-start | bytes 388
  15.5 17.0 %collective-permute-start.7 = (bf16[2,2,8,32,128]{4,3,2,1,0:T(8,128)(2,1)S(1)}, bf16[2,2,8,32,128]{4,3,2,1,0:T(8,128)(2,1)S(1)}, u32[]{:S(2)}, u32[]{:S(2)}) collective-permute-start(bf16[2,2,8,32,128]{4,3,2,1,0:T(8,128)(2,1)S(1)} %get-tuple-element.46), channel_id=1, source_target_pairs={{0,8},{8,0},{16,24},{24,16},{1,9},{9,1},{17,25},{25,17},{2,10},{10... | collective-permute-start | bytes 786440 | tf_op jit(solution)/shard_map/ppermute | solution.py:322
  17.1 18.3 %collective-permute-start.8 = (bf16[2,2,8,32,128]{4,3,2,1,0:T(8,128)(2,1)S(1)}, bf16[2,2,8,32,128]{4,3,2,1,0:T(8,128)(2,1)S(1)}, u32[]{:S(2)}, u32[]{:S(2)}) collective-permute-start(bf16[2,2,8,32,128]{4,3,2,1,0:T(8,128)(2,1)S(1)} %get-tuple-element.47), channel_id=1, source_target_pairs={{0,16},{8,24},{16,0},{24,8},{1,17},{9,25},{17,1},{25,9},{2,18},{10... | collective-permute-start | bytes 786440 | tf_op jit(solution)/shard_map/ppermute | solution.py:322
  17.5 24.5 %collective-permute-start.9 = (bf16[2,2,8,32,128]{4,3,2,1,0:T(8,128)(2,1)S(1)}, bf16[2,2,8,32,128]{4,3,2,1,0:T(8,128)(2,1)S(1)}, u32[]{:S(2)}, u32[]{:S(2)}) collective-permute-start(bf16[2,2,8,32,128]{4,3,2,1,0:T(8,128)(2,1)S(1)} %get-tuple-element.48), channel_id=1, source_target_pairs={{0,24},{8,16},{16,8},{24,0},{1,25},{9,17},{17,9},{25,1},{2,26},{10... | collective-permute-start | bytes 786440 | tf_op jit(solution)/shard_map/ppermute | solution.py:322
  19.1 3.4 %copy-start = (bf16[64,8,64,128]{3,2,1,0:T(8,128)(2,1)S(1)}, bf16[64,8,64,128]{3,2,1,0:T(8,128)(2,1)}, u32[]{:S(2)}) copy-start(bf16[64,8,64,128]{3,2,1,0:T(8,128)(2,1)} %refs_4_.1) | copy-start | bytes 25165828
  22.4 0.7 %copy-start.5 = (s32[4,16]{1,0:T(4,128)S(1)}, s32[4,16]{1,0:T(4,128)}, u32[]{:S(2)}) copy-start(s32[4,16]{1,0:T(4,128)} %refs_0_) | copy-start | bytes 772
  23.1 0.7 %copy-start.6 = (s32[4,16]{1,0:T(4,128)S(1)}, s32[4,16]{1,0:T(4,128)}, u32[]{:S(2)}) copy-start(s32[4,16]{1,0:T(4,128)} %refs_1_.1) | copy-start | bytes 772
  23.8 0.7 %copy-start.7 = (s32[4,16]{1,0:T(4,128)S(1)}, s32[4,16]{1,0:T(4,128)}, u32[]{:S(2)}) copy-start(s32[4,16]{1,0:T(4,128)} %refs_2_.1) | copy-start | bytes 772
  24.5 0.7 %copy-start.8 = (s32[4,16]{1,0:T(4,128)S(1)}, s32[4,16]{1,0:T(4,128)}, u32[]{:S(2)}) copy-start(s32[4,16]{1,0:T(4,128)} %refs_3_.1) | copy-start | bytes 772
  37.1 16.6 %copy-start.3 = (bf16[128,128]{1,0:T(8,128)(2,1)S(1)}, bf16[128,128]{1,0:T(8,128)(2,1)}, u32[]{:S(2)}) copy-start(bf16[128,128]{1,0:T(8,128)(2,1)} %dis_ref.1) | copy-start | bytes 98308
  43.4 3.6 %collective-permute-start.10 = (bf16[8,32,128]{2,1,0:T(8,128)(2,1)S(1)}, bf16[8,32,128]{2,1,0:T(8,128)(2,1)S(1)}, u32[]{:S(2)}, u32[]{:S(2)}) collective-permute-start(bf16[8,32,128]{2,1,0:T(8,128)(2,1)S(1)} %get-tuple-element.50), channel_id=1, source_target_pairs={{0,1},{1,0},{2,3},{3,2},{4,5},{5,4},{6,7},{7,6},{8,9},{9,8},{10,11... | collective-permute-start | bytes 196616 | tf_op jit(solution)/shard_map/ppermute | solution.py:322
  43.5 5.2 %collective-permute-start.11 = (bf16[8,32,128]{2,1,0:T(8,128)(2,1)S(1)}, bf16[8,32,128]{2,1,0:T(8,128)(2,1)S(1)}, u32[]{:S(2)}, u32[]{:S(2)}) collective-permute-start(bf16[8,32,128]{2,1,0:T(8,128)(2,1)S(1)} %get-tuple-element.51), channel_id=1, source_target_pairs={{0,2},{1,3},{2,0},{3,1},{4,6},{5,7},{6,4},{7,5},{8,10},{9,11},{10,... | collective-permute-start | bytes 196616 | tf_op jit(solution)/shard_map/ppermute | solution.py:322
  44.3 5.4 %collective-permute-start.12 = (bf16[8,32,128]{2,1,0:T(8,128)(2,1)S(1)}, bf16[8,32,128]{2,1,0:T(8,128)(2,1)S(1)}, u32[]{:S(2)}, u32[]{:S(2)}) collective-permute-start(bf16[8,32,128]{2,1,0:T(8,128)(2,1)S(1)} %get-tuple-element.52), channel_id=1, source_target_pairs={{0,3},{1,2},{2,1},{3,0},{4,7},{5,6},{6,5},{7,4},{8,11},{9,10},{10,... | collective-permute-start | bytes 196616 | tf_op jit(solution)/shard_map/ppermute | solution.py:322
  45.4 4.9 %collective-permute-start.13 = (bf16[8,32,128]{2,1,0:T(8,128)(2,1)S(1)}, bf16[8,32,128]{2,1,0:T(8,128)(2,1)S(1)}, u32[]{:S(2)}, u32[]{:S(2)}) collective-permute-start(bf16[8,32,128]{2,1,0:T(8,128)(2,1)S(1)} %get-tuple-element.53), channel_id=1, source_target_pairs={{0,4},{1,5},{2,6},{3,7},{4,0},{5,1},{6,2},{7,3},{8,12},{9,13},{10,... | collective-permute-start | bytes 196616 | tf_op jit(solution)/shard_map/ppermute | solution.py:322
  46.0 4.5 %collective-permute-start.14 = (bf16[8,32,128]{2,1,0:T(8,128)(2,1)S(1)}, bf16[8,32,128]{2,1,0:T(8,128)(2,1)S(1)}, u32[]{:S(2)}, u32[]{:S(2)}) collective-permute-start(bf16[8,32,128]{2,1,0:T(8,128)(2,1)S(1)} %get-tuple-element.54), channel_id=1, source_target_pairs={{0,5},{1,4},{2,7},{3,6},{4,1},{5,0},{6,3},{7,2},{8,13},{9,12},{10,... | collective-permute-start | bytes 196616 | tf_op jit(solution)/shard_map/ppermute | solution.py:322
  47.1 5.5 %collective-permute-start.15 = (bf16[8,32,128]{2,1,0:T(8,128)(2,1)S(1)}, bf16[8,32,128]{2,1,0:T(8,128)(2,1)S(1)}, u32[]{:S(2)}, u32[]{:S(2)}) collective-permute-start(bf16[8,32,128]{2,1,0:T(8,128)(2,1)S(1)} %get-tuple-element.55), channel_id=1, source_target_pairs={{0,6},{1,7},{2,4},{3,5},{4,2},{5,3},{6,0},{7,1},{8,14},{9,15},{10,... | collective-permute-start | bytes 196616 | tf_op jit(solution)/shard_map/ppermute | solution.py:322
  48.7 4.9 %collective-permute-start.16 = (bf16[8,32,128]{2,1,0:T(8,128)(2,1)S(1)}, bf16[8,32,128]{2,1,0:T(8,128)(2,1)S(1)}, u32[]{:S(2)}, u32[]{:S(2)}) collective-permute-start(bf16[8,32,128]{2,1,0:T(8,128)(2,1)S(1)} %get-tuple-element.56), channel_id=1, source_target_pairs={{0,7},{1,6},{2,5},{3,4},{4,3},{5,2},{6,1},{7,0},{8,15},{9,14},{10,... | collective-permute-start | bytes 196616 | tf_op jit(solution)/shard_map/ppermute | solution.py:322

commit v3 on v2

--- a/solution.py
+++ b/solution.py
@@ -10,6 +10,10 @@
 AGG_MIB = 20
 OP_CUTS = 4
 LITTLE = pl.CostEstimate(flops=1, bytes_accessed=1, transcendentals=0)
+
+
+def order(count):
+    return sorted(range(count), key=lambda step: (step == 0, -bin(step >> 1).count("1"), -(step & 1), step))
 
 
 def turned(values):
@@ -64,16 +68,16 @@
 def pick(pieces, listing, where, place, partners, per_tile):
     devices = len(pieces)
     dirs, boxes, columns = pieces[0].shape
-    cap = listing.shape[1]
+    cap = listing.shape[0]
 
     def kernel(listing_ref, where_ref, place_ref, *refs):
         slab_ref, outs = refs[devices], refs[devices + 1 :]
-        for step in range(devices):
-            slab_ref[place_ref[0] ^ step] = refs[step][...]
+        for index, step in enumerate(order(devices)):
+            slab_ref[place_ref[0] ^ step] = refs[index][...]
         for index in range(partners):
             other = where_ref[0] ^ (index + 1)
             for slot in range(cap):
-                tile = listing_ref[where_ref[0], slot, other]
+                tile = listing_ref[slot, other]
                 outs[index][slot] = slab_ref[pl.ds(tile * per_tile, per_tile)]
 
     shapes = [(devices, dirs, boxes, columns)] + [(cap, per_tile, dirs, boxes, columns)] * partners
@@ -86,7 +90,7 @@
         compiler_params=pltpu.CompilerParams(vmem_limit_bytes=20 * MIB),
         cost_estimate=LITTLE,
         name="pick",
-    )(listing, where, place, *pieces)
+    )(listing, where, place, *[pieces[step] for step in order(devices)])
     return outs[0], outs[1:]
 
 
@@ -134,7 +138,8 @@
                 def fill_far(entry, _):
                     place = listed[2][tile, entry]
                     sector = lax.div(place, cap)
-                    slot = ((sector ^ where_ref[0]) - 1) * cap + place - sector * cap
+                    step = sector ^ where_ref[0]
+                    slot = (jnp.where(step <= 2, 2 - step, step - 1)) * cap + place - sector * cap
                     slot_table[tile * total + entries + entry] = slot
                     op_table[tile * total + entries + entry] = listed[3][tile, entry]
                     return 0
@@ -292,8 +297,8 @@
 
     def kernel(place_ref, dis_ref, *refs):
         out_ref, scratch = refs[devices], refs[devices + 1]
-        for index in range(devices):
-            first = (place_ref[0] ^ index) * dirs
+        for index, other in enumerate(order(devices)):
+            first = (place_ref[0] ^ other) * dirs
             for inner in range(dirs):
                 at = pl.multiple_of((first + inner) * step, step)
                 scratch[pl.ds(at, step), :] = refs[index][inner].astype(jnp.float32)
@@ -314,7 +319,7 @@
         compiler_params=pltpu.CompilerParams(vmem_limit_bytes=20 * MIB),
         cost_estimate=LITTLE,
         name="disaggregate",
-    )(place, disaggregation, *returned)
+    )(place, disaggregation, *[returned[other] for other in order(devices)])
 
 
 def crossed(pieces, axis):
@@ -342,12 +347,15 @@
         cap = send_tiles.shape[2]
         where = lax.axis_index("sector").astype(jnp.int32).reshape(1)
         place = lax.axis_index("dir").astype(jnp.int32).reshape(1)
-        listing = jnp.swapaxes(send_tiles, 1, 2)
-        outgoing = aggregate(fields, aggregation, place, devices)
+        listing = lax.dynamic_index_in_dim(jnp.swapaxes(send_tiles, 1, 2), where[0], 0, keepdims=False)
+        outgoing = list(aggregate(fields, aggregation, place, devices))
+        outgoing[1], listing = barrier((outgoing[1], listing))
         pieces = crossed(outgoing, "dir")
         slab, leaving = pick(pieces, listing, where, place, partners, per_tile)
         leaving, tile_index = barrier((leaving, near_tile))
+        ranks = sorted(range(1, sectors), key=lambda step: 2 - step if step <= 2 else step - 1)
         arrived = crossed([leaving[0], *leaving], "sector")[1:]
+        arrived = [arrived[step - 1] for step in ranks]
         near_blocks, far_blocks = build(
             operators, tile_index, near_operator, far_slot, far_operator, where, partners, cap
         )

time: 56.1 us -> 53.8 us (0.959)
  waiting for transfers between devices: 16.5 us -> 13.8 us
  starting transfers between devices: 16.2 us -> 16.8 us
    ppermute x17, waiting for transfers between devices: 16.5 us -> 13.8 us  [crossed(): lax.ppermute(pieces[step], axis, [(i, i ^ step) for i in range(count)])]
    ppermute x17, starting transfers between devices: 16.2 us -> 16.8 us  [crossed(): lax.ppermute(pieces[step], axis, [(i, i ^ step) for i in range(count)])]
  transfers between devices with their start and end apart: 17 -> 17, of which waited for: 9 -> 10; matrix products, arithmetic and copies ran while one was open for 0% -> 0% of each run, Pallas kernels for 16% -> 17%
where the time goes in v3:
time: 53.8 us; the launch traced here: 53.4 us
  starting transfers between devices  16.8 us (31%)
  Pallas kernels  13.9 us (26%)
  waiting for transfers between devices  13.8 us (26%)
  local copies, waits for them, and re-layouts  8.78 us (16%)
    ppermute x17, starting transfers between devices, crossed(): lax.ppermute(pieces[step], axis, [(i, i ^ step) for i in range(count)])  16.8 us
    ppermute x17, waiting for transfers between devices, crossed(): lax.ppermute(pieces[step], axis, [(i, i ^ step) for i in range(count)])  13.8 us
    unnamed x18, local copies, waits for them, and re-layouts  8.78 us
    pallas_call x1, Pallas kernels, build(): pl.pallas_call(kernel, grid=(dirs,), out_shape=[jax.ShapeDtypeStruct((dir...  5.83 us
    pallas_call x2, Pallas kernels, far_product(): pl.pallas_call(kernel_last if last else kernel, grid=(dirs // group,), ou...  3.08 us
    pallas_call x1, Pallas kernels, disaggregate(): pl.pallas_call(kernel, grid=(boxes // step,), out_shape=jax.ShapeDtypeStr...  1.73 us
    pallas_call x1, Pallas kernels, near_product(): pl.pallas_call(kernel, grid=(dirs // group,), out_shape=jax.ShapeDtypeStr...  1.53 us
    pallas_call x1, Pallas kernels, aggregate(): pl.pallas_call(kernel, out_shape=[jax.ShapeDtypeStruct((part, boxes, colu...  1.08 us
  transfers between devices with their start and end apart: 17, of which 10 were waited for; matrix products, arithmetic and copies ran while one was open for 0% of the time, Pallas kernels for 17%

profile of v3, /device:TPU:16, one launch (start us, length us, event | category | flops | bytes accessed | tf_op | source)
XLA Modules:
  0.0 53.4 jit_solution(16992828455546136183)
XLA Ops:
  0.0 0.7 %copy-done = s32[4,4,2]{1,2,0:T(2,128)S(1)} copy-done((s32[4,4,2]{1,2,0:T(2,128)S(1)}, s32[4,4,2]{1,2,0:T(2,128)}, u32[]{:S(2)}) %copy-start) | copy-done | bytes 152
  0.7 1.2 %copy-done.2 = bf16[32,128,128]{2,1,0:T(8,128)(2,1)S(1)} copy-done((bf16[32,128,128]{2,1,0:T(8,128)(2,1)S(1)}, bf16[32,128,128]{2,1,0:T(8,128)(2,1)}, u32[]{:S(2)}) %copy-start.2) | copy-done | bytes 1048600
  1.9 0.8 %copy-done.3 = bf16[64,256]{1,0:T(8,128)(2,1)S(1)} copy-done((bf16[64,256]{1,0:T(8,128)(2,1)S(1)}, bf16[64,256]{1,0:T(8,128)(2,1)}, u32[]{:S(2)}) %copy-start.3) | copy-done | bytes 32792
  2.7 1.1 %aggregate.1 = (bf16[8,32,128]{2,1,0:T(8,128)(2,1)S(1)}, bf16[8,32,128]{2,1,0:T(8,128)(2,1)S(1)}, bf16[8,32,128]{2,1,0:T(8,128)(2,1)S(1)}, bf16[8,32,128]{2,1,0:...) custom-call(s32[1]{0:T(128)} %bitcast.place_ref, ...), custom_call_target="tpu_custom_call" | custom-call | flops 1 | bytes 1 | tf_op jit(solution)/shard_map/aggregate/pallas_call | solution.py:56
  3.8 0.1 collective-permute-start.6
  3.8 2.6 %collective-permute-start = (bf16[8,32,128]{2,1,0:T(8,128)(2,1)S(1)}, bf16[8,32,128]{2,1,0:T(8,128)(2,1)S(1)}, u32[]{:S(2)}, u32[]{:S(2)}) collective-permute-start(bf16[8,32,128]{2,1,0:T(8,128)(2,1)S(1)} %get-tuple-element.35), channel_id=1, source_target_pairs={{0,7},{1,6},{2,5},{3,4},{4,3},{5,2},{6,1},{7,0},{8,15},{9,14},{10,... | collective-permute-start | bytes 196616 | tf_op jit(solution)/shard_map/ppermute | solution.py:327
  6.4 0.5 collective-permute-start.1
  6.9 0.9 %collective-permute-start.2 = (bf16[8,32,128]{2,1,0:T(8,128)(2,1)S(1)}, bf16[8,32,128]{2,1,0:T(8,128)(2,1)S(1)}, u32[]{:S(2)}, u32[]{:S(2)}) collective-permute-start(bf16[8,32,128]{2,1,0:T(8,128)(2,1)S(1)} %get-tuple-element.37), channel_id=1, source_target_pairs={{0,3},{1,2},{2,1},{3,0},{4,7},{5,6},{6,5},{7,4},{8,11},{9,10},{10,... | collective-permute-start | bytes 196616 | tf_op jit(solution)/shard_map/ppermute | solution.py:327
  7.8 1.9 %collective-permute-start.3 = (bf16[8,32,128]{2,1,0:T(8,128)(2,1)S(1)}, bf16[8,32,128]{2,1,0:T(8,128)(2,1)S(1)}, u32[]{:S(2)}, u32[]{:S(2)}) collective-permute-start(bf16[8,32,128]{2,1,0:T(8,128)(2,1)S(1)} %get-tuple-element.38), channel_id=1, source_target_pairs={{0,5},{1,4},{2,7},{3,6},{4,1},{5,0},{6,3},{7,2},{8,13},{9,12},{10,... | collective-permute-start | bytes 196616 | tf_op jit(solution)/shard_map/ppermute | solution.py:327
  9.6 0.0 collective-permute-done.6.refs_6_
  9.6 0.5 %collective-permute-start.4 = (bf16[8,32,128]{2,1,0:T(8,128)(2,1)S(1)}, bf16[8,32,128]{2,1,0:T(8,128)(2,1)S(1)}, u32[]{:S(2)}, u32[]{:S(2)}) collective-permute-start(bf16[8,32,128]{2,1,0:T(8,128)(2,1)S(1)} %get-tuple-element.39), channel_id=1, source_target_pairs={{0,2},{1,3},{2,0},{3,1},{4,6},{5,7},{6,4},{7,5},{8,10},{9,11},{10,... | collective-permute-start | bytes 196616 | tf_op jit(solution)/shard_map/ppermute | solution.py:327
  10.2 0.0 collective-permute-done.refs_0_
  10.2 0.5 collective-permute-start.5
  10.7 1.6 %collective-permute-done.1.refs_1_ = bf16[8,32,128]{2,1,0:T(8,128)(2,1)S(1)} collective-permute-done((bf16[8,32,128]{2,1,0:T(8,128)(2,1)S(1)}, bf16[8,32,128]{2,1,0:T(8,128)(2,1)S(1)}, u32[]{:S(2)}, u32[]{:S(2)}) %collective-permute-start.1) | collective-permute-done | bytes 65568 | tf_op jit(solution)/shard_map/ppermute | solution.py:327
  12.3 0.0 collective-permute-done.2.refs_2_
  12.3 0.3 collective-permute-done.3.refs_3_
  12.6 1.3 %collective-permute-done.4.refs_4_ = bf16[8,32,128]{2,1,0:T(8,128)(2,1)S(1)} collective-permute-done((bf16[8,32,128]{2,1,0:T(8,128)(2,1)S(1)}, bf16[8,32,128]{2,1,0:T(8,128)(2,1)S(1)}, u32[]{:S(2)}, u32[]{:S(2)}) %collective-permute-start.4) | collective-permute-done | bytes 65568 | tf_op jit(solution)/shard_map/ppermute | solution.py:327
  13.9 0.5 %collective-permute-done.5.refs_5_ = bf16[8,32,128]{2,1,0:T(8,128)(2,1)S(1)} collective-permute-done((bf16[8,32,128]{2,1,0:T(8,128)(2,1)S(1)}, bf16[8,32,128]{2,1,0:T(8,128)(2,1)S(1)}, u32[]{:S(2)}, u32[]{:S(2)}) %collective-permute-start.5) | collective-permute-done | bytes 65568 | tf_op jit(solution)/shard_map/ppermute | solution.py:327
  14.4 0.6 %pick.1 = (bf16[8,8,32,128]{3,2,1,0:T(8,128)(2,1)S(1)}, bf16[2,2,8,32,128]{4,3,2,1,0:T(8,128)(2,1)S(1)}, bf16[2,2,8,32,128]{4,3,2,1,0:T(8,128)(2,1)S(1)}, bf16[2,2,8,32,128]{4,3,2,1,0:T(8,128)(2,1)S(1)}) custom-call(s32[2,4]{1,0:T(2,128)S(1)} %dynamic-slice_bitcast_fusion.listing_ref, s32[1]{0:T(128)} %bitcast.1.where_ref, s32[1]{0:T(128)} %bitcast.place_ref, ...), custom_call_target="tpu_custom_call" | custom-call | flops 1 | bytes 1 | tf_op jit(solution)/shard_map/pick/pallas_call | solution.py:84
  15.1 0.4 collective-permute-start.7
  15.5 1.6 %collective-permute-start.8 = (bf16[2,2,8,32,128]{4,3,2,1,0:T(8,128)(2,1)S(1)}, bf16[2,2,8,32,128]{4,3,2,1,0:T(8,128)(2,1)S(1)}, u32[]{:S(2)}, u32[]{:S(2)}) collective-permute-start(bf16[2,2,8,32,128]{4,3,2,1,0:T(8,128)(2,1)S(1)} %get-tuple-element.51), channel_id=1, source_target_pairs={{0,8},{8,0},{16,24},{24,16},{1,9},{9,1},{17,25},{25,17},{2,10},{10... | collective-permute-start | bytes 786440 | tf_op jit(solution)/shard_map/ppermute | solution.py:327
  17.0 1.6 %collective-permute-start.9 = (bf16[2,2,8,32,128]{4,3,2,1,0:T(8,128)(2,1)S(1)}, bf16[2,2,8,32,128]{4,3,2,1,0:T(8,128)(2,1)S(1)}, u32[]{:S(2)}, u32[]{:S(2)}) collective-permute-start(bf16[2,2,8,32,128]{4,3,2,1,0:T(8,128)(2,1)S(1)} %get-tuple-element.52), channel_id=1, source_target_pairs={{0,24},{8,16},{16,8},{24,0},{1,25},{9,17},{17,9},{25,1},{2,26},{10... | collective-permute-start | bytes 786440 | tf_op jit(solution)/shard_map/ppermute | solution.py:327
  18.6 3.4 %copy-done.1 = bf16[64,8,64,128]{3,2,1,0:T(8,128)(2,1)S(1)} copy-done((bf16[64,8,64,128]{3,2,1,0:T(8,128)(2,1)S(1)}, bf16[64,8,64,128]{3,2,1,0:T(8,128)(2,1)}, u32[]{:S(2)}) %copy-start.1) | copy-done | bytes 8388632
  22.0 0.7 %copy-done.5 = s32[4,16]{1,0:T(4,128)S(1)} copy-done((s32[4,16]{1,0:T(4,128)S(1)}, s32[4,16]{1,0:T(4,128)}, u32[]{:S(2)}) %copy-start.5) | copy-done | bytes 280
  22.7 0.7 %copy-done.6 = s32[4,16]{1,0:T(4,128)S(1)} copy-done((s32[4,16]{1,0:T(4,128)S(1)}, s32[4,16]{1,0:T(4,128)}, u32[]{:S(2)}) %copy-start.6) | copy-done | bytes 280
  23.4 0.7 %copy-done.7 = s32[4,16]{1,0:T(4,128)S(1)} copy-done((s32[4,16]{1,0:T(4,128)S(1)}, s32[4,16]{1,0:T(4,128)}, u32[]{:S(2)}) %copy-start.7) | copy-done | bytes 280
  24.1 0.7 %copy-done.8 = s32[4,16]{1,0:T(4,128)S(1)} copy-done((s32[4,16]{1,0:T(4,128)S(1)}, s32[4,16]{1,0:T(4,128)}, u32[]{:S(2)}) %copy-start.8) | copy-done | bytes 280
  24.7 5.8 %build.1 = (bf16[8,4,256,128]{3,2,1,0:T(8,128)(2,1)S(1)}, bf16[8,6,256,128]{3,2,1,0:T(8,128)(2,1)S(1)}) custom-call(s32[1]{0:T(128)} %bitcast.1.where_ref, s32[4,16]{1,0:T(4,128)S(1)} %copy-done.5, s32[4,16]{1,0:T(4,128)S(1)} %copy-done.6, s32[4,16]{1,0:T(4,128)S(1)} %copy-done.7, s32[4,16]{1,0:T(4,128)S(1)} %copy-done.8, bf16[64,8,64,128]{3,2,1,0:T(8,128)(2,1)S(1)} %copy-done.1), custom_call_target="tpu_custom_call" | custom-call | flops 1 | bytes 1 | tf_op jit(solution)/shard_map/build/pallas_call | solution.py:166
  30.6 1.5 %near_product.1.before_ref = f32[8,256,128]{2,1,0:T(8,128)S(1)} custom-call(bf16[8,4,256,128]{3,2,1,0:T(8,128)(2,1)S(1)} %get-tuple-element.48.block_ref, bf16[8,8,32,128]{3,2,1,0:T(8,128)(2,1)S(1)} %get-tuple-element.49.slab_ref), custom_call_target="tpu_custom_call" | custom-call | flops 1 | bytes 1 | tf_op jit(solution)/shard_map/near_product/pallas_call | solution.py:214
  32.1 0.0 collective-permute-done.7.refs_0_
  32.1 1.7 %far_first.1.before_ref = f32[8,256,128]{2,1,0:T(8,128)S(1)} custom-call(bf16[8,6,256,128]{3,2,1,0:T(8,128)(2,1)S(1)} %get-tuple-element.47.block_ref, f32[8,256,128]{2,1,0:T(8,128)S(1)} %near_product.1.before_ref, bf16[2,2,8,32,128]{4,3,2,1,0:T(8,128)(2,1)S(1)} %collective-permute-done.7.refs_0_, bf16[2,2,8,32,128]{4,3,2,1,0:T(8,128)(2,1)S(1)} %collective-permute-done.8.refs_1_), custom_call_target="tpu_custom_call" | custom-call | flops 1 | bytes 1 | tf_op jit(solution)/shard_map/far_first/pallas_call | solution.py:278
  33.8 0.0 copy-start.4
  33.8 6.6 %collective-permute-done.9.refs_0_ = bf16[2,2,8,32,128]{4,3,2,1,0:T(8,128)(2,1)S(1)} collective-permute-done((bf16[2,2,8,32,128]{4,3,2,1,0:T(8,128)(2,1)S(1)}, bf16[2,2,8,32,128]{4,3,2,1,0:T(8,128)(2,1)S(1)}, u32[]{:S(2)}, u32[]{:S(2)}) %collective-permute-start.9) | collective-permute-done | bytes 262176 | tf_op jit(solution)/shard_map/ppermute | solution.py:327
  40.5 1.4 %far_last.1 = (bf16[8,32,128]{2,1,0:T(8,128)(2,1)S(1)}, bf16[8,32,128]{2,1,0:T(8,128)(2,1)S(1)}, bf16[8,32,128]{2,1,0:T(8,128)(2,1)S(1)}, bf16[8,32,128]{2,1,0:T...) custom-call(s32[1]{0:T(128)} %bitcast.place_ref, ...), custom_call_target="tpu_custom_call" | custom-call | flops 1 | bytes 1 | tf_op jit(solution)/shard_map/far_last/pallas_call | solution.py:278
  41.9 1.6 %collective-permute-start.10 = (bf16[8,32,128]{2,1,0:T(8,128)(2,1)S(1)}, bf16[8,32,128]{2,1,0:T(8,128)(2,1)S(1)}, u32[]{:S(2)}, u32[]{:S(2)}) collective-permute-start(bf16[8,32,128]{2,1,0:T(8,128)(2,1)S(1)} %get-tuple-element.53), channel_id=1, source_target_pairs={{0,7},{1,6},{2,5},{3,4},{4,3},{5,2},{6,1},{7,0},{8,15},{9,14},{10,... | collective-permute-start | bytes 196616 | tf_op jit(solution)/shard_map/ppermute | solution.py:327
  43.4 1.0 %collective-permute-start.11 = (bf16[8,32,128]{2,1,0:T(8,128)(2,1)S(1)}, bf16[8,32,128]{2,1,0:T(8,128)(2,1)S(1)}, u32[]{:S(2)}, u32[]{:S(2)}) collective-permute-start(bf16[8,32,128]{2,1,0:T(8,128)(2,1)S(1)} %get-tuple-element.54), channel_id=1, source_target_pairs={{0,6},{1,7},{2,4},{3,5},{4,2},{5,3},{6,0},{7,1},{8,14},{9,15},{10,... | collective-permute-start | bytes 196616 | tf_op jit(solution)/shard_map/ppermute | solution.py:327
  44.5 0.6 %collective-permute-start.12 = (bf16[8,32,128]{2,1,0:T(8,128)(2,1)S(1)}, bf16[8,32,128]{2,1,0:T(8,128)(2,1)S(1)}, u32[]{:S(2)}, u32[]{:S(2)}) collective-permute-start(bf16[8,32,128]{2,1,0:T(8,128)(2,1)S(1)} %get-tuple-element.55), channel_id=1, source_target_pairs={{0,3},{1,2},{2,1},{3,0},{4,7},{5,6},{6,5},{7,4},{8,11},{9,10},{10,... | collective-permute-start | bytes 196616 | tf_op jit(solution)/shard_map/ppermute | solution.py:327
  45.1 1.6 %collective-permute-start.13 = (bf16[8,32,128]{2,1,0:T(8,128)(2,1)S(1)}, bf16[8,32,128]{2,1,0:T(8,128)(2,1)S(1)}, u32[]{:S(2)}, u32[]{:S(2)}) collective-permute-start(bf16[8,32,128]{2,1,0:T(8,128)(2,1)S(1)} %get-tuple-element.56), channel_id=1, source_target_pairs={{0,5},{1,4},{2,7},{3,6},{4,1},{5,0},{6,3},{7,2},{8,13},{9,12},{10,... | collective-permute-start | bytes 196616 | tf_op jit(solution)/shard_map/ppermute | solution.py:327
  46.7 0.7 %collective-permute-start.14 = (bf16[8,32,128]{2,1,0:T(8,128)(2,1)S(1)}, bf16[8,32,128]{2,1,0:T(8,128)(2,1)S(1)}, u32[]{:S(2)}, u32[]{:S(2)}) collective-permute-start(bf16[8,32,128]{2,1,0:T(8,128)(2,1)S(1)} %get-tuple-element.57), channel_id=1, source_target_pairs={{0,2},{1,3},{2,0},{3,1},{4,6},{5,7},{6,4},{7,5},{8,10},{9,11},{10,... | collective-permute-start | bytes 196616 | tf_op jit(solution)/shard_map/ppermute | solution.py:327
  47.4 0.0 collective-permute-done.10.refs_0_
  47.4 0.8 %collective-permute-start.15 = (bf16[8,32,128]{2,1,0:T(8,128)(2,1)S(1)}, bf16[8,32,128]{2,1,0:T(8,128)(2,1)S(1)}, u32[]{:S(2)}, u32[]{:S(2)}) collective-permute-start(bf16[8,32,128]{2,1,0:T(8,128)(2,1)S(1)} %get-tuple-element.58), channel_id=1, source_target_pairs={{0,4},{1,5},{2,6},{3,7},{4,0},{5,1},{6,2},{7,3},{8,12},{9,13},{10,... | collective-permute-start | bytes 196616 | tf_op jit(solution)/shard_map/ppermute | solution.py:327
  48.2 1.0 %collective-permute-done.11.refs_1_ = bf16[8,32,128]{2,1,0:T(8,128)(2,1)S(1)} collective-permute-done((bf16[8,32,128]{2,1,0:T(8,128)(2,1)S(1)}, bf16[8,32,128]{2,1,0:T(8,128)(2,1)S(1)}, u32[]{:S(2)}, u32[]{:S(2)}) %collective-permute-start.11) | collective-permute-done | bytes 65568 | tf_op jit(solution)/shard_map/ppermute | solution.py:327
  49.2 0.3 collective-permute-done.12.refs_2_
  49.5 0.6 %collective-permute-done.13.refs_3_ = bf16[8,32,128]{2,1,0:T(8,128)(2,1)S(1)} collective-permute-done((bf16[8,32,128]{2,1,0:T(8,128)(2,1)S(1)}, bf16[8,32,128]{2,1,0:T(8,128)(2,1)S(1)}, u32[]{:S(2)}, u32[]{:S(2)}) %collective-permute-start.13) | collective-permute-done | bytes 65568 | tf_op jit(solution)/shard_map/ppermute | solution.py:327
  50.2 1.0 %collective-permute-done.14.refs_4_ = bf16[8,32,128]{2,1,0:T(8,128)(2,1)S(1)} collective-permute-done((bf16[8,32,128]{2,1,0:T(8,128)(2,1)S(1)}, bf16[8,32,128]{2,1,0:T(8,128)(2,1)S(1)}, u32[]{:S(2)}, u32[]{:S(2)}) %collective-permute-start.14) | collective-permute-done | bytes 65568 | tf_op jit(solution)/shard_map/ppermute | solution.py:327
  51.2 0.5 collective-permute-done.15.refs_5_
  51.7 0.0 collective-permute-done.16.refs_6_
  51.7 1.7 %disaggregate.1 = bf16[32,128,128]{2,1,0:T(8,128)(2,1)} custom-call(s32[1]{0:T(128)} %bitcast.place_ref, bf16[128,128]{1,0:T(8,128)(2,1)S(1)} %copy-done.4, bf16[8,32,128]{2,1,0:T(8,128)(2,1)S(1)} %collective-permute-done.10.refs_0_, bf16[8,32,128]{2,1,0:T(8,128)(2,1)S(1)} %collective-permute-done.11.refs_1_, ...), custom_call_target="tpu_custom_call" | custom-call | flops 1 | bytes 1 | tf_op jit(solution)/shard_map/disaggregate/pallas_call | solution.py:310
  (12 shorter events, 0.0 us)
Async XLA Ops:
  0.0 0.7 %copy-start = (s32[4,4,2]{1,2,0:T(2,128)S(1)}, s32[4,4,2]{1,2,0:T(2,128)}, u32[]{:S(2)}) copy-start(s32[4,4,2]{1,2,0:T(2,128)} %param.17) | copy-start | bytes 388
  0.7 1.2 %copy-start.2 = (bf16[32,128,128]{2,1,0:T(8,128)(2,1)S(1)}, bf16[32,128,128]{2,1,0:T(8,128)(2,1)}, u32[]{:S(2)}) copy-start(bf16[32,128,128]{2,1,0:T(8,128)(2,1)} %fields_ref.1) | copy-start | bytes 3145732
  1.9 0.8 %copy-start.3 = (bf16[64,256]{1,0:T(8,128)(2,1)S(1)}, bf16[64,256]{1,0:T(8,128)(2,1)}, u32[]{:S(2)}) copy-start(bf16[64,256]{1,0:T(8,128)(2,1)} %agg_ref.1) | copy-start | bytes 98308
  3.8 5.9 %collective-permute-start.6 = (bf16[8,32,128]{2,1,0:T(8,128)(2,1)S(1)}, bf16[8,32,128]{2,1,0:T(8,128)(2,1)S(1)}, u32[]{:S(2)}, u32[]{:S(2)}) collective-permute-start(bf16[8,32,128]{2,1,0:T(8,128)(2,1)S(1)} %get-tuple-element.41), channel_id=1, source_target_pairs={{0,1},{1,0},{2,3},{3,2},{4,5},{5,4},{6,7},{7,6},{8,9},{9,8},{10,11... | collective-permute-start | bytes 196616 | tf_op jit(solution)/shard_map/ppermute | solution.py:327
  3.8 6.3 %collective-permute-start = (bf16[8,32,128]{2,1,0:T(8,128)(2,1)S(1)}, bf16[8,32,128]{2,1,0:T(8,128)(2,1)S(1)}, u32[]{:S(2)}, u32[]{:S(2)}) collective-permute-start(bf16[8,32,128]{2,1,0:T(8,128)(2,1)S(1)} %get-tuple-element.35), channel_id=1, source_target_pairs={{0,7},{1,6},{2,5},{3,4},{4,3},{5,2},{6,1},{7,0},{8,15},{9,14},{10,... | collective-permute-start | bytes 196616 | tf_op jit(solution)/shard_map/ppermute | solution.py:327
  6.4 5.9 %collective-permute-start.1 = (bf16[8,32,128]{2,1,0:T(8,128)(2,1)S(1)}, bf16[8,32,128]{2,1,0:T(8,128)(2,1)S(1)}, u32[]{:S(2)}, u32[]{:S(2)}) collective-permute-start(bf16[8,32,128]{2,1,0:T(8,128)(2,1)S(1)} %get-tuple-element.36), channel_id=1, source_target_pairs={{0,6},{1,7},{2,4},{3,5},{4,2},{5,3},{6,0},{7,1},{8,14},{9,15},{10,... | collective-permute-start | bytes 196616 | tf_op jit(solution)/shard_map/ppermute | solution.py:327
  6.9 5.4 %collective-permute-start.2 = (bf16[8,32,128]{2,1,0:T(8,128)(2,1)S(1)}, bf16[8,32,128]{2,1,0:T(8,128)(2,1)S(1)}, u32[]{:S(2)}, u32[]{:S(2)}) collective-permute-start(bf16[8,32,128]{2,1,0:T(8,128)(2,1)S(1)} %get-tuple-element.37), channel_id=1, source_target_pairs={{0,3},{1,2},{2,1},{3,0},{4,7},{5,6},{6,5},{7,4},{8,11},{9,10},{10,... | collective-permute-start | bytes 196616 | tf_op jit(solution)/shard_map/ppermute | solution.py:327
  7.8 4.8 %collective-permute-start.3 = (bf16[8,32,128]{2,1,0:T(8,128)(2,1)S(1)}, bf16[8,32,128]{2,1,0:T(8,128)(2,1)S(1)}, u32[]{:S(2)}, u32[]{:S(2)}) collective-permute-start(bf16[8,32,128]{2,1,0:T(8,128)(2,1)S(1)} %get-tuple-element.38), channel_id=1, source_target_pairs={{0,5},{1,4},{2,7},{3,6},{4,1},{5,0},{6,3},{7,2},{8,13},{9,12},{10,... | collective-permute-start | bytes 196616 | tf_op jit(solution)/shard_map/ppermute | solution.py:327
  9.6 4.3 %collective-permute-start.4 = (bf16[8,32,128]{2,1,0:T(8,128)(2,1)S(1)}, bf16[8,32,128]{2,1,0:T(8,128)(2,1)S(1)}, u32[]{:S(2)}, u32[]{:S(2)}) collective-permute-start(bf16[8,32,128]{2,1,0:T(8,128)(2,1)S(1)} %get-tuple-element.39), channel_id=1, source_target_pairs={{0,2},{1,3},{2,0},{3,1},{4,6},{5,7},{6,4},{7,5},{8,10},{9,11},{10,... | collective-permute-start | bytes 196616 | tf_op jit(solution)/shard_map/ppermute | solution.py:327
  10.2 4.3 %collective-permute-start.5 = (bf16[8,32,128]{2,1,0:T(8,128)(2,1)S(1)}, bf16[8,32,128]{2,1,0:T(8,128)(2,1)S(1)}, u32[]{:S(2)}, u32[]{:S(2)}) collective-permute-start(bf16[8,32,128]{2,1,0:T(8,128)(2,1)S(1)} %get-tuple-element.40), channel_id=1, source_target_pairs={{0,4},{1,5},{2,6},{3,7},{4,0},{5,1},{6,2},{7,3},{8,12},{9,13},{10,... | collective-permute-start | bytes 196616 | tf_op jit(solution)/shard_map/ppermute | solution.py:327
  15.1 17.0 %collective-permute-start.7 = (bf16[2,2,8,32,128]{4,3,2,1,0:T(8,128)(2,1)S(1)}, bf16[2,2,8,32,128]{4,3,2,1,0:T(8,128)(2,1)S(1)}, u32[]{:S(2)}, u32[]{:S(2)}) collective-permute-start(bf16[2,2,8,32,128]{4,3,2,1,0:T(8,128)(2,1)S(1)} %get-tuple-element.50), channel_id=1, source_target_pairs={{0,16},{8,24},{16,0},{24,8},{1,17},{9,25},{17,1},{25,9},{2,18},{10... | collective-permute-start | bytes 786440 | tf_op jit(solution)/shard_map/ppermute | solution.py:327
  15.5 16.7 %collective-permute-start.8 = (bf16[2,2,8,32,128]{4,3,2,1,0:T(8,128)(2,1)S(1)}, bf16[2,2,8,32,128]{4,3,2,1,0:T(8,128)(2,1)S(1)}, u32[]{:S(2)}, u32[]{:S(2)}) collective-permute-start(bf16[2,2,8,32,128]{4,3,2,1,0:T(8,128)(2,1)S(1)} %get-tuple-element.51), channel_id=1, source_target_pairs={{0,8},{8,0},{16,24},{24,16},{1,9},{9,1},{17,25},{25,17},{2,10},{10... | collective-permute-start | bytes 786440 | tf_op jit(solution)/shard_map/ppermute | solution.py:327
  17.0 23.4 %collective-permute-start.9 = (bf16[2,2,8,32,128]{4,3,2,1,0:T(8,128)(2,1)S(1)}, bf16[2,2,8,32,128]{4,3,2,1,0:T(8,128)(2,1)S(1)}, u32[]{:S(2)}, u32[]{:S(2)}) collective-permute-start(bf16[2,2,8,32,128]{4,3,2,1,0:T(8,128)(2,1)S(1)} %get-tuple-element.52), channel_id=1, source_target_pairs={{0,24},{8,16},{16,8},{24,0},{1,25},{9,17},{17,9},{25,1},{2,26},{10... | collective-permute-start | bytes 786440 | tf_op jit(solution)/shard_map/ppermute | solution.py:327
  18.6 3.4 %copy-start.1 = (bf16[64,8,64,128]{3,2,1,0:T(8,128)(2,1)S(1)}, bf16[64,8,64,128]{3,2,1,0:T(8,128)(2,1)}, u32[]{:S(2)}) copy-start(bf16[64,8,64,128]{3,2,1,0:T(8,128)(2,1)} %refs_4_.1) | copy-start | bytes 25165828
  22.0 0.7 %copy-start.5 = (s32[4,16]{1,0:T(4,128)S(1)}, s32[4,16]{1,0:T(4,128)}, u32[]{:S(2)}) copy-start(s32[4,16]{1,0:T(4,128)} %refs_0_) | copy-start | bytes 772
  22.7 0.7 %copy-start.6 = (s32[4,16]{1,0:T(4,128)S(1)}, s32[4,16]{1,0:T(4,128)}, u32[]{:S(2)}) copy-start(s32[4,16]{1,0:T(4,128)} %refs_1_.1) | copy-start | bytes 772
  23.4 0.7 %copy-start.7 = (s32[4,16]{1,0:T(4,128)S(1)}, s32[4,16]{1,0:T(4,128)}, u32[]{:S(2)}) copy-start(s32[4,16]{1,0:T(4,128)} %refs_2_.1) | copy-start | bytes 772
  24.1 0.7 %copy-start.8 = (s32[4,16]{1,0:T(4,128)S(1)}, s32[4,16]{1,0:T(4,128)}, u32[]{:S(2)}) copy-start(s32[4,16]{1,0:T(4,128)} %refs_3_.1) | copy-start | bytes 772
  33.8 17.9 %copy-start.4 = (bf16[128,128]{1,0:T(8,128)(2,1)S(1)}, bf16[128,128]{1,0:T(8,128)(2,1)}, u32[]{:S(2)}) copy-start(bf16[128,128]{1,0:T(8,128)(2,1)} %dis_ref.1) | copy-start | bytes 98308
  41.9 5.5 %collective-permute-start.10 = (bf16[8,32,128]{2,1,0:T(8,128)(2,1)S(1)}, bf16[8,32,128]{2,1,0:T(8,128)(2,1)S(1)}, u32[]{:S(2)}, u32[]{:S(2)}) collective-permute-start(bf16[8,32,128]{2,1,0:T(8,128)(2,1)S(1)} %get-tuple-element.53), channel_id=1, source_target_pairs={{0,7},{1,6},{2,5},{3,4},{4,3},{5,2},{6,1},{7,0},{8,15},{9,14},{10,... | collective-permute-start | bytes 196616 | tf_op jit(solution)/shard_map/ppermute | solution.py:327
  43.4 5.8 %collective-permute-start.11 = (bf16[8,32,128]{2,1,0:T(8,128)(2,1)S(1)}, bf16[8,32,128]{2,1,0:T(8,128)(2,1)S(1)}, u32[]{:S(2)}, u32[]{:S(2)}) collective-permute-start(bf16[8,32,128]{2,1,0:T(8,128)(2,1)S(1)} %get-tuple-element.54), channel_id=1, source_target_pairs={{0,6},{1,7},{2,4},{3,5},{4,2},{5,3},{6,0},{7,1},{8,14},{9,15},{10,... | collective-permute-start | bytes 196616 | tf_op jit(solution)/shard_map/ppermute | solution.py:327
  44.5 5.1 %collective-permute-start.12 = (bf16[8,32,128]{2,1,0:T(8,128)(2,1)S(1)}, bf16[8,32,128]{2,1,0:T(8,128)(2,1)S(1)}, u32[]{:S(2)}, u32[]{:S(2)}) collective-permute-start(bf16[8,32,128]{2,1,0:T(8,128)(2,1)S(1)} %get-tuple-element.55), channel_id=1, source_target_pairs={{0,3},{1,2},{2,1},{3,0},{4,7},{5,6},{6,5},{7,4},{8,11},{9,10},{10,... | collective-permute-start | bytes 196616 | tf_op jit(solution)/shard_map/ppermute | solution.py:327
  45.1 5.1 %collective-permute-start.13 = (bf16[8,32,128]{2,1,0:T(8,128)(2,1)S(1)}, bf16[8,32,128]{2,1,0:T(8,128)(2,1)S(1)}, u32[]{:S(2)}, u32[]{:S(2)}) collective-permute-start(bf16[8,32,128]{2,1,0:T(8,128)(2,1)S(1)} %get-tuple-element.56), channel_id=1, source_target_pairs={{0,5},{1,4},{2,7},{3,6},{4,1},{5,0},{6,3},{7,2},{8,13},{9,12},{10,... | collective-permute-start | bytes 196616 | tf_op jit(solution)/shard_map/ppermute | solution.py:327
  46.7 4.5 %collective-permute-start.14 = (bf16[8,32,128]{2,1,0:T(8,128)(2,1)S(1)}, bf16[8,32,128]{2,1,0:T(8,128)(2,1)S(1)}, u32[]{:S(2)}, u32[]{:S(2)}) collective-permute-start(bf16[8,32,128]{2,1,0:T(8,128)(2,1)S(1)} %get-tuple-element.57), channel_id=1, source_target_pairs={{0,2},{1,3},{2,0},{3,1},{4,6},{5,7},{6,4},{7,5},{8,10},{9,11},{10,... | collective-permute-start | bytes 196616 | tf_op jit(solution)/shard_map/ppermute | solution.py:327
  47.4 4.3 %collective-permute-start.15 = (bf16[8,32,128]{2,1,0:T(8,128)(2,1)S(1)}, bf16[8,32,128]{2,1,0:T(8,128)(2,1)S(1)}, u32[]{:S(2)}, u32[]{:S(2)}) collective-permute-start(bf16[8,32,128]{2,1,0:T(8,128)(2,1)S(1)} %get-tuple-element.58), channel_id=1, source_target_pairs={{0,4},{1,5},{2,6},{3,7},{4,0},{5,1},{6,2},{7,3},{8,12},{9,13},{10,... | collective-permute-start | bytes 196616 | tf_op jit(solution)/shard_map/ppermute | solution.py:327
  49.2 2.4 %collective-permute-start.16 = (bf16[8,32,128]{2,1,0:T(8,128)(2,1)S(1)}, bf16[8,32,128]{2,1,0:T(8,128)(2,1)S(1)}, u32[]{:S(2)}, u32[]{:S(2)}) collective-permute-start(bf16[8,32,128]{2,1,0:T(8,128)(2,1)S(1)} %get-tuple-element.59), channel_id=1, source_target_pairs={{0,1},{1,0},{2,3},{3,2},{4,5},{5,4},{6,7},{7,6},{8,9},{9,8},{10,11... | collective-permute-start | bytes 196616 | tf_op jit(solution)/shard_map/ppermute | solution.py:327

commit v4 on v3

--- a/solution.py
+++ b/solution.py
@@ -9,6 +9,7 @@
 STEP_DIRS = 2
 AGG_MIB = 20
 OP_CUTS = 4
+OUT_CUTS = 8
 LITTLE = pl.CostEstimate(flops=1, bytes_accessed=1, transcendentals=0)
 
 
@@ -46,11 +47,11 @@
         matrix = jnp.concatenate([agg_ref[:, :unknowns], agg_ref[:, unknowns:]], axis=0)
         for box in range(boxes):
             both = jnp.dot(matrix, fields_ref[box], preferred_element_type=jnp.float32)
-            scratch[box * all_dirs : (box + 1) * all_dirs, :] = both[:all_dirs] + turned(both[all_dirs:])
+            scratch[pl.ds(box * (all_dirs + 1), all_dirs), :] = both[:all_dirs] + turned(both[all_dirs:])
         for step in range(devices):
             first = (place_ref[0] ^ step) * part
             for inner in range(part):
-                rows = scratch[pl.ds(first + inner, boxes, stride=all_dirs), :]
+                rows = scratch[pl.ds(first + inner, boxes, stride=all_dirs + 1), :]
                 outs[step][inner] = rows.astype(jnp.bfloat16)
 
     return pl.pallas_call(
@@ -58,7 +59,7 @@
         out_shape=[jax.ShapeDtypeStruct((part, boxes, columns), jnp.bfloat16)] * devices,
         in_specs=smem(1) + vmem(2),
         out_specs=vmem(devices),
-        scratch_shapes=[pltpu.VMEM((boxes * all_dirs, columns), jnp.float32)],
+        scratch_shapes=[pltpu.VMEM((boxes * (all_dirs + 1), columns), jnp.float32)],
         compiler_params=pltpu.CompilerParams(vmem_limit_bytes=AGG_MIB * MIB),
         cost_estimate=LITTLE,
         name="aggregate",
@@ -83,10 +84,9 @@
     shapes = [(devices, dirs, boxes, columns)] + [(cap, per_tile, dirs, boxes, columns)] * partners
     outs = pl.pallas_call(
         kernel,
-        grid=(1,),
         out_shape=[jax.ShapeDtypeStruct(shape, jnp.bfloat16) for shape in shapes],
-        in_specs=smem(3) + [pl.BlockSpec(piece.shape, lambda i: (0, 0, 0)) for piece in pieces],
-        out_specs=[pl.BlockSpec(shape, lambda i, n=len(shape): (0,) * n) for shape in shapes],
+        in_specs=smem(3) + vmem(devices),
+        out_specs=vmem(len(shapes)),
         compiler_params=pltpu.CompilerParams(vmem_limit_bytes=20 * MIB),
         cost_estimate=LITTLE,
         name="pick",
@@ -106,9 +106,9 @@
     tables = (near_tile, near_operator, far_slot, far_operator)
 
     def kernel(where_ref, *refs):
-        sources, op_hbm, near_out, far_out = refs[:4], refs[4], refs[5], refs[6]
-        listed, slot_table, op_table, ops, table_sem, op_sem = refs[7:11], refs[11], refs[12], refs[13], refs[14], refs[15]
-        sums = refs[16:]
+        sources, op_hbm, near_out, far_out, last_out = refs[:4], refs[4], refs[5], refs[6], refs[7]
+        listed, slot_table, op_table, ops, table_sem, op_sem = refs[8:12], refs[12], refs[13], refs[14], refs[15], refs[16]
+        sums = refs[17:]
         near_sum, far_sum = sums[:group], sums[group:]
         now = pl.program_id(0)
 
@@ -160,7 +160,8 @@
             for t in range(group):
                 at = pl.ds((base + t) * rows, rows)
                 near_out[:, at, :] = near_sum[t][...].astype(jnp.bfloat16)
-                far_out[:, at, :] = far_sum[t][...].astype(jnp.bfloat16)
+                far_out[:, at, :] = far_sum[t][: slots - cap].astype(jnp.bfloat16)
+                last_out[:, at, :] = far_sum[t][slots - cap :].astype(jnp.bfloat16)
 
     need = 2 * operators.size + 4 * group * (tiles + slots) * rows * wide + 8 * (tiles + slots) * tiles * rows * wide
     return pl.pallas_call(
@@ -168,12 +169,14 @@
         grid=(dirs,),
         out_shape=[
             jax.ShapeDtypeStruct((dirs, tiles, tiles * rows, wide), jnp.bfloat16),
-            jax.ShapeDtypeStruct((dirs, slots, tiles * rows, wide), jnp.bfloat16),
+            jax.ShapeDtypeStruct((dirs, slots - cap, tiles * rows, wide), jnp.bfloat16),
+            jax.ShapeDtypeStruct((dirs, cap, tiles * rows, wide), jnp.bfloat16),
         ],
         in_specs=smem(1) + [pl.BlockSpec(memory_space=pltpu.HBM)] * 5,
         out_specs=[
             pl.BlockSpec((None, tiles, tiles * rows, wide), lambda k: (k, 0, 0, 0)),
-            pl.BlockSpec((None, slots, tiles * rows, wide), lambda k: (k, 0, 0, 0)),
+            pl.BlockSpec((None, slots - cap, tiles * rows, wide), lambda k: (k, 0, 0, 0)),
+            pl.BlockSpec((None, cap, tiles * rows, wide), lambda k: (k, 0, 0, 0)),
         ],
         scratch_shapes=[pltpu.SMEM(table.shape, jnp.int32) for table in tables]
         + [pltpu.SMEM((tiles * total,), jnp.int32)] * 2
@@ -226,66 +229,72 @@
     )(blocks, slab)
 
 
-def far_product(blocks, arrived, first, before, place, devices, per_tile):
-    dirs, _, rows, wide = blocks.shape
-    cap, _, _, boxes, columns = arrived[0].shape
+def far_sources(arrived, inner):
+    sources = []
+    for piece_ref in arrived:
+        for slot in range(piece_ref.shape[0]):
+            pieces = [piece_ref[slot, piece, inner] for piece in range(piece_ref.shape[1])]
+            sources.append(stack_rows(jnp.concatenate(pieces, axis=0)))
+    return jnp.concatenate(sources, axis=0)
+
+
+def far_first(blocks, arrived, before):
+    dirs, slots, rows, wide = blocks.shape
+    cap, per_tile, _, boxes, columns = arrived[0].shape
     count = len(arrived)
-    slots = count * cap
-    last = place is not None
     group = STEP_DIRS if dirs % STEP_DIRS == 0 else 1
 
     def kernel(block_ref, before_ref, *refs):
-        taken, outs = refs[:count], refs[count:]
-        step = pl.program_id(0)
         for inner in range(group):
-            sources = []
-            for index in range(count):
-                for slot in range(cap):
-                    pieces = [taken[index][slot, piece, inner] for piece in range(per_tile)]
-                    sources.append(stack_rows(jnp.concatenate(pieces, axis=0)))
-            total = before_ref[inner] + jnp.dot(
+            refs[count][inner] = before_ref[inner] + jnp.dot(
                 wide_block(block_ref.at[inner], slots),
-                jnp.concatenate(sources, axis=0),
+                far_sources(refs[:count], inner),
                 preferred_element_type=jnp.float32,
             )
-            if last:
-                total_ref = outs[-1]
-                total_ref[inner] = total
-                for index in range(devices):
-                    at = pl.multiple_of((outs[-2][0] ^ index) * boxes, boxes)
-                    outs[index][step * group + inner] = total_ref[inner, pl.ds(at, boxes), :].astype(jnp.bfloat16)
-            else:
-                outs[0][inner] = total
-
-    def kernel_last(place_ref, block_ref, before_ref, *refs):
-        kernel(block_ref, before_ref, *refs[: count + devices], place_ref, refs[count + devices])
-
-    in_specs = [
-        pl.BlockSpec((group, slots, rows, wide), lambda k: (k, first, 0, 0)),
-        pl.BlockSpec((group, rows, columns), lambda k: (k, 0, 0)),
-    ] + [pl.BlockSpec((cap, per_tile, group, boxes, columns), lambda k: (0, 0, k, 0, 0))] * count
-    operands = [blocks, before, *arrived]
-    if last:
-        in_specs = smem(1) + in_specs
-        operands = [place] + operands
-        out_shape = [jax.ShapeDtypeStruct((dirs, boxes, columns), jnp.bfloat16)] * devices
-        out_specs = [pl.BlockSpec((dirs, boxes, columns), lambda k: (0, 0, 0))] * devices
-        scratch = [pltpu.VMEM((group, rows, columns), jnp.float32)]
-    else:
-        out_shape = [jax.ShapeDtypeStruct((dirs, rows, columns), jnp.float32)]
-        out_specs = [pl.BlockSpec((group, rows, columns), lambda k: (k, 0, 0))]
-        scratch = []
-    return pl.pallas_call(
-        kernel_last if last else kernel,
+
+    return pl.pallas_call(
+        kernel,
         grid=(dirs // group,),
-        out_shape=out_shape,
-        in_specs=in_specs,
-        out_specs=out_specs,
-        scratch_shapes=scratch,
+        out_shape=jax.ShapeDtypeStruct((dirs, rows, columns), jnp.float32),
+        in_specs=[
+            pl.BlockSpec((group, slots, rows, wide), lambda k: (k, 0, 0, 0)),
+            pl.BlockSpec((group, rows, columns), lambda k: (k, 0, 0)),
+        ]
+        + [pl.BlockSpec((cap, per_tile, group, boxes, columns), lambda k: (0, 0, k, 0, 0))] * count,
+        out_specs=pl.BlockSpec((group, rows, columns), lambda k: (k, 0, 0)),
         compiler_params=pltpu.CompilerParams(vmem_limit_bytes=40 * MIB),
         cost_estimate=LITTLE,
-        name="far_last" if last else "far_first",
-    )(*operands)
+        name="far_first",
+    )(blocks, before, *arrived)
+
+
+def far_last(blocks, arrived, before, place, devices):
+    dirs, slots, rows, wide = blocks.shape
+    boxes, columns = arrived.shape[-2:]
+
+    def kernel(place_ref, block_ref, before_ref, arrived_ref, *refs):
+        outs, total_ref = refs[:devices], refs[devices]
+        for inner in range(dirs):
+            total_ref[inner] = before_ref[inner] + jnp.dot(
+                wide_block(block_ref.at[inner], slots),
+                far_sources([arrived_ref], inner),
+                preferred_element_type=jnp.float32,
+            )
+        for index in range(devices):
+            at = pl.multiple_of((place_ref[0] ^ index) * boxes, boxes)
+            for inner in range(dirs):
+                outs[index][inner] = total_ref[inner, pl.ds(at, boxes), :].astype(jnp.bfloat16)
+
+    return pl.pallas_call(
+        kernel,
+        out_shape=[jax.ShapeDtypeStruct((dirs, boxes, columns), jnp.bfloat16)] * devices,
+        in_specs=smem(1) + vmem(3),
+        out_specs=vmem(devices),
+        scratch_shapes=[pltpu.VMEM((dirs, rows, columns), jnp.float32)],
+        compiler_params=pltpu.CompilerParams(vmem_limit_bytes=20 * MIB),
+        cost_estimate=LITTLE,
+        name="far_last",
+    )(place, blocks, before, arrived)
 
 
 def disaggregate(returned, disaggregation, place):
@@ -293,29 +302,38 @@
     devices = len(returned)
     unknowns = disaggregation.shape[0]
     all_dirs = disaggregation.shape[1] // 2
-    step = boxes // 2
+    cuts = OUT_CUTS if boxes % OUT_CUTS == 0 else 1
+    size = boxes // cuts
 
     def kernel(place_ref, dis_ref, *refs):
-        out_ref, scratch = refs[devices], refs[devices + 1]
+        out_hbm, scratch, result, sem = refs[devices:]
         for index, other in enumerate(order(devices)):
             first = (place_ref[0] ^ other) * dirs
             for inner in range(dirs):
-                at = pl.multiple_of((first + inner) * step, step)
-                scratch[pl.ds(at, step), :] = refs[index][inner].astype(jnp.float32)
+                at = (first + inner) * (boxes + 1)
+                scratch[pl.ds(at, boxes), :] = refs[index][inner].astype(jnp.float32)
         matrix = dis_ref[...]
-        for box in range(step):
-            rows = stack_rows(scratch[pl.ds(box, all_dirs, stride=step), :])
-            out_ref[box] = jnp.dot(matrix, rows, preferred_element_type=jnp.float32).astype(jnp.bfloat16)
-
-    return pl.pallas_call(
-        kernel,
-        grid=(boxes // step,),
+        copies = []
+        for cut in range(cuts):
+            for box in range(cut * size, (cut + 1) * size):
+                rows = stack_rows(scratch[pl.ds(box, all_dirs, stride=boxes + 1), :])
+                result[box] = jnp.dot(matrix, rows, preferred_element_type=jnp.float32).astype(jnp.bfloat16)
+            at = pl.ds(cut * size, size)
+            copies.append(pltpu.make_async_copy(result.at[at], out_hbm.at[at], sem.at[cut]))
+            copies[cut].start()
+        for copy in copies:
+            copy.wait()
+
+    return pl.pallas_call(
+        kernel,
         out_shape=jax.ShapeDtypeStruct((boxes, unknowns, columns), jnp.bfloat16),
-        in_specs=smem(1)
-        + [pl.BlockSpec(disaggregation.shape, lambda i: (0, 0))]
-        + [pl.BlockSpec((dirs, step, columns), lambda i: (0, i, 0))] * devices,
-        out_specs=pl.BlockSpec((step, unknowns, columns), lambda i: (i, 0, 0)),
-        scratch_shapes=[pltpu.VMEM((all_dirs * step, columns), jnp.float32)],
+        in_specs=smem(1) + vmem(1 + devices),
+        out_specs=pl.BlockSpec(memory_space=pl.ANY),
+        scratch_shapes=[
+            pltpu.VMEM((all_dirs * (boxes + 1), columns), jnp.float32),
+            pltpu.VMEM((boxes, unknowns, columns), jnp.bfloat16),
+            pltpu.SemaphoreType.DMA((cuts,)),
+        ],
         compiler_params=pltpu.CompilerParams(vmem_limit_bytes=20 * MIB),
         cost_estimate=LITTLE,
         name="disaggregate",
@@ -356,12 +374,12 @@
         ranks = sorted(range(1, sectors), key=lambda step: 2 - step if step <= 2 else step - 1)
         arrived = crossed([leaving[0], *leaving], "sector")[1:]
         arrived = [arrived[step - 1] for step in ranks]
-        near_blocks, far_blocks = build(
+        near_blocks, far_blocks, last_blocks = build(
             operators, tile_index, near_operator, far_slot, far_operator, where, partners, cap
         )
         total = near_product(near_blocks, slab, per_tile)
-        total = far_product(far_blocks, arrived[:-1], 0, total, None, devices, per_tile)[0]
-        incoming = far_product(far_blocks, arrived[-1:], partners - 1, total, place, devices, per_tile)
+        total = far_first(far_blocks, arrived[:-1], total)
+        incoming = far_last(last_blocks, arrived[-1], total, place, devices)
         returned = crossed(incoming, "dir")
         return disaggregate(returned, disaggregation, place)
 

time: 53.8 us -> 52.1 us (0.968)
  Pallas kernels: 13.9 us -> 12 us
    pallas_call x4, Pallas kernels: 5.44 us -> 4.09 us  [the longest x1 1.54 us: far_first(): pl.pallas_call(kernel, grid=(dirs // group,), out_shape=jax.ShapeDtypeStr...]
where the time goes in v4:
time: 52.1 us; the launch traced here: 51.7 us
  starting transfers between devices  16.8 us (32%)
  waiting for transfers between devices  13.9 us (27%)
  Pallas kernels  12 us (23%)
  local copies, waits for them, and re-layouts  8.78 us (17%)
    ppermute x17, starting transfers between devices, crossed(): lax.ppermute(pieces[step], axis, [(i, i ^ step) for i in range(count)])  16.8 us
    ppermute x17, waiting for transfers between devices, crossed(): lax.ppermute(pieces[step], axis, [(i, i ^ step) for i in range(count)])  13.9 us
    unnamed x18, local copies, waits for them, and re-layouts  8.78 us
    pallas_call x1, Pallas kernels, build(): pl.pallas_call(kernel, grid=(dirs,), out_shape=[jax.ShapeDtypeStruct((dir...  5.83 us
    pallas_call x1, Pallas kernels, far_first(): pl.pallas_call(kernel, grid=(dirs // group,), out_shape=jax.ShapeDtypeStr...  1.54 us
    pallas_call x1, Pallas kernels, near_product(): pl.pallas_call(kernel, grid=(dirs // group,), out_shape=jax.ShapeDtypeStr...  1.53 us
    pallas_call x1, Pallas kernels, disaggregate(): pl.pallas_call(kernel, out_shape=jax.ShapeDtypeStruct((boxes, unknowns, c...  1.36 us
  transfers between devices with their start and end apart: 17, of which 10 were waited for; matrix products, arithmetic and copies ran while one was open for 0% of the time, Pallas kernels for 17%

profile of v4, /device:TPU:16, one launch (start us, length us, event | category | flops | bytes accessed | tf_op | source)
XLA Modules:
  0.0 51.7 jit_solution(2742610967637248805)
XLA Ops:
  0.0 0.7 %copy-done = s32[4,4,2]{1,2,0:T(2,128)S(1)} copy-done((s32[4,4,2]{1,2,0:T(2,128)S(1)}, s32[4,4,2]{1,2,0:T(2,128)}, u32[]{:S(2)}) %copy-start) | copy-done | bytes 152
  0.7 1.2 %copy-done.2 = bf16[32,128,128]{2,1,0:T(8,128)(2,1)S(1)} copy-done((bf16[32,128,128]{2,1,0:T(8,128)(2,1)S(1)}, bf16[32,128,128]{2,1,0:T(8,128)(2,1)}, u32[]{:S(2)}) %copy-start.2) | copy-done | bytes 1048600
  1.9 0.8 %copy-done.3 = bf16[64,256]{1,0:T(8,128)(2,1)S(1)} copy-done((bf16[64,256]{1,0:T(8,128)(2,1)S(1)}, bf16[64,256]{1,0:T(8,128)(2,1)}, u32[]{:S(2)}) %copy-start.3) | copy-done | bytes 32792
  2.7 0.6 %aggregate.1 = (bf16[8,32,128]{2,1,0:T(8,128)(2,1)S(1)}, bf16[8,32,128]{2,1,0:T(8,128)(2,1)S(1)}, bf16[8,32,128]{2,1,0:T(8,128)(2,1)S(1)}, bf16[8,32,128]{2,1,0:...) custom-call(s32[1]{0:T(128)} %bitcast.place_ref, ...), custom_call_target="tpu_custom_call" | custom-call | flops 1 | bytes 1 | tf_op jit(solution)/shard_map/aggregate/pallas_call | solution.py:57
  3.3 0.1 collective-permute-start.6
  3.3 2.6 %collective-permute-start = (bf16[8,32,128]{2,1,0:T(8,128)(2,1)S(1)}, bf16[8,32,128]{2,1,0:T(8,128)(2,1)S(1)}, u32[]{:S(2)}, u32[]{:S(2)}) collective-permute-start(bf16[8,32,128]{2,1,0:T(8,128)(2,1)S(1)} %get-tuple-element.36), channel_id=1, source_target_pairs={{0,7},{1,6},{2,5},{3,4},{4,3},{5,2},{6,1},{7,0},{8,15},{9,14},{10,... | collective-permute-start | bytes 196616 | tf_op jit(solution)/shard_map/ppermute | solution.py:345
  5.9 0.5 collective-permute-start.1
  6.4 0.9 %collective-permute-start.2 = (bf16[8,32,128]{2,1,0:T(8,128)(2,1)S(1)}, bf16[8,32,128]{2,1,0:T(8,128)(2,1)S(1)}, u32[]{:S(2)}, u32[]{:S(2)}) collective-permute-start(bf16[8,32,128]{2,1,0:T(8,128)(2,1)S(1)} %get-tuple-element.38), channel_id=1, source_target_pairs={{0,3},{1,2},{2,1},{3,0},{4,7},{5,6},{6,5},{7,4},{8,11},{9,10},{10,... | collective-permute-start | bytes 196616 | tf_op jit(solution)/shard_map/ppermute | solution.py:345
  7.3 1.9 %collective-permute-start.3 = (bf16[8,32,128]{2,1,0:T(8,128)(2,1)S(1)}, bf16[8,32,128]{2,1,0:T(8,128)(2,1)S(1)}, u32[]{:S(2)}, u32[]{:S(2)}) collective-permute-start(bf16[8,32,128]{2,1,0:T(8,128)(2,1)S(1)} %get-tuple-element.39), channel_id=1, source_target_pairs={{0,5},{1,4},{2,7},{3,6},{4,1},{5,0},{6,3},{7,2},{8,13},{9,12},{10,... | collective-permute-start | bytes 196616 | tf_op jit(solution)/shard_map/ppermute | solution.py:345
  9.1 0.0 collective-permute-done.6.refs_6_
  9.1 0.5 %collective-permute-start.4 = (bf16[8,32,128]{2,1,0:T(8,128)(2,1)S(1)}, bf16[8,32,128]{2,1,0:T(8,128)(2,1)S(1)}, u32[]{:S(2)}, u32[]{:S(2)}) collective-permute-start(bf16[8,32,128]{2,1,0:T(8,128)(2,1)S(1)} %get-tuple-element.40), channel_id=1, source_target_pairs={{0,2},{1,3},{2,0},{3,1},{4,6},{5,7},{6,4},{7,5},{8,10},{9,11},{10,... | collective-permute-start | bytes 196616 | tf_op jit(solution)/shard_map/ppermute | solution.py:345
  9.6 0.0 collective-permute-done.refs_0_
  9.6 0.5 collective-permute-start.5
  10.2 1.6 %collective-permute-done.1.refs_1_ = bf16[8,32,128]{2,1,0:T(8,128)(2,1)S(1)} collective-permute-done((bf16[8,32,128]{2,1,0:T(8,128)(2,1)S(1)}, bf16[8,32,128]{2,1,0:T(8,128)(2,1)S(1)}, u32[]{:S(2)}, u32[]{:S(2)}) %collective-permute-start.1) | collective-permute-done | bytes 65568 | tf_op jit(solution)/shard_map/ppermute | solution.py:345
  11.8 0.0 collective-permute-done.2.refs_2_
  11.8 0.3 collective-permute-done.3.refs_3_
  12.1 1.3 %collective-permute-done.4.refs_4_ = bf16[8,32,128]{2,1,0:T(8,128)(2,1)S(1)} collective-permute-done((bf16[8,32,128]{2,1,0:T(8,128)(2,1)S(1)}, bf16[8,32,128]{2,1,0:T(8,128)(2,1)S(1)}, u32[]{:S(2)}, u32[]{:S(2)}) %collective-permute-start.4) | collective-permute-done | bytes 65568 | tf_op jit(solution)/shard_map/ppermute | solution.py:345
  13.4 0.5 %collective-permute-done.5.refs_5_ = bf16[8,32,128]{2,1,0:T(8,128)(2,1)S(1)} collective-permute-done((bf16[8,32,128]{2,1,0:T(8,128)(2,1)S(1)}, bf16[8,32,128]{2,1,0:T(8,128)(2,1)S(1)}, u32[]{:S(2)}, u32[]{:S(2)}) %collective-permute-start.5) | collective-permute-done | bytes 65568 | tf_op jit(solution)/shard_map/ppermute | solution.py:345
  13.9 0.6 %pick.1 = (bf16[8,8,32,128]{3,2,1,0:T(8,128)(2,1)S(1)}, bf16[2,2,8,32,128]{4,3,2,1,0:T(8,128)(2,1)S(1)}, bf16[2,2,8,32,128]{4,3,2,1,0:T(8,128)(2,1)S(1)}, bf16[2,2,8,32,128]{4,3,2,1,0:T(8,128)(2,1)S(1)}) custom-call(s32[2,4]{1,0:T(2,128)S(1)} %dynamic-slice_bitcast_fusion.listing_ref, s32[1]{0:T(128)} %bitcast.1.where_ref, s32[1]{0:T(128)} %bitcast.place_ref, ...), custom_call_target="tpu_custom_call" | custom-call | flops 1 | bytes 1 | tf_op jit(solution)/shard_map/pick/pallas_call | solution.py:85
  14.6 0.4 collective-permute-start.7
  15.0 1.6 %collective-permute-start.8 = (bf16[2,2,8,32,128]{4,3,2,1,0:T(8,128)(2,1)S(1)}, bf16[2,2,8,32,128]{4,3,2,1,0:T(8,128)(2,1)S(1)}, u32[]{:S(2)}, u32[]{:S(2)}) collective-permute-start(bf16[2,2,8,32,128]{4,3,2,1,0:T(8,128)(2,1)S(1)} %get-tuple-element.53), channel_id=1, source_target_pairs={{0,8},{8,0},{16,24},{24,16},{1,9},{9,1},{17,25},{25,17},{2,10},{10... | collective-permute-start | bytes 786440 | tf_op jit(solution)/shard_map/ppermute | solution.py:345
  16.5 1.6 %collective-permute-start.9 = (bf16[2,2,8,32,128]{4,3,2,1,0:T(8,128)(2,1)S(1)}, bf16[2,2,8,32,128]{4,3,2,1,0:T(8,128)(2,1)S(1)}, u32[]{:S(2)}, u32[]{:S(2)}) collective-permute-start(bf16[2,2,8,32,128]{4,3,2,1,0:T(8,128)(2,1)S(1)} %get-tuple-element.54), channel_id=1, source_target_pairs={{0,24},{8,16},{16,8},{24,0},{1,25},{9,17},{17,9},{25,1},{2,26},{10... | collective-permute-start | bytes 786440 | tf_op jit(solution)/shard_map/ppermute | solution.py:345
  18.1 3.4 %copy-done.1 = bf16[64,8,64,128]{3,2,1,0:T(8,128)(2,1)S(1)} copy-done((bf16[64,8,64,128]{3,2,1,0:T(8,128)(2,1)S(1)}, bf16[64,8,64,128]{3,2,1,0:T(8,128)(2,1)}, u32[]{:S(2)}) %copy-start.1) | copy-done | bytes 8388632
  21.5 0.7 %copy-done.5 = s32[4,16]{1,0:T(4,128)S(1)} copy-done((s32[4,16]{1,0:T(4,128)S(1)}, s32[4,16]{1,0:T(4,128)}, u32[]{:S(2)}) %copy-start.5) | copy-done | bytes 280
  22.2 0.7 %copy-done.6 = s32[4,16]{1,0:T(4,128)S(1)} copy-done((s32[4,16]{1,0:T(4,128)S(1)}, s32[4,16]{1,0:T(4,128)}, u32[]{:S(2)}) %copy-start.6) | copy-done | bytes 280
  22.9 0.7 %copy-done.7 = s32[4,16]{1,0:T(4,128)S(1)} copy-done((s32[4,16]{1,0:T(4,128)S(1)}, s32[4,16]{1,0:T(4,128)}, u32[]{:S(2)}) %copy-start.7) | copy-done | bytes 280
  23.5 0.7 %copy-done.8 = s32[4,16]{1,0:T(4,128)S(1)} copy-done((s32[4,16]{1,0:T(4,128)S(1)}, s32[4,16]{1,0:T(4,128)}, u32[]{:S(2)}) %copy-start.8) | copy-done | bytes 280
  24.2 5.8 %build.1 = (bf16[8,4,256,128]{3,2,1,0:T(8,128)(2,1)S(1)}, bf16[8,4,256,128]{3,2,1,0:T(8,128)(2,1)S(1)}, bf16[8,2,256,128]{3,2,1,0:T(8,128)(2,1)S(1)}) custom-call(s32[1]{0:T(128)} %bitcast.1.where_ref, s32[4,16]{1,0:T(4,128)S(1)} %copy-done.5, s32[4,16]{1,0:T(4,128)S(1)} %copy-done.6, s32[4,16]{1,0:T(4,128)S(1)} %copy-done.7, s32[4,16]{1,0:T(4,128)S(1)} %copy-done.8, ...), custom_call_target="tpu_custom_call" | custom-call | flops 1 | bytes 1 | tf_op jit(solution)/shard_map/build/pallas_call | solution.py:167
  30.1 1.5 %near_product.1.before_ref = f32[8,256,128]{2,1,0:T(8,128)S(1)} custom-call(bf16[8,4,256,128]{3,2,1,0:T(8,128)(2,1)S(1)} %get-tuple-element.50.block_ref, bf16[8,8,32,128]{3,2,1,0:T(8,128)(2,1)S(1)} %get-tuple-element.51.slab_ref), custom_call_target="tpu_custom_call" | custom-call | flops 1 | bytes 1 | tf_op jit(solution)/shard_map/near_product/pallas_call | solution.py:217
  31.6 0.0 collective-permute-done.7.refs_0_
  31.6 0.0 collective-permute-done.8.refs_1_
  31.6 1.5 %far_first.1.before_ref = f32[8,256,128]{2,1,0:T(8,128)S(1)} custom-call(bf16[8,4,256,128]{3,2,1,0:T(8,128)(2,1)S(1)} %get-tuple-element.49.block_ref, f32[8,256,128]{2,1,0:T(8,128)S(1)} %near_product.1.before_ref, bf16[2,2,8,32,128]{4,3,2,1,0:T(8,128)(2,1)S(1)} %collective-permute-done.7.refs_0_, bf16[2,2,8,32,128]{4,3,2,1,0:T(8,128)(2,1)S(1)} %collective-permute-done.8.refs_1_), custom_call_target="tpu_custom_call" | custom-call | flops 1 | bytes 1 | tf_op jit(solution)/shard_map/far_first/pallas_call | solution.py:255
  33.2 0.0 copy-start.4
  33.2 6.8 %collective-permute-done.9.arrived_ref = bf16[2,2,8,32,128]{4,3,2,1,0:T(8,128)(2,1)S(1)} collective-permute-done((bf16[2,2,8,32,128]{4,3,2,1,0:T(8,128)(2,1)S(1)}, bf16[2,2,8,32,128]{4,3,2,1,0:T(8,128)(2,1)S(1)}, u32[]{:S(2)}, u32[]{:S(2)}) %collective-permute-start.9) | collective-permute-done | bytes 262176 | tf_op jit(solution)/shard_map/ppermute | solution.py:345
  40.0 0.5 %far_last.1 = (bf16[8,32,128]{2,1,0:T(8,128)(2,1)S(1)}, bf16[8,32,128]{2,1,0:T(8,128)(2,1)S(1)}, bf16[8,32,128]{2,1,0:T(8,128)(2,1)S(1)}, bf16[8,32,128]{2,1,0:T...) custom-call(s32[1]{0:T(128)} %bitcast.place_ref, ...), custom_call_target="tpu_custom_call" | custom-call | flops 1 | bytes 1 | tf_op jit(solution)/shard_map/far_last/pallas_call | solution.py:288
  40.5 1.6 %collective-permute-start.10 = (bf16[8,32,128]{2,1,0:T(8,128)(2,1)S(1)}, bf16[8,32,128]{2,1,0:T(8,128)(2,1)S(1)}, u32[]{:S(2)}, u32[]{:S(2)}) collective-permute-start(bf16[8,32,128]{2,1,0:T(8,128)(2,1)S(1)} %get-tuple-element.55), channel_id=1, source_target_pairs={{0,7},{1,6},{2,5},{3,4},{4,3},{5,2},{6,1},{7,0},{8,15},{9,14},{10,... | collective-permute-start | bytes 196616 | tf_op jit(solution)/shard_map/ppermute | solution.py:345
  42.1 1.0 %collective-permute-start.11 = (bf16[8,32,128]{2,1,0:T(8,128)(2,1)S(1)}, bf16[8,32,128]{2,1,0:T(8,128)(2,1)S(1)}, u32[]{:S(2)}, u32[]{:S(2)}) collective-permute-start(bf16[8,32,128]{2,1,0:T(8,128)(2,1)S(1)} %get-tuple-element.56), channel_id=1, source_target_pairs={{0,6},{1,7},{2,4},{3,5},{4,2},{5,3},{6,0},{7,1},{8,14},{9,15},{10,... | collective-permute-start | bytes 196616 | tf_op jit(solution)/shard_map/ppermute | solution.py:345
  43.1 0.6 %collective-permute-start.12 = (bf16[8,32,128]{2,1,0:T(8,128)(2,1)S(1)}, bf16[8,32,128]{2,1,0:T(8,128)(2,1)S(1)}, u32[]{:S(2)}, u32[]{:S(2)}) collective-permute-start(bf16[8,32,128]{2,1,0:T(8,128)(2,1)S(1)} %get-tuple-element.57), channel_id=1, source_target_pairs={{0,3},{1,2},{2,1},{3,0},{4,7},{5,6},{6,5},{7,4},{8,11},{9,10},{10,... | collective-permute-start | bytes 196616 | tf_op jit(solution)/shard_map/ppermute | solution.py:345
  43.7 1.6 %collective-permute-start.13 = (bf16[8,32,128]{2,1,0:T(8,128)(2,1)S(1)}, bf16[8,32,128]{2,1,0:T(8,128)(2,1)S(1)}, u32[]{:S(2)}, u32[]{:S(2)}) collective-permute-start(bf16[8,32,128]{2,1,0:T(8,128)(2,1)S(1)} %get-tuple-element.58), channel_id=1, source_target_pairs={{0,5},{1,4},{2,7},{3,6},{4,1},{5,0},{6,3},{7,2},{8,13},{9,12},{10,... | collective-permute-start | bytes 196616 | tf_op jit(solution)/shard_map/ppermute | solution.py:345
  45.3 0.7 %collective-permute-start.14 = (bf16[8,32,128]{2,1,0:T(8,128)(2,1)S(1)}, bf16[8,32,128]{2,1,0:T(8,128)(2,1)S(1)}, u32[]{:S(2)}, u32[]{:S(2)}) collective-permute-start(bf16[8,32,128]{2,1,0:T(8,128)(2,1)S(1)} %get-tuple-element.59), channel_id=1, source_target_pairs={{0,2},{1,3},{2,0},{3,1},{4,6},{5,7},{6,4},{7,5},{8,10},{9,11},{10,... | collective-permute-start | bytes 196616 | tf_op jit(solution)/shard_map/ppermute | solution.py:345
  46.0 0.0 collective-permute-done.10.refs_0_
  46.0 0.8 %collective-permute-start.15 = (bf16[8,32,128]{2,1,0:T(8,128)(2,1)S(1)}, bf16[8,32,128]{2,1,0:T(8,128)(2,1)S(1)}, u32[]{:S(2)}, u32[]{:S(2)}) collective-permute-start(bf16[8,32,128]{2,1,0:T(8,128)(2,1)S(1)} %get-tuple-element.60), channel_id=1, source_target_pairs={{0,4},{1,5},{2,6},{3,7},{4,0},{5,1},{6,2},{7,3},{8,12},{9,13},{10,... | collective-permute-start | bytes 196616 | tf_op jit(solution)/shard_map/ppermute | solution.py:345
  46.9 1.0 %collective-permute-done.11.refs_1_ = bf16[8,32,128]{2,1,0:T(8,128)(2,1)S(1)} collective-permute-done((bf16[8,32,128]{2,1,0:T(8,128)(2,1)S(1)}, bf16[8,32,128]{2,1,0:T(8,128)(2,1)S(1)}, u32[]{:S(2)}, u32[]{:S(2)}) %collective-permute-start.11) | collective-permute-done | bytes 65568 | tf_op jit(solution)/shard_map/ppermute | solution.py:345
  47.9 0.3 collective-permute-done.12.refs_2_
  48.2 0.6 %collective-permute-done.13.refs_3_ = bf16[8,32,128]{2,1,0:T(8,128)(2,1)S(1)} collective-permute-done((bf16[8,32,128]{2,1,0:T(8,128)(2,1)S(1)}, bf16[8,32,128]{2,1,0:T(8,128)(2,1)S(1)}, u32[]{:S(2)}, u32[]{:S(2)}) %collective-permute-start.13) | collective-permute-done | bytes 65568 | tf_op jit(solution)/shard_map/ppermute | solution.py:345
  48.8 1.0 %collective-permute-done.14.refs_4_ = bf16[8,32,128]{2,1,0:T(8,128)(2,1)S(1)} collective-permute-done((bf16[8,32,128]{2,1,0:T(8,128)(2,1)S(1)}, bf16[8,32,128]{2,1,0:T(8,128)(2,1)S(1)}, u32[]{:S(2)}, u32[]{:S(2)}) %collective-permute-start.14) | collective-permute-done | bytes 65568 | tf_op jit(solution)/shard_map/ppermute | solution.py:345
  49.8 0.5 %collective-permute-done.15.refs_5_ = bf16[8,32,128]{2,1,0:T(8,128)(2,1)S(1)} collective-permute-done((bf16[8,32,128]{2,1,0:T(8,128)(2,1)S(1)}, bf16[8,32,128]{2,1,0:T(8,128)(2,1)S(1)}, u32[]{:S(2)}, u32[]{:S(2)}) %collective-permute-start.15) | collective-permute-done | bytes 65568 | tf_op jit(solution)/shard_map/ppermute | solution.py:345
  50.3 1.4 %disaggregate.1 = bf16[32,128,128]{2,1,0:T(8,128)(2,1)} custom-call(s32[1]{0:T(128)} %bitcast.place_ref, bf16[128,128]{1,0:T(8,128)(2,1)S(1)} %copy-done.4, bf16[8,32,128]{2,1,0:T(8,128)(2,1)S(1)} %collective-permute-done.10.refs_0_, bf16[8,32,128]{2,1,0:T(8,128)(2,1)S(1)} %collective-permute-done.11.refs_1_, ...), custom_call_target="tpu_custom_call" | custom-call | flops 1 | bytes 1 | tf_op jit(solution)/shard_map/disaggregate/pallas_call | solution.py:327
  (12 shorter events, 0.0 us)
Async XLA Ops:
  0.0 0.7 %copy-start = (s32[4,4,2]{1,2,0:T(2,128)S(1)}, s32[4,4,2]{1,2,0:T(2,128)}, u32[]{:S(2)}) copy-start(s32[4,4,2]{1,2,0:T(2,128)} %param.17) | copy-start | bytes 388
  0.7 1.2 %copy-start.2 = (bf16[32,128,128]{2,1,0:T(8,128)(2,1)S(1)}, bf16[32,128,128]{2,1,0:T(8,128)(2,1)}, u32[]{:S(2)}) copy-start(bf16[32,128,128]{2,1,0:T(8,128)(2,1)} %fields_ref.1) | copy-start | bytes 3145732
  1.9 0.8 %copy-start.3 = (bf16[64,256]{1,0:T(8,128)(2,1)S(1)}, bf16[64,256]{1,0:T(8,128)(2,1)}, u32[]{:S(2)}) copy-start(bf16[64,256]{1,0:T(8,128)(2,1)} %agg_ref.1) | copy-start | bytes 98308
  3.3 5.9 %collective-permute-start.6 = (bf16[8,32,128]{2,1,0:T(8,128)(2,1)S(1)}, bf16[8,32,128]{2,1,0:T(8,128)(2,1)S(1)}, u32[]{:S(2)}, u32[]{:S(2)}) collective-permute-start(bf16[8,32,128]{2,1,0:T(8,128)(2,1)S(1)} %get-tuple-element.42), channel_id=1, source_target_pairs={{0,1},{1,0},{2,3},{3,2},{4,5},{5,4},{6,7},{7,6},{8,9},{9,8},{10,11... | collective-permute-start | bytes 196616 | tf_op jit(solution)/shard_map/ppermute | solution.py:345
  3.3 6.3 %collective-permute-start = (bf16[8,32,128]{2,1,0:T(8,128)(2,1)S(1)}, bf16[8,32,128]{2,1,0:T(8,128)(2,1)S(1)}, u32[]{:S(2)}, u32[]{:S(2)}) collective-permute-start(bf16[8,32,128]{2,1,0:T(8,128)(2,1)S(1)} %get-tuple-element.36), channel_id=1, source_target_pairs={{0,7},{1,6},{2,5},{3,4},{4,3},{5,2},{6,1},{7,0},{8,15},{9,14},{10,... | collective-permute-start | bytes 196616 | tf_op jit(solution)/shard_map/ppermute | solution.py:345
  5.9 5.9 %collective-permute-start.1 = (bf16[8,32,128]{2,1,0:T(8,128)(2,1)S(1)}, bf16[8,32,128]{2,1,0:T(8,128)(2,1)S(1)}, u32[]{:S(2)}, u32[]{:S(2)}) collective-permute-start(bf16[8,32,128]{2,1,0:T(8,128)(2,1)S(1)} %get-tuple-element.37), channel_id=1, source_target_pairs={{0,6},{1,7},{2,4},{3,5},{4,2},{5,3},{6,0},{7,1},{8,14},{9,15},{10,... | collective-permute-start | bytes 196616 | tf_op jit(solution)/shard_map/ppermute | solution.py:345
  6.4 5.4 %collective-permute-start.2 = (bf16[8,32,128]{2,1,0:T(8,128)(2,1)S(1)}, bf16[8,32,128]{2,1,0:T(8,128)(2,1)S(1)}, u32[]{:S(2)}, u32[]{:S(2)}) collective-permute-start(bf16[8,32,128]{2,1,0:T(8,128)(2,1)S(1)} %get-tuple-element.38), channel_id=1, source_target_pairs={{0,3},{1,2},{2,1},{3,0},{4,7},{5,6},{6,5},{7,4},{8,11},{9,10},{10,... | collective-permute-start | bytes 196616 | tf_op jit(solution)/shard_map/ppermute | solution.py:345
  7.3 4.8 %collective-permute-start.3 = (bf16[8,32,128]{2,1,0:T(8,128)(2,1)S(1)}, bf16[8,32,128]{2,1,0:T(8,128)(2,1)S(1)}, u32[]{:S(2)}, u32[]{:S(2)}) collective-permute-start(bf16[8,32,128]{2,1,0:T(8,128)(2,1)S(1)} %get-tuple-element.39), channel_id=1, source_target_pairs={{0,5},{1,4},{2,7},{3,6},{4,1},{5,0},{6,3},{7,2},{8,13},{9,12},{10,... | collective-permute-start | bytes 196616 | tf_op jit(solution)/shard_map/ppermute | solution.py:345
  9.1 4.3 %collective-permute-start.4 = (bf16[8,32,128]{2,1,0:T(8,128)(2,1)S(1)}, bf16[8,32,128]{2,1,0:T(8,128)(2,1)S(1)}, u32[]{:S(2)}, u32[]{:S(2)}) collective-permute-start(bf16[8,32,128]{2,1,0:T(8,128)(2,1)S(1)} %get-tuple-element.40), channel_id=1, source_target_pairs={{0,2},{1,3},{2,0},{3,1},{4,6},{5,7},{6,4},{7,5},{8,10},{9,11},{10,... | collective-permute-start | bytes 196616 | tf_op jit(solution)/shard_map/ppermute | solution.py:345
  9.6 4.3 %collective-permute-start.5 = (bf16[8,32,128]{2,1,0:T(8,128)(2,1)S(1)}, bf16[8,32,128]{2,1,0:T(8,128)(2,1)S(1)}, u32[]{:S(2)}, u32[]{:S(2)}) collective-permute-start(bf16[8,32,128]{2,1,0:T(8,128)(2,1)S(1)} %get-tuple-element.41), channel_id=1, source_target_pairs={{0,4},{1,5},{2,6},{3,7},{4,0},{5,1},{6,2},{7,3},{8,12},{9,13},{10,... | collective-permute-start | bytes 196616 | tf_op jit(solution)/shard_map/ppermute | solution.py:345
  14.6 17.0 %collective-permute-start.7 = (bf16[2,2,8,32,128]{4,3,2,1,0:T(8,128)(2,1)S(1)}, bf16[2,2,8,32,128]{4,3,2,1,0:T(8,128)(2,1)S(1)}, u32[]{:S(2)}, u32[]{:S(2)}) collective-permute-start(bf16[2,2,8,32,128]{4,3,2,1,0:T(8,128)(2,1)S(1)} %get-tuple-element.52), channel_id=1, source_target_pairs={{0,16},{8,24},{16,0},{24,8},{1,17},{9,25},{17,1},{25,9},{2,18},{10... | collective-permute-start | bytes 786440 | tf_op jit(solution)/shard_map/ppermute | solution.py:345
  15.0 16.7 %collective-permute-start.8 = (bf16[2,2,8,32,128]{4,3,2,1,0:T(8,128)(2,1)S(1)}, bf16[2,2,8,32,128]{4,3,2,1,0:T(8,128)(2,1)S(1)}, u32[]{:S(2)}, u32[]{:S(2)}) collective-permute-start(bf16[2,2,8,32,128]{4,3,2,1,0:T(8,128)(2,1)S(1)} %get-tuple-element.53), channel_id=1, source_target_pairs={{0,8},{8,0},{16,24},{24,16},{1,9},{9,1},{17,25},{25,17},{2,10},{10... | collective-permute-start | bytes 786440 | tf_op jit(solution)/shard_map/ppermute | solution.py:345
  16.5 23.4 %collective-permute-start.9 = (bf16[2,2,8,32,128]{4,3,2,1,0:T(8,128)(2,1)S(1)}, bf16[2,2,8,32,128]{4,3,2,1,0:T(8,128)(2,1)S(1)}, u32[]{:S(2)}, u32[]{:S(2)}) collective-permute-start(bf16[2,2,8,32,128]{4,3,2,1,0:T(8,128)(2,1)S(1)} %get-tuple-element.54), channel_id=1, source_target_pairs={{0,24},{8,16},{16,8},{24,0},{1,25},{9,17},{17,9},{25,1},{2,26},{10... | collective-permute-start | bytes 786440 | tf_op jit(solution)/shard_map/ppermute | solution.py:345
  18.1 3.4 %copy-start.1 = (bf16[64,8,64,128]{3,2,1,0:T(8,128)(2,1)S(1)}, bf16[64,8,64,128]{3,2,1,0:T(8,128)(2,1)}, u32[]{:S(2)}) copy-start(bf16[64,8,64,128]{3,2,1,0:T(8,128)(2,1)} %refs_4_.1) | copy-start | bytes 25165828
  21.5 0.7 %copy-start.5 = (s32[4,16]{1,0:T(4,128)S(1)}, s32[4,16]{1,0:T(4,128)}, u32[]{:S(2)}) copy-start(s32[4,16]{1,0:T(4,128)} %refs_0_) | copy-start | bytes 772
  22.2 0.7 %copy-start.6 = (s32[4,16]{1,0:T(4,128)S(1)}, s32[4,16]{1,0:T(4,128)}, u32[]{:S(2)}) copy-start(s32[4,16]{1,0:T(4,128)} %refs_1_.1) | copy-start | bytes 772
  22.9 0.7 %copy-start.7 = (s32[4,16]{1,0:T(4,128)S(1)}, s32[4,16]{1,0:T(4,128)}, u32[]{:S(2)}) copy-start(s32[4,16]{1,0:T(4,128)} %refs_2_.1) | copy-start | bytes 772
  23.5 0.7 %copy-start.8 = (s32[4,16]{1,0:T(4,128)S(1)}, s32[4,16]{1,0:T(4,128)}, u32[]{:S(2)}) copy-start(s32[4,16]{1,0:T(4,128)} %refs_3_.1) | copy-start | bytes 772
  33.2 17.1 %copy-start.4 = (bf16[128,128]{1,0:T(8,128)(2,1)S(1)}, bf16[128,128]{1,0:T(8,128)(2,1)}, u32[]{:S(2)}) copy-start(bf16[128,128]{1,0:T(8,128)(2,1)} %dis_ref.1) | copy-start | bytes 98308
  40.5 5.5 %collective-permute-start.10 = (bf16[8,32,128]{2,1,0:T(8,128)(2,1)S(1)}, bf16[8,32,128]{2,1,0:T(8,128)(2,1)S(1)}, u32[]{:S(2)}, u32[]{:S(2)}) collective-permute-start(bf16[8,32,128]{2,1,0:T(8,128)(2,1)S(1)} %get-tuple-element.55), channel_id=1, source_target_pairs={{0,7},{1,6},{2,5},{3,4},{4,3},{5,2},{6,1},{7,0},{8,15},{9,14},{10,... | collective-permute-start | bytes 196616 | tf_op jit(solution)/shard_map/ppermute | solution.py:345
  42.1 5.8 %collective-permute-start.11 = (bf16[8,32,128]{2,1,0:T(8,128)(2,1)S(1)}, bf16[8,32,128]{2,1,0:T(8,128)(2,1)S(1)}, u32[]{:S(2)}, u32[]{:S(2)}) collective-permute-start(bf16[8,32,128]{2,1,0:T(8,128)(2,1)S(1)} %get-tuple-element.56), channel_id=1, source_target_pairs={{0,6},{1,7},{2,4},{3,5},{4,2},{5,3},{6,0},{7,1},{8,14},{9,15},{10,... | collective-permute-start | bytes 196616 | tf_op jit(solution)/shard_map/ppermute | solution.py:345
  43.1 5.1 %collective-permute-start.12 = (bf16[8,32,128]{2,1,0:T(8,128)(2,1)S(1)}, bf16[8,32,128]{2,1,0:T(8,128)(2,1)S(1)}, u32[]{:S(2)}, u32[]{:S(2)}) collective-permute-start(bf16[8,32,128]{2,1,0:T(8,128)(2,1)S(1)} %get-tuple-element.57), channel_id=1, source_target_pairs={{0,3},{1,2},{2,1},{3,0},{4,7},{5,6},{6,5},{7,4},{8,11},{9,10},{10,... | collective-permute-start | bytes 196616 | tf_op jit(solution)/shard_map/ppermute | solution.py:345
  43.7 5.1 %collective-permute-start.13 = (bf16[8,32,128]{2,1,0:T(8,128)(2,1)S(1)}, bf16[8,32,128]{2,1,0:T(8,128)(2,1)S(1)}, u32[]{:S(2)}, u32[]{:S(2)}) collective-permute-start(bf16[8,32,128]{2,1,0:T(8,128)(2,1)S(1)} %get-tuple-element.58), channel_id=1, source_target_pairs={{0,5},{1,4},{2,7},{3,6},{4,1},{5,0},{6,3},{7,2},{8,13},{9,12},{10,... | collective-permute-start | bytes 196616 | tf_op jit(solution)/shard_map/ppermute | solution.py:345
  45.3 4.5 %collective-permute-start.14 = (bf16[8,32,128]{2,1,0:T(8,128)(2,1)S(1)}, bf16[8,32,128]{2,1,0:T(8,128)(2,1)S(1)}, u32[]{:S(2)}, u32[]{:S(2)}) collective-permute-start(bf16[8,32,128]{2,1,0:T(8,128)(2,1)S(1)} %get-tuple-element.59), channel_id=1, source_target_pairs={{0,2},{1,3},{2,0},{3,1},{4,6},{5,7},{6,4},{7,5},{8,10},{9,11},{10,... | collective-permute-start | bytes 196616 | tf_op jit(solution)/shard_map/ppermute | solution.py:345
  46.0 4.3 %collective-permute-start.15 = (bf16[8,32,128]{2,1,0:T(8,128)(2,1)S(1)}, bf16[8,32,128]{2,1,0:T(8,128)(2,1)S(1)}, u32[]{:S(2)}, u32[]{:S(2)}) collective-permute-start(bf16[8,32,128]{2,1,0:T(8,128)(2,1)S(1)} %get-tuple-element.60), channel_id=1, source_target_pairs={{0,4},{1,5},{2,6},{3,7},{4,0},{5,1},{6,2},{7,3},{8,12},{9,13},{10,... | collective-permute-start | bytes 196616 | tf_op jit(solution)/shard_map/ppermute | solution.py:345
  47.9 2.4 %collective-permute-start.16 = (bf16[8,32,128]{2,1,0:T(8,128)(2,1)S(1)}, bf16[8,32,128]{2,1,0:T(8,128)(2,1)S(1)}, u32[]{:S(2)}, u32[]{:S(2)}) collective-permute-start(bf16[8,32,128]{2,1,0:T(8,128)(2,1)S(1)} %get-tuple-element.61), channel_id=1, source_target_pairs={{0,1},{1,0},{2,3},{3,2},{4,5},{5,4},{6,7},{7,6},{8,9},{9,8},{10,11... | collective-permute-start | bytes 196616 | tf_op jit(solution)/shard_map/ppermute | solution.py:345

commit v5 on v4

--- a/solution.py
+++ b/solution.py
@@ -367,7 +367,7 @@
         place = lax.axis_index("dir").astype(jnp.int32).reshape(1)
         listing = lax.dynamic_index_in_dim(jnp.swapaxes(send_tiles, 1, 2), where[0], 0, keepdims=False)
         outgoing = list(aggregate(fields, aggregation, place, devices))
-        outgoing[1], listing = barrier((outgoing[1], listing))
+        outgoing[0], listing = barrier((outgoing[0], listing))
         pieces = crossed(outgoing, "dir")
         slab, leaving = pick(pieces, listing, where, place, partners, per_tile)
         leaving, tile_index = barrier((leaving, near_tile))

time: 52.1 us -> 51.1 us (0.981)
  local copies, waits for them, and re-layouts: 8.78 us -> 8.11 us
    unnamed x18, local copies, waits for them, and re-layouts: 8.78 us -> 8.11 us
  transfers between devices with their start and end apart: 17 -> 17, of which waited for: 10 -> 12; matrix products, arithmetic and copies ran while one was open for 0% -> 0% of each run, Pallas kernels for 17% -> 18%
where the time goes in v5:
time: 51.1 us; the launch traced here: 50.8 us
  starting transfers between devices  16.7 us (33%)
  waiting for transfers between devices  13.8 us (27%)
  Pallas kernels  12 us (23%)
  local copies, waits for them, and re-layouts  8.11 us (16%)
    ppermute x17, starting transfers between devices, crossed(): lax.ppermute(pieces[step], axis, [(i, i ^ step) for i in range(count)])  16.7 us
    ppermute x17, waiting for transfers between devices, crossed(): lax.ppermute(pieces[step], axis, [(i, i ^ step) for i in range(count)])  13.8 us
    unnamed x18, local copies, waits for them, and re-layouts  8.11 us
    pallas_call x1, Pallas kernels, build(): pl.pallas_call(kernel, grid=(dirs,), out_shape=[jax.ShapeDtypeStruct((dir...  5.83 us
    pallas_call x1, Pallas kernels, far_first(): pl.pallas_call(kernel, grid=(dirs // group,), out_shape=jax.ShapeDtypeStr...  1.55 us
    pallas_call x1, Pallas kernels, near_product(): pl.pallas_call(kernel, grid=(dirs // group,), out_shape=jax.ShapeDtypeStr...  1.53 us
    pallas_call x1, Pallas kernels, disaggregate(): pl.pallas_call(kernel, out_shape=jax.ShapeDtypeStruct((boxes, unknowns, c...  1.36 us
  transfers between devices with their start and end apart: 17, of which 12 were waited for; matrix products, arithmetic and copies ran while one was open for 0% of the time, Pallas kernels for 18%

profile of v5, /device:TPU:16, one launch (start us, length us, event | category | flops | bytes accessed | tf_op | source)
XLA Modules:
  0.0 50.8 jit_solution(498761221997036223)
XLA Ops:
  0.0 1.2 %copy-done.2 = bf16[32,128,128]{2,1,0:T(8,128)(2,1)S(1)} copy-done((bf16[32,128,128]{2,1,0:T(8,128)(2,1)S(1)}, bf16[32,128,128]{2,1,0:T(8,128)(2,1)}, u32[]{:S(2)}) %copy-start.2) | copy-done | bytes 1048600
  1.2 0.8 %copy-done.3 = bf16[64,256]{1,0:T(8,128)(2,1)S(1)} copy-done((bf16[64,256]{1,0:T(8,128)(2,1)S(1)}, bf16[64,256]{1,0:T(8,128)(2,1)}, u32[]{:S(2)}) %copy-start.3) | copy-done | bytes 32792
  2.0 0.6 %aggregate.1 = (bf16[8,32,128]{2,1,0:T(8,128)(2,1)S(1)}, bf16[8,32,128]{2,1,0:T(8,128)(2,1)S(1)}, bf16[8,32,128]{2,1,0:T(8,128)(2,1)S(1)}, bf16[8,32,128]{2,1,0:...) custom-call(s32[1]{0:T(128)} %bitcast.place_ref, ...), custom_call_target="tpu_custom_call" | custom-call | flops 1 | bytes 1 | tf_op jit(solution)/shard_map/aggregate/pallas_call | solution.py:57
  2.6 2.0 %collective-permute-start = (bf16[8,32,128]{2,1,0:T(8,128)(2,1)S(1)}, bf16[8,32,128]{2,1,0:T(8,128)(2,1)S(1)}, u32[]{:S(2)}, u32[]{:S(2)}) collective-permute-start(bf16[8,32,128]{2,1,0:T(8,128)(2,1)S(1)} %get-tuple-element.36), channel_id=1, source_target_pairs={{0,7},{1,6},{2,5},{3,4},{4,3},{5,2},{6,1},{7,0},{8,15},{9,14},{10,... | collective-permute-start | bytes 196616 | tf_op jit(solution)/shard_map/ppermute | solution.py:345
  4.5 0.6 %collective-permute-start.1 = (bf16[8,32,128]{2,1,0:T(8,128)(2,1)S(1)}, bf16[8,32,128]{2,1,0:T(8,128)(2,1)S(1)}, u32[]{:S(2)}, u32[]{:S(2)}) collective-permute-start(bf16[8,32,128]{2,1,0:T(8,128)(2,1)S(1)} %get-tuple-element.37), channel_id=1, source_target_pairs={{0,6},{1,7},{2,4},{3,5},{4,2},{5,3},{6,0},{7,1},{8,14},{9,15},{10,... | collective-permute-start | bytes 196616 | tf_op jit(solution)/shard_map/ppermute | solution.py:345
  5.2 1.3 %collective-permute-start.2 = (bf16[8,32,128]{2,1,0:T(8,128)(2,1)S(1)}, bf16[8,32,128]{2,1,0:T(8,128)(2,1)S(1)}, u32[]{:S(2)}, u32[]{:S(2)}) collective-permute-start(bf16[8,32,128]{2,1,0:T(8,128)(2,1)S(1)} %get-tuple-element.38), channel_id=1, source_target_pairs={{0,3},{1,2},{2,1},{3,0},{4,7},{5,6},{6,5},{7,4},{8,11},{9,10},{10,... | collective-permute-start | bytes 196616 | tf_op jit(solution)/shard_map/ppermute | solution.py:345
  6.5 1.3 %collective-permute-start.3 = (bf16[8,32,128]{2,1,0:T(8,128)(2,1)S(1)}, bf16[8,32,128]{2,1,0:T(8,128)(2,1)S(1)}, u32[]{:S(2)}, u32[]{:S(2)}) collective-permute-start(bf16[8,32,128]{2,1,0:T(8,128)(2,1)S(1)} %get-tuple-element.39), channel_id=1, source_target_pairs={{0,5},{1,4},{2,7},{3,6},{4,1},{5,0},{6,3},{7,2},{8,13},{9,12},{10,... | collective-permute-start | bytes 196616 | tf_op jit(solution)/shard_map/ppermute | solution.py:345
  7.8 0.5 collective-permute-start.4
  8.3 0.0 collective-permute-done.refs_0_
  8.3 1.2 %collective-permute-start.5 = (bf16[8,32,128]{2,1,0:T(8,128)(2,1)S(1)}, bf16[8,32,128]{2,1,0:T(8,128)(2,1)S(1)}, u32[]{:S(2)}, u32[]{:S(2)}) collective-permute-start(bf16[8,32,128]{2,1,0:T(8,128)(2,1)S(1)} %get-tuple-element.41), channel_id=1, source_target_pairs={{0,4},{1,5},{2,6},{3,7},{4,0},{5,1},{6,2},{7,3},{8,12},{9,13},{10,... | collective-permute-start | bytes 196616 | tf_op jit(solution)/shard_map/ppermute | solution.py:345
  9.4 1.0 %collective-permute-done.1.refs_1_ = bf16[8,32,128]{2,1,0:T(8,128)(2,1)S(1)} collective-permute-done((bf16[8,32,128]{2,1,0:T(8,128)(2,1)S(1)}, bf16[8,32,128]{2,1,0:T(8,128)(2,1)S(1)}, u32[]{:S(2)}, u32[]{:S(2)}) %collective-permute-start.1) | collective-permute-done | bytes 65568 | tf_op jit(solution)/shard_map/ppermute | solution.py:345
  10.4 0.0 collective-permute-start.6
  10.4 0.3 collective-permute-done.2.refs_2_
  10.7 0.8 %collective-permute-done.3.refs_3_ = bf16[8,32,128]{2,1,0:T(8,128)(2,1)S(1)} collective-permute-done((bf16[8,32,128]{2,1,0:T(8,128)(2,1)S(1)}, bf16[8,32,128]{2,1,0:T(8,128)(2,1)S(1)}, u32[]{:S(2)}, u32[]{:S(2)}) %collective-permute-start.3) | collective-permute-done | bytes 65568 | tf_op jit(solution)/shard_map/ppermute | solution.py:345
  11.5 0.7 %collective-permute-done.4.refs_4_ = bf16[8,32,128]{2,1,0:T(8,128)(2,1)S(1)} collective-permute-done((bf16[8,32,128]{2,1,0:T(8,128)(2,1)S(1)}, bf16[8,32,128]{2,1,0:T(8,128)(2,1)S(1)}, u32[]{:S(2)}, u32[]{:S(2)}) %collective-permute-start.4) | collective-permute-done | bytes 65568 | tf_op jit(solution)/shard_map/ppermute | solution.py:345
  12.2 0.7 %collective-permute-done.5.refs_5_ = bf16[8,32,128]{2,1,0:T(8,128)(2,1)S(1)} collective-permute-done((bf16[8,32,128]{2,1,0:T(8,128)(2,1)S(1)}, bf16[8,32,128]{2,1,0:T(8,128)(2,1)S(1)}, u32[]{:S(2)}, u32[]{:S(2)}) %collective-permute-start.5) | collective-permute-done | bytes 65568 | tf_op jit(solution)/shard_map/ppermute | solution.py:345
  12.9 0.0 collective-permute-done.6.refs_6_
  12.9 0.6 %pick.1 = (bf16[8,8,32,128]{3,2,1,0:T(8,128)(2,1)S(1)}, bf16[2,2,8,32,128]{4,3,2,1,0:T(8,128)(2,1)S(1)}, bf16[2,2,8,32,128]{4,3,2,1,0:T(8,128)(2,1)S(1)}, bf16[2,2,8,32,128]{4,3,2,1,0:T(8,128)(2,1)S(1)}) custom-call(s32[2,4]{1,0:T(2,128)S(1)} %dynamic-slice_bitcast_fusion.listing_ref, s32[1]{0:T(128)} %bitcast.1.where_ref, s32[1]{0:T(128)} %bitcast.place_ref, ...), custom_call_target="tpu_custom_call" | custom-call | flops 1 | bytes 1 | tf_op jit(solution)/shard_map/pick/pallas_call | solution.py:85
  13.6 0.4 collective-permute-start.7
  14.0 1.6 %collective-permute-start.8 = (bf16[2,2,8,32,128]{4,3,2,1,0:T(8,128)(2,1)S(1)}, bf16[2,2,8,32,128]{4,3,2,1,0:T(8,128)(2,1)S(1)}, u32[]{:S(2)}, u32[]{:S(2)}) collective-permute-start(bf16[2,2,8,32,128]{4,3,2,1,0:T(8,128)(2,1)S(1)} %get-tuple-element.53), channel_id=1, source_target_pairs={{0,8},{8,0},{16,24},{24,16},{1,9},{9,1},{17,25},{25,17},{2,10},{10... | collective-permute-start | bytes 786440 | tf_op jit(solution)/shard_map/ppermute | solution.py:345
  15.5 1.6 %collective-permute-start.9 = (bf16[2,2,8,32,128]{4,3,2,1,0:T(8,128)(2,1)S(1)}, bf16[2,2,8,32,128]{4,3,2,1,0:T(8,128)(2,1)S(1)}, u32[]{:S(2)}, u32[]{:S(2)}) collective-permute-start(bf16[2,2,8,32,128]{4,3,2,1,0:T(8,128)(2,1)S(1)} %get-tuple-element.54), channel_id=1, source_target_pairs={{0,24},{8,16},{16,8},{24,0},{1,25},{9,17},{17,9},{25,1},{2,26},{10... | collective-permute-start | bytes 786440 | tf_op jit(solution)/shard_map/ppermute | solution.py:345
  17.1 3.4 %copy-done.1 = bf16[64,8,64,128]{3,2,1,0:T(8,128)(2,1)S(1)} copy-done((bf16[64,8,64,128]{3,2,1,0:T(8,128)(2,1)S(1)}, bf16[64,8,64,128]{3,2,1,0:T(8,128)(2,1)}, u32[]{:S(2)}) %copy-start.1) | copy-done | bytes 8388632
  20.5 0.7 %copy-done.5 = s32[4,16]{1,0:T(4,128)S(1)} copy-done((s32[4,16]{1,0:T(4,128)S(1)}, s32[4,16]{1,0:T(4,128)}, u32[]{:S(2)}) %copy-start.5) | copy-done | bytes 280
  21.2 0.7 %copy-done.6 = s32[4,16]{1,0:T(4,128)S(1)} copy-done((s32[4,16]{1,0:T(4,128)S(1)}, s32[4,16]{1,0:T(4,128)}, u32[]{:S(2)}) %copy-start.6) | copy-done | bytes 280
  21.9 0.7 %copy-done.7 = s32[4,16]{1,0:T(4,128)S(1)} copy-done((s32[4,16]{1,0:T(4,128)S(1)}, s32[4,16]{1,0:T(4,128)}, u32[]{:S(2)}) %copy-start.7) | copy-done | bytes 280
  22.5 0.7 %copy-done.8 = s32[4,16]{1,0:T(4,128)S(1)} copy-done((s32[4,16]{1,0:T(4,128)S(1)}, s32[4,16]{1,0:T(4,128)}, u32[]{:S(2)}) %copy-start.8) | copy-done | bytes 280
  23.2 5.8 %build.1 = (bf16[8,4,256,128]{3,2,1,0:T(8,128)(2,1)S(1)}, bf16[8,4,256,128]{3,2,1,0:T(8,128)(2,1)S(1)}, bf16[8,2,256,128]{3,2,1,0:T(8,128)(2,1)S(1)}) custom-call(s32[1]{0:T(128)} %bitcast.1.where_ref, s32[4,16]{1,0:T(4,128)S(1)} %copy-done.5, s32[4,16]{1,0:T(4,128)S(1)} %copy-done.6, s32[4,16]{1,0:T(4,128)S(1)} %copy-done.7, s32[4,16]{1,0:T(4,128)S(1)} %copy-done.8, ...), custom_call_target="tpu_custom_call" | custom-call | flops 1 | bytes 1 | tf_op jit(solution)/shard_map/build/pallas_call | solution.py:167
  29.1 1.5 %near_product.1.before_ref = f32[8,256,128]{2,1,0:T(8,128)S(1)} custom-call(bf16[8,4,256,128]{3,2,1,0:T(8,128)(2,1)S(1)} %get-tuple-element.50.block_ref, bf16[8,8,32,128]{3,2,1,0:T(8,128)(2,1)S(1)} %get-tuple-element.51.slab_ref), custom_call_target="tpu_custom_call" | custom-call | flops 1 | bytes 1 | tf_op jit(solution)/shard_map/near_product/pallas_call | solution.py:217
  30.6 0.0 collective-permute-done.8.refs_1_
  30.6 1.5 %far_first.1.before_ref = f32[8,256,128]{2,1,0:T(8,128)S(1)} custom-call(bf16[8,4,256,128]{3,2,1,0:T(8,128)(2,1)S(1)} %get-tuple-element.49.block_ref, f32[8,256,128]{2,1,0:T(8,128)S(1)} %near_product.1.before_ref, bf16[2,2,8,32,128]{4,3,2,1,0:T(8,128)(2,1)S(1)} %collective-permute-done.7.refs_0_, bf16[2,2,8,32,128]{4,3,2,1,0:T(8,128)(2,1)S(1)} %collective-permute-done.8.refs_1_), custom_call_target="tpu_custom_call" | custom-call | flops 1 | bytes 1 | tf_op jit(solution)/shard_map/far_first/pallas_call | solution.py:255
  32.2 0.0 copy-start.4
  32.2 7.1 %collective-permute-done.9.arrived_ref = bf16[2,2,8,32,128]{4,3,2,1,0:T(8,128)(2,1)S(1)} collective-permute-done((bf16[2,2,8,32,128]{4,3,2,1,0:T(8,128)(2,1)S(1)}, bf16[2,2,8,32,128]{4,3,2,1,0:T(8,128)(2,1)S(1)}, u32[]{:S(2)}, u32[]{:S(2)}) %collective-permute-start.9) | collective-permute-done | bytes 262176 | tf_op jit(solution)/shard_map/ppermute | solution.py:345
  39.3 0.5 %far_last.1 = (bf16[8,32,128]{2,1,0:T(8,128)(2,1)S(1)}, bf16[8,32,128]{2,1,0:T(8,128)(2,1)S(1)}, bf16[8,32,128]{2,1,0:T(8,128)(2,1)S(1)}, bf16[8,32,128]{2,1,0:T...) custom-call(s32[1]{0:T(128)} %bitcast.place_ref, ...), custom_call_target="tpu_custom_call" | custom-call | flops 1 | bytes 1 | tf_op jit(solution)/shard_map/far_last/pallas_call | solution.py:288
  39.9 0.8 %collective-permute-start.10 = (bf16[8,32,128]{2,1,0:T(8,128)(2,1)S(1)}, bf16[8,32,128]{2,1,0:T(8,128)(2,1)S(1)}, u32[]{:S(2)}, u32[]{:S(2)}) collective-permute-start(bf16[8,32,128]{2,1,0:T(8,128)(2,1)S(1)} %get-tuple-element.55), channel_id=1, source_target_pairs={{0,7},{1,6},{2,5},{3,4},{4,3},{5,2},{6,1},{7,0},{8,15},{9,14},{10,... | collective-permute-start | bytes 196616 | tf_op jit(solution)/shard_map/ppermute | solution.py:345
  40.7 1.8 %collective-permute-start.11 = (bf16[8,32,128]{2,1,0:T(8,128)(2,1)S(1)}, bf16[8,32,128]{2,1,0:T(8,128)(2,1)S(1)}, u32[]{:S(2)}, u32[]{:S(2)}) collective-permute-start(bf16[8,32,128]{2,1,0:T(8,128)(2,1)S(1)} %get-tuple-element.56), channel_id=1, source_target_pairs={{0,6},{1,7},{2,4},{3,5},{4,2},{5,3},{6,0},{7,1},{8,14},{9,15},{10,... | collective-permute-start | bytes 196616 | tf_op jit(solution)/shard_map/ppermute | solution.py:345
  42.5 1.0 %collective-permute-start.12 = (bf16[8,32,128]{2,1,0:T(8,128)(2,1)S(1)}, bf16[8,32,128]{2,1,0:T(8,128)(2,1)S(1)}, u32[]{:S(2)}, u32[]{:S(2)}) collective-permute-start(bf16[8,32,128]{2,1,0:T(8,128)(2,1)S(1)} %get-tuple-element.57), channel_id=1, source_target_pairs={{0,3},{1,2},{2,1},{3,0},{4,7},{5,6},{6,5},{7,4},{8,11},{9,10},{10,... | collective-permute-start | bytes 196616 | tf_op jit(solution)/shard_map/ppermute | solution.py:345
  43.5 0.4 collective-permute-start.13
  43.9 1.1 %collective-permute-start.14 = (bf16[8,32,128]{2,1,0:T(8,128)(2,1)S(1)}, bf16[8,32,128]{2,1,0:T(8,128)(2,1)S(1)}, u32[]{:S(2)}, u32[]{:S(2)}) collective-permute-start(bf16[8,32,128]{2,1,0:T(8,128)(2,1)S(1)} %get-tuple-element.59), channel_id=1, source_target_pairs={{0,2},{1,3},{2,0},{3,1},{4,6},{5,7},{6,4},{7,5},{8,10},{9,11},{10,... | collective-permute-start | bytes 196616 | tf_op jit(solution)/shard_map/ppermute | solution.py:345
  45.0 0.1 collective-permute-done.10.refs_0_
  45.0 1.2 %collective-permute-start.15 = (bf16[8,32,128]{2,1,0:T(8,128)(2,1)S(1)}, bf16[8,32,128]{2,1,0:T(8,128)(2,1)S(1)}, u32[]{:S(2)}, u32[]{:S(2)}) collective-permute-start(bf16[8,32,128]{2,1,0:T(8,128)(2,1)S(1)} %get-tuple-element.60), channel_id=1, source_target_pairs={{0,4},{1,5},{2,6},{3,7},{4,0},{5,1},{6,2},{7,3},{8,12},{9,13},{10,... | collective-permute-start | bytes 196616 | tf_op jit(solution)/shard_map/ppermute | solution.py:345
  46.2 0.6 %collective-permute-done.11.refs_1_ = bf16[8,32,128]{2,1,0:T(8,128)(2,1)S(1)} collective-permute-done((bf16[8,32,128]{2,1,0:T(8,128)(2,1)S(1)}, bf16[8,32,128]{2,1,0:T(8,128)(2,1)S(1)}, u32[]{:S(2)}, u32[]{:S(2)}) %collective-permute-start.11) | collective-permute-done | bytes 65568 | tf_op jit(solution)/shard_map/ppermute | solution.py:345
  46.8 0.0 collective-permute-start.16
  46.8 0.3 collective-permute-done.12.refs_2_
  47.1 0.6 %collective-permute-done.13.refs_3_ = bf16[8,32,128]{2,1,0:T(8,128)(2,1)S(1)} collective-permute-done((bf16[8,32,128]{2,1,0:T(8,128)(2,1)S(1)}, bf16[8,32,128]{2,1,0:T(8,128)(2,1)S(1)}, u32[]{:S(2)}, u32[]{:S(2)}) %collective-permute-start.13) | collective-permute-done | bytes 65568 | tf_op jit(solution)/shard_map/ppermute | solution.py:345
  47.7 1.2 %collective-permute-done.14.refs_4_ = bf16[8,32,128]{2,1,0:T(8,128)(2,1)S(1)} collective-permute-done((bf16[8,32,128]{2,1,0:T(8,128)(2,1)S(1)}, bf16[8,32,128]{2,1,0:T(8,128)(2,1)S(1)}, u32[]{:S(2)}, u32[]{:S(2)}) %collective-permute-start.14) | collective-permute-done | bytes 65568 | tf_op jit(solution)/shard_map/ppermute | solution.py:345
  48.9 0.5 %collective-permute-done.15.refs_5_ = bf16[8,32,128]{2,1,0:T(8,128)(2,1)S(1)} collective-permute-done((bf16[8,32,128]{2,1,0:T(8,128)(2,1)S(1)}, bf16[8,32,128]{2,1,0:T(8,128)(2,1)S(1)}, u32[]{:S(2)}, u32[]{:S(2)}) %collective-permute-start.15) | collective-permute-done | bytes 65568 | tf_op jit(solution)/shard_map/ppermute | solution.py:345
  49.4 0.0 collective-permute-done.16.refs_6_
  49.5 1.4 %disaggregate.1 = bf16[32,128,128]{2,1,0:T(8,128)(2,1)} custom-call(s32[1]{0:T(128)} %bitcast.place_ref, bf16[128,128]{1,0:T(8,128)(2,1)S(1)} %copy-done.4, bf16[8,32,128]{2,1,0:T(8,128)(2,1)S(1)} %collective-permute-done.10.refs_0_, bf16[8,32,128]{2,1,0:T(8,128)(2,1)S(1)} %collective-permute-done.11.refs_1_, ...), custom_call_target="tpu_custom_call" | custom-call | flops 1 | bytes 1 | tf_op jit(solution)/shard_map/disaggregate/pallas_call | solution.py:327
  (12 shorter events, 0.0 us)
Async XLA Ops:
  0.0 10.4 %copy-start = (s32[4,4,2]{1,2,0:T(2,128)S(1)}, s32[4,4,2]{1,2,0:T(2,128)}, u32[]{:S(2)}) copy-start(s32[4,4,2]{1,2,0:T(2,128)} %param.17) | copy-start | bytes 388
  0.0 1.2 %copy-start.2 = (bf16[32,128,128]{2,1,0:T(8,128)(2,1)S(1)}, bf16[32,128,128]{2,1,0:T(8,128)(2,1)}, u32[]{:S(2)}) copy-start(bf16[32,128,128]{2,1,0:T(8,128)(2,1)} %fields_ref.1) | copy-start | bytes 3145732
  1.2 0.8 %copy-start.3 = (bf16[64,256]{1,0:T(8,128)(2,1)S(1)}, bf16[64,256]{1,0:T(8,128)(2,1)}, u32[]{:S(2)}) copy-start(bf16[64,256]{1,0:T(8,128)(2,1)} %agg_ref.1) | copy-start | bytes 98308
  2.6 5.7 %collective-permute-start = (bf16[8,32,128]{2,1,0:T(8,128)(2,1)S(1)}, bf16[8,32,128]{2,1,0:T(8,128)(2,1)S(1)}, u32[]{:S(2)}, u32[]{:S(2)}) collective-permute-start(bf16[8,32,128]{2,1,0:T(8,128)(2,1)S(1)} %get-tuple-element.36), channel_id=1, source_target_pairs={{0,7},{1,6},{2,5},{3,4},{4,3},{5,2},{6,1},{7,0},{8,15},{9,14},{10,... | collective-permute-start | bytes 196616 | tf_op jit(solution)/shard_map/ppermute | solution.py:345
  4.5 5.9 %collective-permute-start.1 = (bf16[8,32,128]{2,1,0:T(8,128)(2,1)S(1)}, bf16[8,32,128]{2,1,0:T(8,128)(2,1)S(1)}, u32[]{:S(2)}, u32[]{:S(2)}) collective-permute-start(bf16[8,32,128]{2,1,0:T(8,128)(2,1)S(1)} %get-tuple-element.37), channel_id=1, source_target_pairs={{0,6},{1,7},{2,4},{3,5},{4,2},{5,3},{6,0},{7,1},{8,14},{9,15},{10,... | collective-permute-start | bytes 196616 | tf_op jit(solution)/shard_map/ppermute | solution.py:345
  5.2 5.5 %collective-permute-start.2 = (bf16[8,32,128]{2,1,0:T(8,128)(2,1)S(1)}, bf16[8,32,128]{2,1,0:T(8,128)(2,1)S(1)}, u32[]{:S(2)}, u32[]{:S(2)}) collective-permute-start(bf16[8,32,128]{2,1,0:T(8,128)(2,1)S(1)} %get-tuple-element.38), channel_id=1, source_target_pairs={{0,3},{1,2},{2,1},{3,0},{4,7},{5,6},{6,5},{7,4},{8,11},{9,10},{10,... | collective-permute-start | bytes 196616 | tf_op jit(solution)/shard_map/ppermute | solution.py:345
  6.5 5.0 %collective-permute-start.3 = (bf16[8,32,128]{2,1,0:T(8,128)(2,1)S(1)}, bf16[8,32,128]{2,1,0:T(8,128)(2,1)S(1)}, u32[]{:S(2)}, u32[]{:S(2)}) collective-permute-start(bf16[8,32,128]{2,1,0:T(8,128)(2,1)S(1)} %get-tuple-element.39), channel_id=1, source_target_pairs={{0,5},{1,4},{2,7},{3,6},{4,1},{5,0},{6,3},{7,2},{8,13},{9,12},{10,... | collective-permute-start | bytes 196616 | tf_op jit(solution)/shard_map/ppermute | solution.py:345
  7.8 4.4 %collective-permute-start.4 = (bf16[8,32,128]{2,1,0:T(8,128)(2,1)S(1)}, bf16[8,32,128]{2,1,0:T(8,128)(2,1)S(1)}, u32[]{:S(2)}, u32[]{:S(2)}) collective-permute-start(bf16[8,32,128]{2,1,0:T(8,128)(2,1)S(1)} %get-tuple-element.40), channel_id=1, source_target_pairs={{0,2},{1,3},{2,0},{3,1},{4,6},{5,7},{6,4},{7,5},{8,10},{9,11},{10,... | collective-permute-start | bytes 196616 | tf_op jit(solution)/shard_map/ppermute | solution.py:345
  8.3 4.6 %collective-permute-start.5 = (bf16[8,32,128]{2,1,0:T(8,128)(2,1)S(1)}, bf16[8,32,128]{2,1,0:T(8,128)(2,1)S(1)}, u32[]{:S(2)}, u32[]{:S(2)}) collective-permute-start(bf16[8,32,128]{2,1,0:T(8,128)(2,1)S(1)} %get-tuple-element.41), channel_id=1, source_target_pairs={{0,4},{1,5},{2,6},{3,7},{4,0},{5,1},{6,2},{7,3},{8,12},{9,13},{10,... | collective-permute-start | bytes 196616 | tf_op jit(solution)/shard_map/ppermute | solution.py:345
  10.4 2.5 %collective-permute-start.6 = (bf16[8,32,128]{2,1,0:T(8,128)(2,1)S(1)}, bf16[8,32,128]{2,1,0:T(8,128)(2,1)S(1)}, u32[]{:S(2)}, u32[]{:S(2)}) collective-permute-start(bf16[8,32,128]{2,1,0:T(8,128)(2,1)S(1)} %get-tuple-element.42), channel_id=1, source_target_pairs={{0,1},{1,0},{2,3},{3,2},{4,5},{5,4},{6,7},{7,6},{8,9},{9,8},{10,11... | collective-permute-start | bytes 196616 | tf_op jit(solution)/shard_map/ppermute | solution.py:345
  13.6 17.0 %collective-permute-start.7 = (bf16[2,2,8,32,128]{4,3,2,1,0:T(8,128)(2,1)S(1)}, bf16[2,2,8,32,128]{4,3,2,1,0:T(8,128)(2,1)S(1)}, u32[]{:S(2)}, u32[]{:S(2)}) collective-permute-start(bf16[2,2,8,32,128]{4,3,2,1,0:T(8,128)(2,1)S(1)} %get-tuple-element.52), channel_id=1, source_target_pairs={{0,16},{8,24},{16,0},{24,8},{1,17},{9,25},{17,1},{25,9},{2,18},{10... | collective-permute-start | bytes 786440 | tf_op jit(solution)/shard_map/ppermute | solution.py:345
  14.0 16.7 %collective-permute-start.8 = (bf16[2,2,8,32,128]{4,3,2,1,0:T(8,128)(2,1)S(1)}, bf16[2,2,8,32,128]{4,3,2,1,0:T(8,128)(2,1)S(1)}, u32[]{:S(2)}, u32[]{:S(2)}) collective-permute-start(bf16[2,2,8,32,128]{4,3,2,1,0:T(8,128)(2,1)S(1)} %get-tuple-element.53), channel_id=1, source_target_pairs={{0,8},{8,0},{16,24},{24,16},{1,9},{9,1},{17,25},{25,17},{2,10},{10... | collective-permute-start | bytes 786440 | tf_op jit(solution)/shard_map/ppermute | solution.py:345
  15.5 23.8 %collective-permute-start.9 = (bf16[2,2,8,32,128]{4,3,2,1,0:T(8,128)(2,1)S(1)}, bf16[2,2,8,32,128]{4,3,2,1,0:T(8,128)(2,1)S(1)}, u32[]{:S(2)}, u32[]{:S(2)}) collective-permute-start(bf16[2,2,8,32,128]{4,3,2,1,0:T(8,128)(2,1)S(1)} %get-tuple-element.54), channel_id=1, source_target_pairs={{0,24},{8,16},{16,8},{24,0},{1,25},{9,17},{17,9},{25,1},{2,26},{10... | collective-permute-start | bytes 786440 | tf_op jit(solution)/shard_map/ppermute | solution.py:345
  17.1 3.4 %copy-start.1 = (bf16[64,8,64,128]{3,2,1,0:T(8,128)(2,1)S(1)}, bf16[64,8,64,128]{3,2,1,0:T(8,128)(2,1)}, u32[]{:S(2)}) copy-start(bf16[64,8,64,128]{3,2,1,0:T(8,128)(2,1)} %refs_4_.1) | copy-start | bytes 25165828
  20.5 0.7 %copy-start.5 = (s32[4,16]{1,0:T(4,128)S(1)}, s32[4,16]{1,0:T(4,128)}, u32[]{:S(2)}) copy-start(s32[4,16]{1,0:T(4,128)} %refs_0_) | copy-start | bytes 772
  21.2 0.7 %copy-start.6 = (s32[4,16]{1,0:T(4,128)S(1)}, s32[4,16]{1,0:T(4,128)}, u32[]{:S(2)}) copy-start(s32[4,16]{1,0:T(4,128)} %refs_1_.1) | copy-start | bytes 772
  21.9 0.7 %copy-start.7 = (s32[4,16]{1,0:T(4,128)S(1)}, s32[4,16]{1,0:T(4,128)}, u32[]{:S(2)}) copy-start(s32[4,16]{1,0:T(4,128)} %refs_2_.1) | copy-start | bytes 772
  22.5 0.7 %copy-start.8 = (s32[4,16]{1,0:T(4,128)S(1)}, s32[4,16]{1,0:T(4,128)}, u32[]{:S(2)}) copy-start(s32[4,16]{1,0:T(4,128)} %refs_3_.1) | copy-start | bytes 772
  32.2 17.3 %copy-start.4 = (bf16[128,128]{1,0:T(8,128)(2,1)S(1)}, bf16[128,128]{1,0:T(8,128)(2,1)}, u32[]{:S(2)}) copy-start(bf16[128,128]{1,0:T(8,128)(2,1)} %dis_ref.1) | copy-start | bytes 98308
  39.9 5.2 %collective-permute-start.10 = (bf16[8,32,128]{2,1,0:T(8,128)(2,1)S(1)}, bf16[8,32,128]{2,1,0:T(8,128)(2,1)S(1)}, u32[]{:S(2)}, u32[]{:S(2)}) collective-permute-start(bf16[8,32,128]{2,1,0:T(8,128)(2,1)S(1)} %get-tuple-element.55), channel_id=1, source_target_pairs={{0,7},{1,6},{2,5},{3,4},{4,3},{5,2},{6,1},{7,0},{8,15},{9,14},{10,... | collective-permute-start | bytes 196616 | tf_op jit(solution)/shard_map/ppermute | solution.py:345
  40.7 6.1 %collective-permute-start.11 = (bf16[8,32,128]{2,1,0:T(8,128)(2,1)S(1)}, bf16[8,32,128]{2,1,0:T(8,128)(2,1)S(1)}, u32[]{:S(2)}, u32[]{:S(2)}) collective-permute-start(bf16[8,32,128]{2,1,0:T(8,128)(2,1)S(1)} %get-tuple-element.56), channel_id=1, source_target_pairs={{0,6},{1,7},{2,4},{3,5},{4,2},{5,3},{6,0},{7,1},{8,14},{9,15},{10,... | collective-permute-start | bytes 196616 | tf_op jit(solution)/shard_map/ppermute | solution.py:345
  42.5 4.6 %collective-permute-start.12 = (bf16[8,32,128]{2,1,0:T(8,128)(2,1)S(1)}, bf16[8,32,128]{2,1,0:T(8,128)(2,1)S(1)}, u32[]{:S(2)}, u32[]{:S(2)}) collective-permute-start(bf16[8,32,128]{2,1,0:T(8,128)(2,1)S(1)} %get-tuple-element.57), channel_id=1, source_target_pairs={{0,3},{1,2},{2,1},{3,0},{4,7},{5,6},{6,5},{7,4},{8,11},{9,10},{10,... | collective-permute-start | bytes 196616 | tf_op jit(solution)/shard_map/ppermute | solution.py:345
  43.5 4.3 %collective-permute-start.13 = (bf16[8,32,128]{2,1,0:T(8,128)(2,1)S(1)}, bf16[8,32,128]{2,1,0:T(8,128)(2,1)S(1)}, u32[]{:S(2)}, u32[]{:S(2)}) collective-permute-start(bf16[8,32,128]{2,1,0:T(8,128)(2,1)S(1)} %get-tuple-element.58), channel_id=1, source_target_pairs={{0,5},{1,4},{2,7},{3,6},{4,1},{5,0},{6,3},{7,2},{8,13},{9,12},{10,... | collective-permute-start | bytes 196616 | tf_op jit(solution)/shard_map/ppermute | solution.py:345
  43.9 5.0 %collective-permute-start.14 = (bf16[8,32,128]{2,1,0:T(8,128)(2,1)S(1)}, bf16[8,32,128]{2,1,0:T(8,128)(2,1)S(1)}, u32[]{:S(2)}, u32[]{:S(2)}) collective-permute-start(bf16[8,32,128]{2,1,0:T(8,128)(2,1)S(1)} %get-tuple-element.59), channel_id=1, source_target_pairs={{0,2},{1,3},{2,0},{3,1},{4,6},{5,7},{6,4},{7,5},{8,10},{9,11},{10,... | collective-permute-start | bytes 196616 | tf_op jit(solution)/shard_map/ppermute | solution.py:345
  45.0 4.4 %collective-permute-start.15 = (bf16[8,32,128]{2,1,0:T(8,128)(2,1)S(1)}, bf16[8,32,128]{2,1,0:T(8,128)(2,1)S(1)}, u32[]{:S(2)}, u32[]{:S(2)}) collective-permute-start(bf16[8,32,128]{2,1,0:T(8,128)(2,1)S(1)} %get-tuple-element.60), channel_id=1, source_target_pairs={{0,4},{1,5},{2,6},{3,7},{4,0},{5,1},{6,2},{7,3},{8,12},{9,13},{10,... | collective-permute-start | bytes 196616 | tf_op jit(solution)/shard_map/ppermute | solution.py:345
  46.8 2.6 %collective-permute-start.16 = (bf16[8,32,128]{2,1,0:T(8,128)(2,1)S(1)}, bf16[8,32,128]{2,1,0:T(8,128)(2,1)S(1)}, u32[]{:S(2)}, u32[]{:S(2)}) collective-permute-start(bf16[8,32,128]{2,1,0:T(8,128)(2,1)S(1)} %get-tuple-element.61), channel_id=1, source_target_pairs={{0,1},{1,0},{2,3},{3,2},{4,5},{5,4},{6,7},{7,6},{8,9},{9,8},{10,11... | collective-permute-start | bytes 196616 | tf_op jit(solution)/shard_map/ppermute | solution.py:345

commit v6 on v5

--- a/solution.py
+++ b/solution.py
@@ -59,7 +59,7 @@
         out_shape=[jax.ShapeDtypeStruct((part, boxes, columns), jnp.bfloat16)] * devices,
         in_specs=smem(1) + vmem(2),
         out_specs=vmem(devices),
-        scratch_shapes=[pltpu.VMEM((boxes * (all_dirs + 1), columns), jnp.float32)],
+        scratch_shapes=[pltpu.VMEM(((boxes + 1) * (all_dirs + 1), columns), jnp.float32)],
         compiler_params=pltpu.CompilerParams(vmem_limit_bytes=AGG_MIB * MIB),
         cost_estimate=LITTLE,
         name="aggregate",
@@ -330,7 +330,7 @@
         in_specs=smem(1) + vmem(1 + devices),
         out_specs=pl.BlockSpec(memory_space=pl.ANY),
         scratch_shapes=[
-            pltpu.VMEM((all_dirs * (boxes + 1), columns), jnp.float32),
+            pltpu.VMEM(((all_dirs + 1) * (boxes + 1), columns), jnp.float32),
             pltpu.VMEM((boxes, unknowns, columns), jnp.bfloat16),
             pltpu.SemaphoreType.DMA((cuts,)),
         ],

time: 51.1 us -> 51.1 us (level)
  no operation moved by 1% of the time
where the time goes in v6:
time: 51.1 us; the launch traced here: 50.8 us
  starting transfers between devices  16.7 us (33%)
  waiting for transfers between devices  13.8 us (27%)
  Pallas kernels  12 us (23%)
  local copies, waits for them, and re-layouts  8.11 us (16%)
    ppermute x17, starting transfers between devices, crossed(): lax.ppermute(pieces[step], axis, [(i, i ^ step) for i in range(count)])  16.7 us
    ppermute x17, waiting for transfers between devices, crossed(): lax.ppermute(pieces[step], axis, [(i, i ^ step) for i in range(count)])  13.8 us
    unnamed x18, local copies, waits for them, and re-layouts  8.11 us
    pallas_call x1, Pallas kernels, build(): pl.pallas_call(kernel, grid=(dirs,), out_shape=[jax.ShapeDtypeStruct((dir...  5.83 us
    pallas_call x1, Pallas kernels, far_first(): pl.pallas_call(kernel, grid=(dirs // group,), out_shape=jax.ShapeDtypeStr...  1.55 us
    pallas_call x1, Pallas kernels, near_product(): pl.pallas_call(kernel, grid=(dirs // group,), out_shape=jax.ShapeDtypeStr...  1.53 us
    pallas_call x1, Pallas kernels, disaggregate(): pl.pallas_call(kernel, out_shape=jax.ShapeDtypeStruct((boxes, unknowns, c...  1.37 us
  transfers between devices with their start and end apart: 17, of which 12 were waited for; matrix products, arithmetic and copies ran while one was open for 0% of the time, Pallas kernels for 18%

profile of v6, /device:TPU:16, one launch (start us, length us, event | category | flops | bytes accessed | tf_op | source)
XLA Modules:
  0.0 50.8 jit_solution(5603906408618958768)
XLA Ops:
  0.0 1.2 %copy-done.2 = bf16[32,128,128]{2,1,0:T(8,128)(2,1)S(1)} copy-done((bf16[32,128,128]{2,1,0:T(8,128)(2,1)S(1)}, bf16[32,128,128]{2,1,0:T(8,128)(2,1)}, u32[]{:S(2)}) %copy-start.2) | copy-done | bytes 1048600
  1.2 0.8 %copy-done.3 = bf16[64,256]{1,0:T(8,128)(2,1)S(1)} copy-done((bf16[64,256]{1,0:T(8,128)(2,1)S(1)}, bf16[64,256]{1,0:T(8,128)(2,1)}, u32[]{:S(2)}) %copy-start.3) | copy-done | bytes 32792
  2.0 0.6 %aggregate.1 = (bf16[8,32,128]{2,1,0:T(8,128)(2,1)S(1)}, bf16[8,32,128]{2,1,0:T(8,128)(2,1)S(1)}, bf16[8,32,128]{2,1,0:T(8,128)(2,1)S(1)}, bf16[8,32,128]{2,1,0:...) custom-call(s32[1]{0:T(128)} %bitcast.place_ref, ...), custom_call_target="tpu_custom_call" | custom-call | flops 1 | bytes 1 | tf_op jit(solution)/shard_map/aggregate/pallas_call | solution.py:57
  2.6 2.0 %collective-permute-start = (bf16[8,32,128]{2,1,0:T(8,128)(2,1)S(1)}, bf16[8,32,128]{2,1,0:T(8,128)(2,1)S(1)}, u32[]{:S(2)}, u32[]{:S(2)}) collective-permute-start(bf16[8,32,128]{2,1,0:T(8,128)(2,1)S(1)} %get-tuple-element.36), channel_id=1, source_target_pairs={{0,7},{1,6},{2,5},{3,4},{4,3},{5,2},{6,1},{7,0},{8,15},{9,14},{10,... | collective-permute-start | bytes 196616 | tf_op jit(solution)/shard_map/ppermute | solution.py:345
  4.5 0.6 %collective-permute-start.1 = (bf16[8,32,128]{2,1,0:T(8,128)(2,1)S(1)}, bf16[8,32,128]{2,1,0:T(8,128)(2,1)S(1)}, u32[]{:S(2)}, u32[]{:S(2)}) collective-permute-start(bf16[8,32,128]{2,1,0:T(8,128)(2,1)S(1)} %get-tuple-element.37), channel_id=1, source_target_pairs={{0,6},{1,7},{2,4},{3,5},{4,2},{5,3},{6,0},{7,1},{8,14},{9,15},{10,... | collective-permute-start | bytes 196616 | tf_op jit(solution)/shard_map/ppermute | solution.py:345
  5.2 1.3 %collective-permute-start.2 = (bf16[8,32,128]{2,1,0:T(8,128)(2,1)S(1)}, bf16[8,32,128]{2,1,0:T(8,128)(2,1)S(1)}, u32[]{:S(2)}, u32[]{:S(2)}) collective-permute-start(bf16[8,32,128]{2,1,0:T(8,128)(2,1)S(1)} %get-tuple-element.38), channel_id=1, source_target_pairs={{0,3},{1,2},{2,1},{3,0},{4,7},{5,6},{6,5},{7,4},{8,11},{9,10},{10,... | collective-permute-start | bytes 196616 | tf_op jit(solution)/shard_map/ppermute | solution.py:345
  6.5 1.3 %collective-permute-start.3 = (bf16[8,32,128]{2,1,0:T(8,128)(2,1)S(1)}, bf16[8,32,128]{2,1,0:T(8,128)(2,1)S(1)}, u32[]{:S(2)}, u32[]{:S(2)}) collective-permute-start(bf16[8,32,128]{2,1,0:T(8,128)(2,1)S(1)} %get-tuple-element.39), channel_id=1, source_target_pairs={{0,5},{1,4},{2,7},{3,6},{4,1},{5,0},{6,3},{7,2},{8,13},{9,12},{10,... | collective-permute-start | bytes 196616 | tf_op jit(solution)/shard_map/ppermute | solution.py:345
  7.8 0.5 collective-permute-start.4
  8.3 0.0 collective-permute-done.refs_0_
  8.3 1.2 %collective-permute-start.5 = (bf16[8,32,128]{2,1,0:T(8,128)(2,1)S(1)}, bf16[8,32,128]{2,1,0:T(8,128)(2,1)S(1)}, u32[]{:S(2)}, u32[]{:S(2)}) collective-permute-start(bf16[8,32,128]{2,1,0:T(8,128)(2,1)S(1)} %get-tuple-element.41), channel_id=1, source_target_pairs={{0,4},{1,5},{2,6},{3,7},{4,0},{5,1},{6,2},{7,3},{8,12},{9,13},{10,... | collective-permute-start | bytes 196616 | tf_op jit(solution)/shard_map/ppermute | solution.py:345
  9.4 1.0 %collective-permute-done.1.refs_1_ = bf16[8,32,128]{2,1,0:T(8,128)(2,1)S(1)} collective-permute-done((bf16[8,32,128]{2,1,0:T(8,128)(2,1)S(1)}, bf16[8,32,128]{2,1,0:T(8,128)(2,1)S(1)}, u32[]{:S(2)}, u32[]{:S(2)}) %collective-permute-start.1) | collective-permute-done | bytes 65568 | tf_op jit(solution)/shard_map/ppermute | solution.py:345
  10.4 0.0 collective-permute-start.6
  10.4 0.3 collective-permute-done.2.refs_2_
  10.7 0.8 %collective-permute-done.3.refs_3_ = bf16[8,32,128]{2,1,0:T(8,128)(2,1)S(1)} collective-permute-done((bf16[8,32,128]{2,1,0:T(8,128)(2,1)S(1)}, bf16[8,32,128]{2,1,0:T(8,128)(2,1)S(1)}, u32[]{:S(2)}, u32[]{:S(2)}) %collective-permute-start.3) | collective-permute-done | bytes 65568 | tf_op jit(solution)/shard_map/ppermute | solution.py:345
  11.5 0.7 %collective-permute-done.4.refs_4_ = bf16[8,32,128]{2,1,0:T(8,128)(2,1)S(1)} collective-permute-done((bf16[8,32,128]{2,1,0:T(8,128)(2,1)S(1)}, bf16[8,32,128]{2,1,0:T(8,128)(2,1)S(1)}, u32[]{:S(2)}, u32[]{:S(2)}) %collective-permute-start.4) | collective-permute-done | bytes 65568 | tf_op jit(solution)/shard_map/ppermute | solution.py:345
  12.2 0.7 %collective-permute-done.5.refs_5_ = bf16[8,32,128]{2,1,0:T(8,128)(2,1)S(1)} collective-permute-done((bf16[8,32,128]{2,1,0:T(8,128)(2,1)S(1)}, bf16[8,32,128]{2,1,0:T(8,128)(2,1)S(1)}, u32[]{:S(2)}, u32[]{:S(2)}) %collective-permute-start.5) | collective-permute-done | bytes 65568 | tf_op jit(solution)/shard_map/ppermute | solution.py:345
  12.9 0.0 collective-permute-done.6.refs_6_
  12.9 0.6 %pick.1 = (bf16[8,8,32,128]{3,2,1,0:T(8,128)(2,1)S(1)}, bf16[2,2,8,32,128]{4,3,2,1,0:T(8,128)(2,1)S(1)}, bf16[2,2,8,32,128]{4,3,2,1,0:T(8,128)(2,1)S(1)}, bf16[2,2,8,32,128]{4,3,2,1,0:T(8,128)(2,1)S(1)}) custom-call(s32[2,4]{1,0:T(2,128)S(1)} %dynamic-slice_bitcast_fusion.listing_ref, s32[1]{0:T(128)} %bitcast.1.where_ref, s32[1]{0:T(128)} %bitcast.place_ref, ...), custom_call_target="tpu_custom_call" | custom-call | flops 1 | bytes 1 | tf_op jit(solution)/shard_map/pick/pallas_call | solution.py:85
  13.6 0.4 collective-permute-start.7
  14.0 1.6 %collective-permute-start.8 = (bf16[2,2,8,32,128]{4,3,2,1,0:T(8,128)(2,1)S(1)}, bf16[2,2,8,32,128]{4,3,2,1,0:T(8,128)(2,1)S(1)}, u32[]{:S(2)}, u32[]{:S(2)}) collective-permute-start(bf16[2,2,8,32,128]{4,3,2,1,0:T(8,128)(2,1)S(1)} %get-tuple-element.53), channel_id=1, source_target_pairs={{0,8},{8,0},{16,24},{24,16},{1,9},{9,1},{17,25},{25,17},{2,10},{10... | collective-permute-start | bytes 786440 | tf_op jit(solution)/shard_map/ppermute | solution.py:345
  15.5 1.6 %collective-permute-start.9 = (bf16[2,2,8,32,128]{4,3,2,1,0:T(8,128)(2,1)S(1)}, bf16[2,2,8,32,128]{4,3,2,1,0:T(8,128)(2,1)S(1)}, u32[]{:S(2)}, u32[]{:S(2)}) collective-permute-start(bf16[2,2,8,32,128]{4,3,2,1,0:T(8,128)(2,1)S(1)} %get-tuple-element.54), channel_id=1, source_target_pairs={{0,24},{8,16},{16,8},{24,0},{1,25},{9,17},{17,9},{25,1},{2,26},{10... | collective-permute-start | bytes 786440 | tf_op jit(solution)/shard_map/ppermute | solution.py:345
  17.1 3.4 %copy-done.1 = bf16[64,8,64,128]{3,2,1,0:T(8,128)(2,1)S(1)} copy-done((bf16[64,8,64,128]{3,2,1,0:T(8,128)(2,1)S(1)}, bf16[64,8,64,128]{3,2,1,0:T(8,128)(2,1)}, u32[]{:S(2)}) %copy-start.1) | copy-done | bytes 8388632
  20.5 0.7 %copy-done.5 = s32[4,16]{1,0:T(4,128)S(1)} copy-done((s32[4,16]{1,0:T(4,128)S(1)}, s32[4,16]{1,0:T(4,128)}, u32[]{:S(2)}) %copy-start.5) | copy-done | bytes 280
  21.2 0.7 %copy-done.6 = s32[4,16]{1,0:T(4,128)S(1)} copy-done((s32[4,16]{1,0:T(4,128)S(1)}, s32[4,16]{1,0:T(4,128)}, u32[]{:S(2)}) %copy-start.6) | copy-done | bytes 280
  21.9 0.7 %copy-done.7 = s32[4,16]{1,0:T(4,128)S(1)} copy-done((s32[4,16]{1,0:T(4,128)S(1)}, s32[4,16]{1,0:T(4,128)}, u32[]{:S(2)}) %copy-start.7) | copy-done | bytes 280
  22.5 0.7 %copy-done.8 = s32[4,16]{1,0:T(4,128)S(1)} copy-done((s32[4,16]{1,0:T(4,128)S(1)}, s32[4,16]{1,0:T(4,128)}, u32[]{:S(2)}) %copy-start.8) | copy-done | bytes 280
  23.2 5.8 %build.1 = (bf16[8,4,256,128]{3,2,1,0:T(8,128)(2,1)S(1)}, bf16[8,4,256,128]{3,2,1,0:T(8,128)(2,1)S(1)}, bf16[8,2,256,128]{3,2,1,0:T(8,128)(2,1)S(1)}) custom-call(s32[1]{0:T(128)} %bitcast.1.where_ref, s32[4,16]{1,0:T(4,128)S(1)} %copy-done.5, s32[4,16]{1,0:T(4,128)S(1)} %copy-done.6, s32[4,16]{1,0:T(4,128)S(1)} %copy-done.7, s32[4,16]{1,0:T(4,128)S(1)} %copy-done.8, ...), custom_call_target="tpu_custom_call" | custom-call | flops 1 | bytes 1 | tf_op jit(solution)/shard_map/build/pallas_call | solution.py:167
  29.1 1.5 %near_product.1.before_ref = f32[8,256,128]{2,1,0:T(8,128)S(1)} custom-call(bf16[8,4,256,128]{3,2,1,0:T(8,128)(2,1)S(1)} %get-tuple-element.50.block_ref, bf16[8,8,32,128]{3,2,1,0:T(8,128)(2,1)S(1)} %get-tuple-element.51.slab_ref), custom_call_target="tpu_custom_call" | custom-call | flops 1 | bytes 1 | tf_op jit(solution)/shard_map/near_product/pallas_call | solution.py:217
  30.6 0.0 collective-permute-done.7.refs_0_
  30.6 0.0 collective-permute-done.8.refs_1_
  30.6 1.5 %far_first.1.before_ref = f32[8,256,128]{2,1,0:T(8,128)S(1)} custom-call(bf16[8,4,256,128]{3,2,1,0:T(8,128)(2,1)S(1)} %get-tuple-element.49.block_ref, f32[8,256,128]{2,1,0:T(8,128)S(1)} %near_product.1.before_ref, bf16[2,2,8,32,128]{4,3,2,1,0:T(8,128)(2,1)S(1)} %collective-permute-done.7.refs_0_, bf16[2,2,8,32,128]{4,3,2,1,0:T(8,128)(2,1)S(1)} %collective-permute-done.8.refs_1_), custom_call_target="tpu_custom_call" | custom-call | flops 1 | bytes 1 | tf_op jit(solution)/shard_map/far_first/pallas_call | solution.py:255
  32.2 0.0 copy-start.4
  32.2 7.1 %collective-permute-done.9.arrived_ref = bf16[2,2,8,32,128]{4,3,2,1,0:T(8,128)(2,1)S(1)} collective-permute-done((bf16[2,2,8,32,128]{4,3,2,1,0:T(8,128)(2,1)S(1)}, bf16[2,2,8,32,128]{4,3,2,1,0:T(8,128)(2,1)S(1)}, u32[]{:S(2)}, u32[]{:S(2)}) %collective-permute-start.9) | collective-permute-done | bytes 262176 | tf_op jit(solution)/shard_map/ppermute | solution.py:345
  39.3 0.5 %far_last.1 = (bf16[8,32,128]{2,1,0:T(8,128)(2,1)S(1)}, bf16[8,32,128]{2,1,0:T(8,128)(2,1)S(1)}, bf16[8,32,128]{2,1,0:T(8,128)(2,1)S(1)}, bf16[8,32,128]{2,1,0:T...) custom-call(s32[1]{0:T(128)} %bitcast.place_ref, ...), custom_call_target="tpu_custom_call" | custom-call | flops 1 | bytes 1 | tf_op jit(solution)/shard_map/far_last/pallas_call | solution.py:288
  39.9 0.8 %collective-permute-start.10 = (bf16[8,32,128]{2,1,0:T(8,128)(2,1)S(1)}, bf16[8,32,128]{2,1,0:T(8,128)(2,1)S(1)}, u32[]{:S(2)}, u32[]{:S(2)}) collective-permute-start(bf16[8,32,128]{2,1,0:T(8,128)(2,1)S(1)} %get-tuple-element.55), channel_id=1, source_target_pairs={{0,7},{1,6},{2,5},{3,4},{4,3},{5,2},{6,1},{7,0},{8,15},{9,14},{10,... | collective-permute-start | bytes 196616 | tf_op jit(solution)/shard_map/ppermute | solution.py:345
  40.7 1.8 %collective-permute-start.11 = (bf16[8,32,128]{2,1,0:T(8,128)(2,1)S(1)}, bf16[8,32,128]{2,1,0:T(8,128)(2,1)S(1)}, u32[]{:S(2)}, u32[]{:S(2)}) collective-permute-start(bf16[8,32,128]{2,1,0:T(8,128)(2,1)S(1)} %get-tuple-element.56), channel_id=1, source_target_pairs={{0,6},{1,7},{2,4},{3,5},{4,2},{5,3},{6,0},{7,1},{8,14},{9,15},{10,... | collective-permute-start | bytes 196616 | tf_op jit(solution)/shard_map/ppermute | solution.py:345
  42.5 1.0 %collective-permute-start.12 = (bf16[8,32,128]{2,1,0:T(8,128)(2,1)S(1)}, bf16[8,32,128]{2,1,0:T(8,128)(2,1)S(1)}, u32[]{:S(2)}, u32[]{:S(2)}) collective-permute-start(bf16[8,32,128]{2,1,0:T(8,128)(2,1)S(1)} %get-tuple-element.57), channel_id=1, source_target_pairs={{0,3},{1,2},{2,1},{3,0},{4,7},{5,6},{6,5},{7,4},{8,11},{9,10},{10,... | collective-permute-start | bytes 196616 | tf_op jit(solution)/shard_map/ppermute | solution.py:345
  43.5 0.4 collective-permute-start.13
  43.9 1.1 %collective-permute-start.14 = (bf16[8,32,128]{2,1,0:T(8,128)(2,1)S(1)}, bf16[8,32,128]{2,1,0:T(8,128)(2,1)S(1)}, u32[]{:S(2)}, u32[]{:S(2)}) collective-permute-start(bf16[8,32,128]{2,1,0:T(8,128)(2,1)S(1)} %get-tuple-element.59), channel_id=1, source_target_pairs={{0,2},{1,3},{2,0},{3,1},{4,6},{5,7},{6,4},{7,5},{8,10},{9,11},{10,... | collective-permute-start | bytes 196616 | tf_op jit(solution)/shard_map/ppermute | solution.py:345
  45.0 0.1 collective-permute-done.10.refs_0_
  45.0 1.2 %collective-permute-start.15 = (bf16[8,32,128]{2,1,0:T(8,128)(2,1)S(1)}, bf16[8,32,128]{2,1,0:T(8,128)(2,1)S(1)}, u32[]{:S(2)}, u32[]{:S(2)}) collective-permute-start(bf16[8,32,128]{2,1,0:T(8,128)(2,1)S(1)} %get-tuple-element.60), channel_id=1, source_target_pairs={{0,4},{1,5},{2,6},{3,7},{4,0},{5,1},{6,2},{7,3},{8,12},{9,13},{10,... | collective-permute-start | bytes 196616 | tf_op jit(solution)/shard_map/ppermute | solution.py:345
  46.2 0.6 %collective-permute-done.11.refs_1_ = bf16[8,32,128]{2,1,0:T(8,128)(2,1)S(1)} collective-permute-done((bf16[8,32,128]{2,1,0:T(8,128)(2,1)S(1)}, bf16[8,32,128]{2,1,0:T(8,128)(2,1)S(1)}, u32[]{:S(2)}, u32[]{:S(2)}) %collective-permute-start.11) | collective-permute-done | bytes 65568 | tf_op jit(solution)/shard_map/ppermute | solution.py:345
  46.8 0.0 collective-permute-start.16
  46.8 0.3 collective-permute-done.12.refs_2_
  47.1 0.6 %collective-permute-done.13.refs_3_ = bf16[8,32,128]{2,1,0:T(8,128)(2,1)S(1)} collective-permute-done((bf16[8,32,128]{2,1,0:T(8,128)(2,1)S(1)}, bf16[8,32,128]{2,1,0:T(8,128)(2,1)S(1)}, u32[]{:S(2)}, u32[]{:S(2)}) %collective-permute-start.13) | collective-permute-done | bytes 65568 | tf_op jit(solution)/shard_map/ppermute | solution.py:345
  47.7 1.2 %collective-permute-done.14.refs_4_ = bf16[8,32,128]{2,1,0:T(8,128)(2,1)S(1)} collective-permute-done((bf16[8,32,128]{2,1,0:T(8,128)(2,1)S(1)}, bf16[8,32,128]{2,1,0:T(8,128)(2,1)S(1)}, u32[]{:S(2)}, u32[]{:S(2)}) %collective-permute-start.14) | collective-permute-done | bytes 65568 | tf_op jit(solution)/shard_map/ppermute | solution.py:345
  48.9 0.5 %collective-permute-done.15.refs_5_ = bf16[8,32,128]{2,1,0:T(8,128)(2,1)S(1)} collective-permute-done((bf16[8,32,128]{2,1,0:T(8,128)(2,1)S(1)}, bf16[8,32,128]{2,1,0:T(8,128)(2,1)S(1)}, u32[]{:S(2)}, u32[]{:S(2)}) %collective-permute-start.15) | collective-permute-done | bytes 65568 | tf_op jit(solution)/shard_map/ppermute | solution.py:345
  49.4 1.4 %disaggregate.1 = bf16[32,128,128]{2,1,0:T(8,128)(2,1)} custom-call(s32[1]{0:T(128)} %bitcast.place_ref, bf16[128,128]{1,0:T(8,128)(2,1)S(1)} %copy-done.4, bf16[8,32,128]{2,1,0:T(8,128)(2,1)S(1)} %collective-permute-done.10.refs_0_, bf16[8,32,128]{2,1,0:T(8,128)(2,1)S(1)} %collective-permute-done.11.refs_1_, ...), custom_call_target="tpu_custom_call" | custom-call | flops 1 | bytes 1 | tf_op jit(solution)/shard_map/disaggregate/pallas_call | solution.py:327
  (12 shorter events, 0.0 us)
Async XLA Ops:
  0.0 10.4 %copy-start = (s32[4,4,2]{1,2,0:T(2,128)S(1)}, s32[4,4,2]{1,2,0:T(2,128)}, u32[]{:S(2)}) copy-start(s32[4,4,2]{1,2,0:T(2,128)} %param.17) | copy-start | bytes 388
  0.0 1.2 %copy-start.2 = (bf16[32,128,128]{2,1,0:T(8,128)(2,1)S(1)}, bf16[32,128,128]{2,1,0:T(8,128)(2,1)}, u32[]{:S(2)}) copy-start(bf16[32,128,128]{2,1,0:T(8,128)(2,1)} %fields_ref.1) | copy-start | bytes 3145732
  1.2 0.8 %copy-start.3 = (bf16[64,256]{1,0:T(8,128)(2,1)S(1)}, bf16[64,256]{1,0:T(8,128)(2,1)}, u32[]{:S(2)}) copy-start(bf16[64,256]{1,0:T(8,128)(2,1)} %agg_ref.1) | copy-start | bytes 98308
  2.6 5.7 %collective-permute-start = (bf16[8,32,128]{2,1,0:T(8,128)(2,1)S(1)}, bf16[8,32,128]{2,1,0:T(8,128)(2,1)S(1)}, u32[]{:S(2)}, u32[]{:S(2)}) collective-permute-start(bf16[8,32,128]{2,1,0:T(8,128)(2,1)S(1)} %get-tuple-element.36), channel_id=1, source_target_pairs={{0,7},{1,6},{2,5},{3,4},{4,3},{5,2},{6,1},{7,0},{8,15},{9,14},{10,... | collective-permute-start | bytes 196616 | tf_op jit(solution)/shard_map/ppermute | solution.py:345
  4.5 5.9 %collective-permute-start.1 = (bf16[8,32,128]{2,1,0:T(8,128)(2,1)S(1)}, bf16[8,32,128]{2,1,0:T(8,128)(2,1)S(1)}, u32[]{:S(2)}, u32[]{:S(2)}) collective-permute-start(bf16[8,32,128]{2,1,0:T(8,128)(2,1)S(1)} %get-tuple-element.37), channel_id=1, source_target_pairs={{0,6},{1,7},{2,4},{3,5},{4,2},{5,3},{6,0},{7,1},{8,14},{9,15},{10,... | collective-permute-start | bytes 196616 | tf_op jit(solution)/shard_map/ppermute | solution.py:345
  5.2 5.5 %collective-permute-start.2 = (bf16[8,32,128]{2,1,0:T(8,128)(2,1)S(1)}, bf16[8,32,128]{2,1,0:T(8,128)(2,1)S(1)}, u32[]{:S(2)}, u32[]{:S(2)}) collective-permute-start(bf16[8,32,128]{2,1,0:T(8,128)(2,1)S(1)} %get-tuple-element.38), channel_id=1, source_target_pairs={{0,3},{1,2},{2,1},{3,0},{4,7},{5,6},{6,5},{7,4},{8,11},{9,10},{10,... | collective-permute-start | bytes 196616 | tf_op jit(solution)/shard_map/ppermute | solution.py:345
  6.5 5.0 %collective-permute-start.3 = (bf16[8,32,128]{2,1,0:T(8,128)(2,1)S(1)}, bf16[8,32,128]{2,1,0:T(8,128)(2,1)S(1)}, u32[]{:S(2)}, u32[]{:S(2)}) collective-permute-start(bf16[8,32,128]{2,1,0:T(8,128)(2,1)S(1)} %get-tuple-element.39), channel_id=1, source_target_pairs={{0,5},{1,4},{2,7},{3,6},{4,1},{5,0},{6,3},{7,2},{8,13},{9,12},{10,... | collective-permute-start | bytes 196616 | tf_op jit(solution)/shard_map/ppermute | solution.py:345
  7.8 4.4 %collective-permute-start.4 = (bf16[8,32,128]{2,1,0:T(8,128)(2,1)S(1)}, bf16[8,32,128]{2,1,0:T(8,128)(2,1)S(1)}, u32[]{:S(2)}, u32[]{:S(2)}) collective-permute-start(bf16[8,32,128]{2,1,0:T(8,128)(2,1)S(1)} %get-tuple-element.40), channel_id=1, source_target_pairs={{0,2},{1,3},{2,0},{3,1},{4,6},{5,7},{6,4},{7,5},{8,10},{9,11},{10,... | collective-permute-start | bytes 196616 | tf_op jit(solution)/shard_map/ppermute | solution.py:345
  8.3 4.6 %collective-permute-start.5 = (bf16[8,32,128]{2,1,0:T(8,128)(2,1)S(1)}, bf16[8,32,128]{2,1,0:T(8,128)(2,1)S(1)}, u32[]{:S(2)}, u32[]{:S(2)}) collective-permute-start(bf16[8,32,128]{2,1,0:T(8,128)(2,1)S(1)} %get-tuple-element.41), channel_id=1, source_target_pairs={{0,4},{1,5},{2,6},{3,7},{4,0},{5,1},{6,2},{7,3},{8,12},{9,13},{10,... | collective-permute-start | bytes 196616 | tf_op jit(solution)/shard_map/ppermute | solution.py:345
  10.4 2.5 %collective-permute-start.6 = (bf16[8,32,128]{2,1,0:T(8,128)(2,1)S(1)}, bf16[8,32,128]{2,1,0:T(8,128)(2,1)S(1)}, u32[]{:S(2)}, u32[]{:S(2)}) collective-permute-start(bf16[8,32,128]{2,1,0:T(8,128)(2,1)S(1)} %get-tuple-element.42), channel_id=1, source_target_pairs={{0,1},{1,0},{2,3},{3,2},{4,5},{5,4},{6,7},{7,6},{8,9},{9,8},{10,11... | collective-permute-start | bytes 196616 | tf_op jit(solution)/shard_map/ppermute | solution.py:345
  13.6 17.0 %collective-permute-start.7 = (bf16[2,2,8,32,128]{4,3,2,1,0:T(8,128)(2,1)S(1)}, bf16[2,2,8,32,128]{4,3,2,1,0:T(8,128)(2,1)S(1)}, u32[]{:S(2)}, u32[]{:S(2)}) collective-permute-start(bf16[2,2,8,32,128]{4,3,2,1,0:T(8,128)(2,1)S(1)} %get-tuple-element.52), channel_id=1, source_target_pairs={{0,16},{8,24},{16,0},{24,8},{1,17},{9,25},{17,1},{25,9},{2,18},{10... | collective-permute-start | bytes 786440 | tf_op jit(solution)/shard_map/ppermute | solution.py:345
  14.0 16.7 %collective-permute-start.8 = (bf16[2,2,8,32,128]{4,3,2,1,0:T(8,128)(2,1)S(1)}, bf16[2,2,8,32,128]{4,3,2,1,0:T(8,128)(2,1)S(1)}, u32[]{:S(2)}, u32[]{:S(2)}) collective-permute-start(bf16[2,2,8,32,128]{4,3,2,1,0:T(8,128)(2,1)S(1)} %get-tuple-element.53), channel_id=1, source_target_pairs={{0,8},{8,0},{16,24},{24,16},{1,9},{9,1},{17,25},{25,17},{2,10},{10... | collective-permute-start | bytes 786440 | tf_op jit(solution)/shard_map/ppermute | solution.py:345
  15.5 23.8 %collective-permute-start.9 = (bf16[2,2,8,32,128]{4,3,2,1,0:T(8,128)(2,1)S(1)}, bf16[2,2,8,32,128]{4,3,2,1,0:T(8,128)(2,1)S(1)}, u32[]{:S(2)}, u32[]{:S(2)}) collective-permute-start(bf16[2,2,8,32,128]{4,3,2,1,0:T(8,128)(2,1)S(1)} %get-tuple-element.54), channel_id=1, source_target_pairs={{0,24},{8,16},{16,8},{24,0},{1,25},{9,17},{17,9},{25,1},{2,26},{10... | collective-permute-start | bytes 786440 | tf_op jit(solution)/shard_map/ppermute | solution.py:345
  17.1 3.4 %copy-start.1 = (bf16[64,8,64,128]{3,2,1,0:T(8,128)(2,1)S(1)}, bf16[64,8,64,128]{3,2,1,0:T(8,128)(2,1)}, u32[]{:S(2)}) copy-start(bf16[64,8,64,128]{3,2,1,0:T(8,128)(2,1)} %refs_4_.1) | copy-start | bytes 25165828
  20.5 0.7 %copy-start.5 = (s32[4,16]{1,0:T(4,128)S(1)}, s32[4,16]{1,0:T(4,128)}, u32[]{:S(2)}) copy-start(s32[4,16]{1,0:T(4,128)} %refs_0_) | copy-start | bytes 772
  21.2 0.7 %copy-start.6 = (s32[4,16]{1,0:T(4,128)S(1)}, s32[4,16]{1,0:T(4,128)}, u32[]{:S(2)}) copy-start(s32[4,16]{1,0:T(4,128)} %refs_1_.1) | copy-start | bytes 772
  21.9 0.7 %copy-start.7 = (s32[4,16]{1,0:T(4,128)S(1)}, s32[4,16]{1,0:T(4,128)}, u32[]{:S(2)}) copy-start(s32[4,16]{1,0:T(4,128)} %refs_2_.1) | copy-start | bytes 772
  22.5 0.7 %copy-start.8 = (s32[4,16]{1,0:T(4,128)S(1)}, s32[4,16]{1,0:T(4,128)}, u32[]{:S(2)}) copy-start(s32[4,16]{1,0:T(4,128)} %refs_3_.1) | copy-start | bytes 772
  32.2 17.3 %copy-start.4 = (bf16[128,128]{1,0:T(8,128)(2,1)S(1)}, bf16[128,128]{1,0:T(8,128)(2,1)}, u32[]{:S(2)}) copy-start(bf16[128,128]{1,0:T(8,128)(2,1)} %dis_ref.1) | copy-start | bytes 98308
  39.9 5.2 %collective-permute-start.10 = (bf16[8,32,128]{2,1,0:T(8,128)(2,1)S(1)}, bf16[8,32,128]{2,1,0:T(8,128)(2,1)S(1)}, u32[]{:S(2)}, u32[]{:S(2)}) collective-permute-start(bf16[8,32,128]{2,1,0:T(8,128)(2,1)S(1)} %get-tuple-element.55), channel_id=1, source_target_pairs={{0,7},{1,6},{2,5},{3,4},{4,3},{5,2},{6,1},{7,0},{8,15},{9,14},{10,... | collective-permute-start | bytes 196616 | tf_op jit(solution)/shard_map/ppermute | solution.py:345
  40.7 6.1 %collective-permute-start.11 = (bf16[8,32,128]{2,1,0:T(8,128)(2,1)S(1)}, bf16[8,32,128]{2,1,0:T(8,128)(2,1)S(1)}, u32[]{:S(2)}, u32[]{:S(2)}) collective-permute-start(bf16[8,32,128]{2,1,0:T(8,128)(2,1)S(1)} %get-tuple-element.56), channel_id=1, source_target_pairs={{0,6},{1,7},{2,4},{3,5},{4,2},{5,3},{6,0},{7,1},{8,14},{9,15},{10,... | collective-permute-start | bytes 196616 | tf_op jit(solution)/shard_map/ppermute | solution.py:345
  42.5 4.6 %collective-permute-start.12 = (bf16[8,32,128]{2,1,0:T(8,128)(2,1)S(1)}, bf16[8,32,128]{2,1,0:T(8,128)(2,1)S(1)}, u32[]{:S(2)}, u32[]{:S(2)}) collective-permute-start(bf16[8,32,128]{2,1,0:T(8,128)(2,1)S(1)} %get-tuple-element.57), channel_id=1, source_target_pairs={{0,3},{1,2},{2,1},{3,0},{4,7},{5,6},{6,5},{7,4},{8,11},{9,10},{10,... | collective-permute-start | bytes 196616 | tf_op jit(solution)/shard_map/ppermute | solution.py:345
  43.5 4.3 %collective-permute-start.13 = (bf16[8,32,128]{2,1,0:T(8,128)(2,1)S(1)}, bf16[8,32,128]{2,1,0:T(8,128)(2,1)S(1)}, u32[]{:S(2)}, u32[]{:S(2)}) collective-permute-start(bf16[8,32,128]{2,1,0:T(8,128)(2,1)S(1)} %get-tuple-element.58), channel_id=1, source_target_pairs={{0,5},{1,4},{2,7},{3,6},{4,1},{5,0},{6,3},{7,2},{8,13},{9,12},{10,... | collective-permute-start | bytes 196616 | tf_op jit(solution)/shard_map/ppermute | solution.py:345
  43.9 5.0 %collective-permute-start.14 = (bf16[8,32,128]{2,1,0:T(8,128)(2,1)S(1)}, bf16[8,32,128]{2,1,0:T(8,128)(2,1)S(1)}, u32[]{:S(2)}, u32[]{:S(2)}) collective-permute-start(bf16[8,32,128]{2,1,0:T(8,128)(2,1)S(1)} %get-tuple-element.59), channel_id=1, source_target_pairs={{0,2},{1,3},{2,0},{3,1},{4,6},{5,7},{6,4},{7,5},{8,10},{9,11},{10,... | collective-permute-start | bytes 196616 | tf_op jit(solution)/shard_map/ppermute | solution.py:345
  45.0 4.4 %collective-permute-start.15 = (bf16[8,32,128]{2,1,0:T(8,128)(2,1)S(1)}, bf16[8,32,128]{2,1,0:T(8,128)(2,1)S(1)}, u32[]{:S(2)}, u32[]{:S(2)}) collective-permute-start(bf16[8,32,128]{2,1,0:T(8,128)(2,1)S(1)} %get-tuple-element.60), channel_id=1, source_target_pairs={{0,4},{1,5},{2,6},{3,7},{4,0},{5,1},{6,2},{7,3},{8,12},{9,13},{10,... | collective-permute-start | bytes 196616 | tf_op jit(solution)/shard_map/ppermute | solution.py:345
  46.8 2.6 %collective-permute-start.16 = (bf16[8,32,128]{2,1,0:T(8,128)(2,1)S(1)}, bf16[8,32,128]{2,1,0:T(8,128)(2,1)S(1)}, u32[]{:S(2)}, u32[]{:S(2)}) collective-permute-start(bf16[8,32,128]{2,1,0:T(8,128)(2,1)S(1)} %get-tuple-element.61), channel_id=1, source_target_pairs={{0,1},{1,0},{2,3},{3,2},{4,5},{5,4},{6,7},{7,6},{8,9},{9,8},{10,11... | collective-permute-start | bytes 196616 | tf_op jit(solution)/shard_map/ppermute | solution.py:345

commit v7 on v6

--- a/solution.py
+++ b/solution.py
@@ -45,9 +45,13 @@
     def kernel(place_ref, fields_ref, agg_ref, *refs):
         outs, scratch = refs[:devices], refs[devices]
         matrix = jnp.concatenate([agg_ref[:, :unknowns], agg_ref[:, unknowns:]], axis=0)
-        for box in range(boxes):
-            both = jnp.dot(matrix, fields_ref[box], preferred_element_type=jnp.float32)
-            scratch[pl.ds(box * (all_dirs + 1), all_dirs), :] = both[:all_dirs] + turned(both[all_dirs:])
+        for box in range(0, boxes, 2):
+            pair = jnp.concatenate([fields_ref[box], fields_ref[box + 1]], axis=1)
+            wide = jnp.dot(matrix, pair, preferred_element_type=jnp.float32)
+            for side in range(2):
+                both = wide[:, side * columns : (side + 1) * columns]
+                at = pl.ds((box + side) * (all_dirs + 1), all_dirs)
+                scratch[at, :] = both[:all_dirs] + turned(both[all_dirs:])
         for step in range(devices):
             first = (place_ref[0] ^ step) * part
             for inner in range(part):
@@ -315,9 +319,11 @@
         matrix = dis_ref[...]
         copies = []
         for cut in range(cuts):
-            for box in range(cut * size, (cut + 1) * size):
-                rows = stack_rows(scratch[pl.ds(box, all_dirs, stride=boxes + 1), :])
-                result[box] = jnp.dot(matrix, rows, preferred_element_type=jnp.float32).astype(jnp.bfloat16)
+            for box in range(cut * size, (cut + 1) * size, 2):
+                rows = [stack_rows(scratch[pl.ds(box + side, all_dirs, stride=boxes + 1), :]) for side in range(2)]
+                both = jnp.dot(matrix, jnp.concatenate(rows, axis=1), preferred_element_type=jnp.float32)
+                for side in range(2):
+                    result[box + side] = both[:, side * columns : (side + 1) * columns].astype(jnp.bfloat16)
             at = pl.ds(cut * size, size)
             copies.append(pltpu.make_async_copy(result.at[at], out_hbm.at[at], sem.at[cut]))
             copies[cut].start()

time: 51.1 us -> 51.1 us (level)
  transfers between devices with their start and end apart: 17 -> 17, of which waited for: 12 -> 11; matrix products, arithmetic and copies ran while one was open for 0% -> 0% of each run, Pallas kernels for 18% -> 18%
where the time goes in v7:
time: 51.1 us; the launch traced here: 50.8 us
  starting transfers between devices  16.8 us (33%)
  waiting for transfers between devices  13.8 us (27%)
  Pallas kernels  12 us (23%)
  local copies, waits for them, and re-layouts  8.11 us (16%)
    ppermute x17, starting transfers between devices, crossed(): lax.ppermute(pieces[step], axis, [(i, i ^ step) for i in range(count)])  16.8 us
    ppermute x17, waiting for transfers between devices, crossed(): lax.ppermute(pieces[step], axis, [(i, i ^ step) for i in range(count)])  13.8 us
    unnamed x18, local copies, waits for them, and re-layouts  8.11 us
    pallas_call x1, Pallas kernels, build(): pl.pallas_call(kernel, grid=(dirs,), out_shape=[jax.ShapeDtypeStruct((dir...  5.83 us
    pallas_call x1, Pallas kernels, far_first(): pl.pallas_call(kernel, grid=(dirs // group,), out_shape=jax.ShapeDtypeStr...  1.55 us
    pallas_call x1, Pallas kernels, near_product(): pl.pallas_call(kernel, grid=(dirs // group,), out_shape=jax.ShapeDtypeStr...  1.53 us
    pallas_call x1, Pallas kernels, disaggregate(): pl.pallas_call(kernel, out_shape=jax.ShapeDtypeStruct((boxes, unknowns, c...  1.38 us
  transfers between devices with their start and end apart: 17, of which 11 were waited for; matrix products, arithmetic and copies ran while one was open for 0% of the time, Pallas kernels for 18%

profile of v7, /device:TPU:16, one launch (start us, length us, event | category | flops | bytes accessed | tf_op | source)
XLA Modules:
  0.0 50.8 jit_solution(16645338687576624487)
XLA Ops:
  0.0 1.2 %copy-done.2 = bf16[32,128,128]{2,1,0:T(8,128)(2,1)S(1)} copy-done((bf16[32,128,128]{2,1,0:T(8,128)(2,1)S(1)}, bf16[32,128,128]{2,1,0:T(8,128)(2,1)}, u32[]{:S(2)}) %copy-start.2) | copy-done | bytes 1048600
  1.2 0.8 %copy-done.3 = bf16[64,256]{1,0:T(8,128)(2,1)S(1)} copy-done((bf16[64,256]{1,0:T(8,128)(2,1)S(1)}, bf16[64,256]{1,0:T(8,128)(2,1)}, u32[]{:S(2)}) %copy-start.3) | copy-done | bytes 32792
  2.0 0.6 %aggregate.1 = (bf16[8,32,128]{2,1,0:T(8,128)(2,1)S(1)}, bf16[8,32,128]{2,1,0:T(8,128)(2,1)S(1)}, bf16[8,32,128]{2,1,0:T(8,128)(2,1)S(1)}, bf16[8,32,128]{2,1,0:...) custom-call(s32[1]{0:T(128)} %bitcast.place_ref, ...), custom_call_target="tpu_custom_call" | custom-call | flops 1 | bytes 1 | tf_op jit(solution)/shard_map/aggregate/pallas_call | solution.py:61
  2.6 2.0 %collective-permute-start = (bf16[8,32,128]{2,1,0:T(8,128)(2,1)S(1)}, bf16[8,32,128]{2,1,0:T(8,128)(2,1)S(1)}, u32[]{:S(2)}, u32[]{:S(2)}) collective-permute-start(bf16[8,32,128]{2,1,0:T(8,128)(2,1)S(1)} %get-tuple-element.36), channel_id=1, source_target_pairs={{0,7},{1,6},{2,5},{3,4},{4,3},{5,2},{6,1},{7,0},{8,15},{9,14},{10,... | collective-permute-start | bytes 196616 | tf_op jit(solution)/shard_map/ppermute | solution.py:351
  4.5 0.6 %collective-permute-start.1 = (bf16[8,32,128]{2,1,0:T(8,128)(2,1)S(1)}, bf16[8,32,128]{2,1,0:T(8,128)(2,1)S(1)}, u32[]{:S(2)}, u32[]{:S(2)}) collective-permute-start(bf16[8,32,128]{2,1,0:T(8,128)(2,1)S(1)} %get-tuple-element.37), channel_id=1, source_target_pairs={{0,6},{1,7},{2,4},{3,5},{4,2},{5,3},{6,0},{7,1},{8,14},{9,15},{10,... | collective-permute-start | bytes 196616 | tf_op jit(solution)/shard_map/ppermute | solution.py:351
  5.2 1.3 %collective-permute-start.2 = (bf16[8,32,128]{2,1,0:T(8,128)(2,1)S(1)}, bf16[8,32,128]{2,1,0:T(8,128)(2,1)S(1)}, u32[]{:S(2)}, u32[]{:S(2)}) collective-permute-start(bf16[8,32,128]{2,1,0:T(8,128)(2,1)S(1)} %get-tuple-element.38), channel_id=1, source_target_pairs={{0,3},{1,2},{2,1},{3,0},{4,7},{5,6},{6,5},{7,4},{8,11},{9,10},{10,... | collective-permute-start | bytes 196616 | tf_op jit(solution)/shard_map/ppermute | solution.py:351
  6.5 1.3 %collective-permute-start.3 = (bf16[8,32,128]{2,1,0:T(8,128)(2,1)S(1)}, bf16[8,32,128]{2,1,0:T(8,128)(2,1)S(1)}, u32[]{:S(2)}, u32[]{:S(2)}) collective-permute-start(bf16[8,32,128]{2,1,0:T(8,128)(2,1)S(1)} %get-tuple-element.39), channel_id=1, source_target_pairs={{0,5},{1,4},{2,7},{3,6},{4,1},{5,0},{6,3},{7,2},{8,13},{9,12},{10,... | collective-permute-start | bytes 196616 | tf_op jit(solution)/shard_map/ppermute | solution.py:351
  7.8 0.5 %collective-permute-start.4 = (bf16[8,32,128]{2,1,0:T(8,128)(2,1)S(1)}, bf16[8,32,128]{2,1,0:T(8,128)(2,1)S(1)}, u32[]{:S(2)}, u32[]{:S(2)}) collective-permute-start(bf16[8,32,128]{2,1,0:T(8,128)(2,1)S(1)} %get-tuple-element.40), channel_id=1, source_target_pairs={{0,2},{1,3},{2,0},{3,1},{4,6},{5,7},{6,4},{7,5},{8,10},{9,11},{10,... | collective-permute-start | bytes 196616 | tf_op jit(solution)/shard_map/ppermute | solution.py:351
  8.3 0.0 collective-permute-done.refs_0_
  8.3 1.1 %collective-permute-start.5 = (bf16[8,32,128]{2,1,0:T(8,128)(2,1)S(1)}, bf16[8,32,128]{2,1,0:T(8,128)(2,1)S(1)}, u32[]{:S(2)}, u32[]{:S(2)}) collective-permute-start(bf16[8,32,128]{2,1,0:T(8,128)(2,1)S(1)} %get-tuple-element.41), channel_id=1, source_target_pairs={{0,4},{1,5},{2,6},{3,7},{4,0},{5,1},{6,2},{7,3},{8,12},{9,13},{10,... | collective-permute-start | bytes 196616 | tf_op jit(solution)/shard_map/ppermute | solution.py:351
  9.4 1.0 %collective-permute-done.1.refs_1_ = bf16[8,32,128]{2,1,0:T(8,128)(2,1)S(1)} collective-permute-done((bf16[8,32,128]{2,1,0:T(8,128)(2,1)S(1)}, bf16[8,32,128]{2,1,0:T(8,128)(2,1)S(1)}, u32[]{:S(2)}, u32[]{:S(2)}) %collective-permute-start.1) | collective-permute-done | bytes 65568 | tf_op jit(solution)/shard_map/ppermute | solution.py:351
  10.4 0.0 collective-permute-start.6
  10.4 0.3 collective-permute-done.2.refs_2_
  10.7 0.8 %collective-permute-done.3.refs_3_ = bf16[8,32,128]{2,1,0:T(8,128)(2,1)S(1)} collective-permute-done((bf16[8,32,128]{2,1,0:T(8,128)(2,1)S(1)}, bf16[8,32,128]{2,1,0:T(8,128)(2,1)S(1)}, u32[]{:S(2)}, u32[]{:S(2)}) %collective-permute-start.3) | collective-permute-done | bytes 65568 | tf_op jit(solution)/shard_map/ppermute | solution.py:351
  11.5 0.7 %collective-permute-done.4.refs_4_ = bf16[8,32,128]{2,1,0:T(8,128)(2,1)S(1)} collective-permute-done((bf16[8,32,128]{2,1,0:T(8,128)(2,1)S(1)}, bf16[8,32,128]{2,1,0:T(8,128)(2,1)S(1)}, u32[]{:S(2)}, u32[]{:S(2)}) %collective-permute-start.4) | collective-permute-done | bytes 65568 | tf_op jit(solution)/shard_map/ppermute | solution.py:351
  12.2 0.7 %collective-permute-done.5.refs_5_ = bf16[8,32,128]{2,1,0:T(8,128)(2,1)S(1)} collective-permute-done((bf16[8,32,128]{2,1,0:T(8,128)(2,1)S(1)}, bf16[8,32,128]{2,1,0:T(8,128)(2,1)S(1)}, u32[]{:S(2)}, u32[]{:S(2)}) %collective-permute-start.5) | collective-permute-done | bytes 65568 | tf_op jit(solution)/shard_map/ppermute | solution.py:351
  12.9 0.0 collective-permute-done.6.refs_6_
  12.9 0.6 %pick.1 = (bf16[8,8,32,128]{3,2,1,0:T(8,128)(2,1)S(1)}, bf16[2,2,8,32,128]{4,3,2,1,0:T(8,128)(2,1)S(1)}, bf16[2,2,8,32,128]{4,3,2,1,0:T(8,128)(2,1)S(1)}, bf16[2,2,8,32,128]{4,3,2,1,0:T(8,128)(2,1)S(1)}) custom-call(s32[2,4]{1,0:T(2,128)S(1)} %dynamic-slice_bitcast_fusion.listing_ref, s32[1]{0:T(128)} %bitcast.1.where_ref, s32[1]{0:T(128)} %bitcast.place_ref, ...), custom_call_target="tpu_custom_call" | custom-call | flops 1 | bytes 1 | tf_op jit(solution)/shard_map/pick/pallas_call | solution.py:89
  13.6 0.4 collective-permute-start.7
  14.0 1.6 %collective-permute-start.8 = (bf16[2,2,8,32,128]{4,3,2,1,0:T(8,128)(2,1)S(1)}, bf16[2,2,8,32,128]{4,3,2,1,0:T(8,128)(2,1)S(1)}, u32[]{:S(2)}, u32[]{:S(2)}) collective-permute-start(bf16[2,2,8,32,128]{4,3,2,1,0:T(8,128)(2,1)S(1)} %get-tuple-element.53), channel_id=1, source_target_pairs={{0,8},{8,0},{16,24},{24,16},{1,9},{9,1},{17,25},{25,17},{2,10},{10... | collective-permute-start | bytes 786440 | tf_op jit(solution)/shard_map/ppermute | solution.py:351
  15.5 1.6 %collective-permute-start.9 = (bf16[2,2,8,32,128]{4,3,2,1,0:T(8,128)(2,1)S(1)}, bf16[2,2,8,32,128]{4,3,2,1,0:T(8,128)(2,1)S(1)}, u32[]{:S(2)}, u32[]{:S(2)}) collective-permute-start(bf16[2,2,8,32,128]{4,3,2,1,0:T(8,128)(2,1)S(1)} %get-tuple-element.54), channel_id=1, source_target_pairs={{0,24},{8,16},{16,8},{24,0},{1,25},{9,17},{17,9},{25,1},{2,26},{10... | collective-permute-start | bytes 786440 | tf_op jit(solution)/shard_map/ppermute | solution.py:351
  17.1 3.4 %copy-done.1 = bf16[64,8,64,128]{3,2,1,0:T(8,128)(2,1)S(1)} copy-done((bf16[64,8,64,128]{3,2,1,0:T(8,128)(2,1)S(1)}, bf16[64,8,64,128]{3,2,1,0:T(8,128)(2,1)}, u32[]{:S(2)}) %copy-start.1) | copy-done | bytes 8388632
  20.5 0.7 %copy-done.5 = s32[4,16]{1,0:T(4,128)S(1)} copy-done((s32[4,16]{1,0:T(4,128)S(1)}, s32[4,16]{1,0:T(4,128)}, u32[]{:S(2)}) %copy-start.5) | copy-done | bytes 280
  21.2 0.7 %copy-done.6 = s32[4,16]{1,0:T(4,128)S(1)} copy-done((s32[4,16]{1,0:T(4,128)S(1)}, s32[4,16]{1,0:T(4,128)}, u32[]{:S(2)}) %copy-start.6) | copy-done | bytes 280
  21.9 0.7 %copy-done.7 = s32[4,16]{1,0:T(4,128)S(1)} copy-done((s32[4,16]{1,0:T(4,128)S(1)}, s32[4,16]{1,0:T(4,128)}, u32[]{:S(2)}) %copy-start.7) | copy-done | bytes 280
  22.5 0.7 %copy-done.8 = s32[4,16]{1,0:T(4,128)S(1)} copy-done((s32[4,16]{1,0:T(4,128)S(1)}, s32[4,16]{1,0:T(4,128)}, u32[]{:S(2)}) %copy-start.8) | copy-done | bytes 280
  23.2 5.8 %build.1 = (bf16[8,4,256,128]{3,2,1,0:T(8,128)(2,1)S(1)}, bf16[8,4,256,128]{3,2,1,0:T(8,128)(2,1)S(1)}, bf16[8,2,256,128]{3,2,1,0:T(8,128)(2,1)S(1)}) custom-call(s32[1]{0:T(128)} %bitcast.1.where_ref, s32[4,16]{1,0:T(4,128)S(1)} %copy-done.5, s32[4,16]{1,0:T(4,128)S(1)} %copy-done.6, s32[4,16]{1,0:T(4,128)S(1)} %copy-done.7, s32[4,16]{1,0:T(4,128)S(1)} %copy-done.8, ...), custom_call_target="tpu_custom_call" | custom-call | flops 1 | bytes 1 | tf_op jit(solution)/shard_map/build/pallas_call | solution.py:171
  29.1 1.5 %near_product.1.before_ref = f32[8,256,128]{2,1,0:T(8,128)S(1)} custom-call(bf16[8,4,256,128]{3,2,1,0:T(8,128)(2,1)S(1)} %get-tuple-element.50.block_ref, bf16[8,8,32,128]{3,2,1,0:T(8,128)(2,1)S(1)} %get-tuple-element.51.slab_ref), custom_call_target="tpu_custom_call" | custom-call | flops 1 | bytes 1 | tf_op jit(solution)/shard_map/near_product/pallas_call | solution.py:221
  30.6 0.0 collective-permute-done.8.refs_1_
  30.6 1.5 %far_first.1.before_ref = f32[8,256,128]{2,1,0:T(8,128)S(1)} custom-call(bf16[8,4,256,128]{3,2,1,0:T(8,128)(2,1)S(1)} %get-tuple-element.49.block_ref, f32[8,256,128]{2,1,0:T(8,128)S(1)} %near_product.1.before_ref, bf16[2,2,8,32,128]{4,3,2,1,0:T(8,128)(2,1)S(1)} %collective-permute-done.7.refs_0_, bf16[2,2,8,32,128]{4,3,2,1,0:T(8,128)(2,1)S(1)} %collective-permute-done.8.refs_1_), custom_call_target="tpu_custom_call" | custom-call | flops 1 | bytes 1 | tf_op jit(solution)/shard_map/far_first/pallas_call | solution.py:259
  32.2 0.0 copy-start.4
  32.2 7.1 %collective-permute-done.9.arrived_ref = bf16[2,2,8,32,128]{4,3,2,1,0:T(8,128)(2,1)S(1)} collective-permute-done((bf16[2,2,8,32,128]{4,3,2,1,0:T(8,128)(2,1)S(1)}, bf16[2,2,8,32,128]{4,3,2,1,0:T(8,128)(2,1)S(1)}, u32[]{:S(2)}, u32[]{:S(2)}) %collective-permute-start.9) | collective-permute-done | bytes 262176 | tf_op jit(solution)/shard_map/ppermute | solution.py:351
  39.3 0.5 %far_last.1 = (bf16[8,32,128]{2,1,0:T(8,128)(2,1)S(1)}, bf16[8,32,128]{2,1,0:T(8,128)(2,1)S(1)}, bf16[8,32,128]{2,1,0:T(8,128)(2,1)S(1)}, bf16[8,32,128]{2,1,0:T...) custom-call(s32[1]{0:T(128)} %bitcast.place_ref, ...), custom_call_target="tpu_custom_call" | custom-call | flops 1 | bytes 1 | tf_op jit(solution)/shard_map/far_last/pallas_call | solution.py:292
  39.8 0.9 %collective-permute-start.10 = (bf16[8,32,128]{2,1,0:T(8,128)(2,1)S(1)}, bf16[8,32,128]{2,1,0:T(8,128)(2,1)S(1)}, u32[]{:S(2)}, u32[]{:S(2)}) collective-permute-start(bf16[8,32,128]{2,1,0:T(8,128)(2,1)S(1)} %get-tuple-element.55), channel_id=1, source_target_pairs={{0,7},{1,6},{2,5},{3,4},{4,3},{5,2},{6,1},{7,0},{8,15},{9,14},{10,... | collective-permute-start | bytes 196616 | tf_op jit(solution)/shard_map/ppermute | solution.py:351
  40.7 1.7 %collective-permute-start.11 = (bf16[8,32,128]{2,1,0:T(8,128)(2,1)S(1)}, bf16[8,32,128]{2,1,0:T(8,128)(2,1)S(1)}, u32[]{:S(2)}, u32[]{:S(2)}) collective-permute-start(bf16[8,32,128]{2,1,0:T(8,128)(2,1)S(1)} %get-tuple-element.56), channel_id=1, source_target_pairs={{0,6},{1,7},{2,4},{3,5},{4,2},{5,3},{6,0},{7,1},{8,14},{9,15},{10,... | collective-permute-start | bytes 196616 | tf_op jit(solution)/shard_map/ppermute | solution.py:351
  42.4 1.0 %collective-permute-start.12 = (bf16[8,32,128]{2,1,0:T(8,128)(2,1)S(1)}, bf16[8,32,128]{2,1,0:T(8,128)(2,1)S(1)}, u32[]{:S(2)}, u32[]{:S(2)}) collective-permute-start(bf16[8,32,128]{2,1,0:T(8,128)(2,1)S(1)} %get-tuple-element.57), channel_id=1, source_target_pairs={{0,3},{1,2},{2,1},{3,0},{4,7},{5,6},{6,5},{7,4},{8,11},{9,10},{10,... | collective-permute-start | bytes 196616 | tf_op jit(solution)/shard_map/ppermute | solution.py:351
  43.5 0.4 collective-permute-start.13
  43.9 1.1 %collective-permute-start.14 = (bf16[8,32,128]{2,1,0:T(8,128)(2,1)S(1)}, bf16[8,32,128]{2,1,0:T(8,128)(2,1)S(1)}, u32[]{:S(2)}, u32[]{:S(2)}) collective-permute-start(bf16[8,32,128]{2,1,0:T(8,128)(2,1)S(1)} %get-tuple-element.59), channel_id=1, source_target_pairs={{0,2},{1,3},{2,0},{3,1},{4,6},{5,7},{6,4},{7,5},{8,10},{9,11},{10,... | collective-permute-start | bytes 196616 | tf_op jit(solution)/shard_map/ppermute | solution.py:351
  45.0 0.0 collective-permute-done.10.refs_0_
  45.0 1.2 %collective-permute-start.15 = (bf16[8,32,128]{2,1,0:T(8,128)(2,1)S(1)}, bf16[8,32,128]{2,1,0:T(8,128)(2,1)S(1)}, u32[]{:S(2)}, u32[]{:S(2)}) collective-permute-start(bf16[8,32,128]{2,1,0:T(8,128)(2,1)S(1)} %get-tuple-element.60), channel_id=1, source_target_pairs={{0,4},{1,5},{2,6},{3,7},{4,0},{5,1},{6,2},{7,3},{8,12},{9,13},{10,... | collective-permute-start | bytes 196616 | tf_op jit(solution)/shard_map/ppermute | solution.py:351
  46.2 0.6 %collective-permute-done.11.refs_1_ = bf16[8,32,128]{2,1,0:T(8,128)(2,1)S(1)} collective-permute-done((bf16[8,32,128]{2,1,0:T(8,128)(2,1)S(1)}, bf16[8,32,128]{2,1,0:T(8,128)(2,1)S(1)}, u32[]{:S(2)}, u32[]{:S(2)}) %collective-permute-start.11) | collective-permute-done | bytes 65568 | tf_op jit(solution)/shard_map/ppermute | solution.py:351
  46.8 0.0 collective-permute-start.16
  46.8 0.3 collective-permute-done.12.refs_2_
  47.1 0.6 %collective-permute-done.13.refs_3_ = bf16[8,32,128]{2,1,0:T(8,128)(2,1)S(1)} collective-permute-done((bf16[8,32,128]{2,1,0:T(8,128)(2,1)S(1)}, bf16[8,32,128]{2,1,0:T(8,128)(2,1)S(1)}, u32[]{:S(2)}, u32[]{:S(2)}) %collective-permute-start.13) | collective-permute-done | bytes 65568 | tf_op jit(solution)/shard_map/ppermute | solution.py:351
  47.7 1.2 %collective-permute-done.14.refs_4_ = bf16[8,32,128]{2,1,0:T(8,128)(2,1)S(1)} collective-permute-done((bf16[8,32,128]{2,1,0:T(8,128)(2,1)S(1)}, bf16[8,32,128]{2,1,0:T(8,128)(2,1)S(1)}, u32[]{:S(2)}, u32[]{:S(2)}) %collective-permute-start.14) | collective-permute-done | bytes 65568 | tf_op jit(solution)/shard_map/ppermute | solution.py:351
  48.9 0.5 collective-permute-done.15.refs_5_
  49.4 0.0 collective-permute-done.16.refs_6_
  49.4 1.4 %disaggregate.1 = bf16[32,128,128]{2,1,0:T(8,128)(2,1)} custom-call(s32[1]{0:T(128)} %bitcast.place_ref, bf16[128,128]{1,0:T(8,128)(2,1)S(1)} %copy-done.4, bf16[8,32,128]{2,1,0:T(8,128)(2,1)S(1)} %collective-permute-done.10.refs_0_, bf16[8,32,128]{2,1,0:T(8,128)(2,1)S(1)} %collective-permute-done.11.refs_1_, ...), custom_call_target="tpu_custom_call" | custom-call | flops 1 | bytes 1 | tf_op jit(solution)/shard_map/disaggregate/pallas_call | solution.py:333
  (12 shorter events, 0.0 us)
Async XLA Ops:
  0.0 10.4 %copy-start = (s32[4,4,2]{1,2,0:T(2,128)S(1)}, s32[4,4,2]{1,2,0:T(2,128)}, u32[]{:S(2)}) copy-start(s32[4,4,2]{1,2,0:T(2,128)} %param.17) | copy-start | bytes 388
  0.0 1.2 %copy-start.2 = (bf16[32,128,128]{2,1,0:T(8,128)(2,1)S(1)}, bf16[32,128,128]{2,1,0:T(8,128)(2,1)}, u32[]{:S(2)}) copy-start(bf16[32,128,128]{2,1,0:T(8,128)(2,1)} %fields_ref.1) | copy-start | bytes 3145732
  1.2 0.8 %copy-start.3 = (bf16[64,256]{1,0:T(8,128)(2,1)S(1)}, bf16[64,256]{1,0:T(8,128)(2,1)}, u32[]{:S(2)}) copy-start(bf16[64,256]{1,0:T(8,128)(2,1)} %agg_ref.1) | copy-start | bytes 98308
  2.6 5.7 %collective-permute-start = (bf16[8,32,128]{2,1,0:T(8,128)(2,1)S(1)}, bf16[8,32,128]{2,1,0:T(8,128)(2,1)S(1)}, u32[]{:S(2)}, u32[]{:S(2)}) collective-permute-start(bf16[8,32,128]{2,1,0:T(8,128)(2,1)S(1)} %get-tuple-element.36), channel_id=1, source_target_pairs={{0,7},{1,6},{2,5},{3,4},{4,3},{5,2},{6,1},{7,0},{8,15},{9,14},{10,... | collective-permute-start | bytes 196616 | tf_op jit(solution)/shard_map/ppermute | solution.py:351
  4.5 5.9 %collective-permute-start.1 = (bf16[8,32,128]{2,1,0:T(8,128)(2,1)S(1)}, bf16[8,32,128]{2,1,0:T(8,128)(2,1)S(1)}, u32[]{:S(2)}, u32[]{:S(2)}) collective-permute-start(bf16[8,32,128]{2,1,0:T(8,128)(2,1)S(1)} %get-tuple-element.37), channel_id=1, source_target_pairs={{0,6},{1,7},{2,4},{3,5},{4,2},{5,3},{6,0},{7,1},{8,14},{9,15},{10,... | collective-permute-start | bytes 196616 | tf_op jit(solution)/shard_map/ppermute | solution.py:351
  5.2 5.5 %collective-permute-start.2 = (bf16[8,32,128]{2,1,0:T(8,128)(2,1)S(1)}, bf16[8,32,128]{2,1,0:T(8,128)(2,1)S(1)}, u32[]{:S(2)}, u32[]{:S(2)}) collective-permute-start(bf16[8,32,128]{2,1,0:T(8,128)(2,1)S(1)} %get-tuple-element.38), channel_id=1, source_target_pairs={{0,3},{1,2},{2,1},{3,0},{4,7},{5,6},{6,5},{7,4},{8,11},{9,10},{10,... | collective-permute-start | bytes 196616 | tf_op jit(solution)/shard_map/ppermute | solution.py:351
  6.5 5.0 %collective-permute-start.3 = (bf16[8,32,128]{2,1,0:T(8,128)(2,1)S(1)}, bf16[8,32,128]{2,1,0:T(8,128)(2,1)S(1)}, u32[]{:S(2)}, u32[]{:S(2)}) collective-permute-start(bf16[8,32,128]{2,1,0:T(8,128)(2,1)S(1)} %get-tuple-element.39), channel_id=1, source_target_pairs={{0,5},{1,4},{2,7},{3,6},{4,1},{5,0},{6,3},{7,2},{8,13},{9,12},{10,... | collective-permute-start | bytes 196616 | tf_op jit(solution)/shard_map/ppermute | solution.py:351
  7.8 4.4 %collective-permute-start.4 = (bf16[8,32,128]{2,1,0:T(8,128)(2,1)S(1)}, bf16[8,32,128]{2,1,0:T(8,128)(2,1)S(1)}, u32[]{:S(2)}, u32[]{:S(2)}) collective-permute-start(bf16[8,32,128]{2,1,0:T(8,128)(2,1)S(1)} %get-tuple-element.40), channel_id=1, source_target_pairs={{0,2},{1,3},{2,0},{3,1},{4,6},{5,7},{6,4},{7,5},{8,10},{9,11},{10,... | collective-permute-start | bytes 196616 | tf_op jit(solution)/shard_map/ppermute | solution.py:351
  8.3 4.6 %collective-permute-start.5 = (bf16[8,32,128]{2,1,0:T(8,128)(2,1)S(1)}, bf16[8,32,128]{2,1,0:T(8,128)(2,1)S(1)}, u32[]{:S(2)}, u32[]{:S(2)}) collective-permute-start(bf16[8,32,128]{2,1,0:T(8,128)(2,1)S(1)} %get-tuple-element.41), channel_id=1, source_target_pairs={{0,4},{1,5},{2,6},{3,7},{4,0},{5,1},{6,2},{7,3},{8,12},{9,13},{10,... | collective-permute-start | bytes 196616 | tf_op jit(solution)/shard_map/ppermute | solution.py:351
  10.4 2.5 %collective-permute-start.6 = (bf16[8,32,128]{2,1,0:T(8,128)(2,1)S(1)}, bf16[8,32,128]{2,1,0:T(8,128)(2,1)S(1)}, u32[]{:S(2)}, u32[]{:S(2)}) collective-permute-start(bf16[8,32,128]{2,1,0:T(8,128)(2,1)S(1)} %get-tuple-element.42), channel_id=1, source_target_pairs={{0,1},{1,0},{2,3},{3,2},{4,5},{5,4},{6,7},{7,6},{8,9},{9,8},{10,11... | collective-permute-start | bytes 196616 | tf_op jit(solution)/shard_map/ppermute | solution.py:351
  13.6 17.0 %collective-permute-start.7 = (bf16[2,2,8,32,128]{4,3,2,1,0:T(8,128)(2,1)S(1)}, bf16[2,2,8,32,128]{4,3,2,1,0:T(8,128)(2,1)S(1)}, u32[]{:S(2)}, u32[]{:S(2)}) collective-permute-start(bf16[2,2,8,32,128]{4,3,2,1,0:T(8,128)(2,1)S(1)} %get-tuple-element.52), channel_id=1, source_target_pairs={{0,16},{8,24},{16,0},{24,8},{1,17},{9,25},{17,1},{25,9},{2,18},{10... | collective-permute-start | bytes 786440 | tf_op jit(solution)/shard_map/ppermute | solution.py:351
  14.0 16.7 %collective-permute-start.8 = (bf16[2,2,8,32,128]{4,3,2,1,0:T(8,128)(2,1)S(1)}, bf16[2,2,8,32,128]{4,3,2,1,0:T(8,128)(2,1)S(1)}, u32[]{:S(2)}, u32[]{:S(2)}) collective-permute-start(bf16[2,2,8,32,128]{4,3,2,1,0:T(8,128)(2,1)S(1)} %get-tuple-element.53), channel_id=1, source_target_pairs={{0,8},{8,0},{16,24},{24,16},{1,9},{9,1},{17,25},{25,17},{2,10},{10... | collective-permute-start | bytes 786440 | tf_op jit(solution)/shard_map/ppermute | solution.py:351
  15.5 23.7 %collective-permute-start.9 = (bf16[2,2,8,32,128]{4,3,2,1,0:T(8,128)(2,1)S(1)}, bf16[2,2,8,32,128]{4,3,2,1,0:T(8,128)(2,1)S(1)}, u32[]{:S(2)}, u32[]{:S(2)}) collective-permute-start(bf16[2,2,8,32,128]{4,3,2,1,0:T(8,128)(2,1)S(1)} %get-tuple-element.54), channel_id=1, source_target_pairs={{0,24},{8,16},{16,8},{24,0},{1,25},{9,17},{17,9},{25,1},{2,26},{10... | collective-permute-start | bytes 786440 | tf_op jit(solution)/shard_map/ppermute | solution.py:351
  17.1 3.4 %copy-start.1 = (bf16[64,8,64,128]{3,2,1,0:T(8,128)(2,1)S(1)}, bf16[64,8,64,128]{3,2,1,0:T(8,128)(2,1)}, u32[]{:S(2)}) copy-start(bf16[64,8,64,128]{3,2,1,0:T(8,128)(2,1)} %refs_4_.1) | copy-start | bytes 25165828
  20.5 0.7 %copy-start.5 = (s32[4,16]{1,0:T(4,128)S(1)}, s32[4,16]{1,0:T(4,128)}, u32[]{:S(2)}) copy-start(s32[4,16]{1,0:T(4,128)} %refs_0_) | copy-start | bytes 772
  21.2 0.7 %copy-start.6 = (s32[4,16]{1,0:T(4,128)S(1)}, s32[4,16]{1,0:T(4,128)}, u32[]{:S(2)}) copy-start(s32[4,16]{1,0:T(4,128)} %refs_1_.1) | copy-start | bytes 772
  21.9 0.7 %copy-start.7 = (s32[4,16]{1,0:T(4,128)S(1)}, s32[4,16]{1,0:T(4,128)}, u32[]{:S(2)}) copy-start(s32[4,16]{1,0:T(4,128)} %refs_2_.1) | copy-start | bytes 772
  22.5 0.7 %copy-start.8 = (s32[4,16]{1,0:T(4,128)S(1)}, s32[4,16]{1,0:T(4,128)}, u32[]{:S(2)}) copy-start(s32[4,16]{1,0:T(4,128)} %refs_3_.1) | copy-start | bytes 772
  32.2 17.2 %copy-start.4 = (bf16[128,128]{1,0:T(8,128)(2,1)S(1)}, bf16[128,128]{1,0:T(8,128)(2,1)}, u32[]{:S(2)}) copy-start(bf16[128,128]{1,0:T(8,128)(2,1)} %dis_ref.1) | copy-start | bytes 98308
  39.8 5.2 %collective-permute-start.10 = (bf16[8,32,128]{2,1,0:T(8,128)(2,1)S(1)}, bf16[8,32,128]{2,1,0:T(8,128)(2,1)S(1)}, u32[]{:S(2)}, u32[]{:S(2)}) collective-permute-start(bf16[8,32,128]{2,1,0:T(8,128)(2,1)S(1)} %get-tuple-element.55), channel_id=1, source_target_pairs={{0,7},{1,6},{2,5},{3,4},{4,3},{5,2},{6,1},{7,0},{8,15},{9,14},{10,... | collective-permute-start | bytes 196616 | tf_op jit(solution)/shard_map/ppermute | solution.py:351
  40.7 6.1 %collective-permute-start.11 = (bf16[8,32,128]{2,1,0:T(8,128)(2,1)S(1)}, bf16[8,32,128]{2,1,0:T(8,128)(2,1)S(1)}, u32[]{:S(2)}, u32[]{:S(2)}) collective-permute-start(bf16[8,32,128]{2,1,0:T(8,128)(2,1)S(1)} %get-tuple-element.56), channel_id=1, source_target_pairs={{0,6},{1,7},{2,4},{3,5},{4,2},{5,3},{6,0},{7,1},{8,14},{9,15},{10,... | collective-permute-start | bytes 196616 | tf_op jit(solution)/shard_map/ppermute | solution.py:351
  42.4 4.7 %collective-permute-start.12 = (bf16[8,32,128]{2,1,0:T(8,128)(2,1)S(1)}, bf16[8,32,128]{2,1,0:T(8,128)(2,1)S(1)}, u32[]{:S(2)}, u32[]{:S(2)}) collective-permute-start(bf16[8,32,128]{2,1,0:T(8,128)(2,1)S(1)} %get-tuple-element.57), channel_id=1, source_target_pairs={{0,3},{1,2},{2,1},{3,0},{4,7},{5,6},{6,5},{7,4},{8,11},{9,10},{10,... | collective-permute-start | bytes 196616 | tf_op jit(solution)/shard_map/ppermute | solution.py:351
  43.5 4.2 %collective-permute-start.13 = (bf16[8,32,128]{2,1,0:T(8,128)(2,1)S(1)}, bf16[8,32,128]{2,1,0:T(8,128)(2,1)S(1)}, u32[]{:S(2)}, u32[]{:S(2)}) collective-permute-start(bf16[8,32,128]{2,1,0:T(8,128)(2,1)S(1)} %get-tuple-element.58), channel_id=1, source_target_pairs={{0,5},{1,4},{2,7},{3,6},{4,1},{5,0},{6,3},{7,2},{8,13},{9,12},{10,... | collective-permute-start | bytes 196616 | tf_op jit(solution)/shard_map/ppermute | solution.py:351
  43.9 5.0 %collective-permute-start.14 = (bf16[8,32,128]{2,1,0:T(8,128)(2,1)S(1)}, bf16[8,32,128]{2,1,0:T(8,128)(2,1)S(1)}, u32[]{:S(2)}, u32[]{:S(2)}) collective-permute-start(bf16[8,32,128]{2,1,0:T(8,128)(2,1)S(1)} %get-tuple-element.59), channel_id=1, source_target_pairs={{0,2},{1,3},{2,0},{3,1},{4,6},{5,7},{6,4},{7,5},{8,10},{9,11},{10,... | collective-permute-start | bytes 196616 | tf_op jit(solution)/shard_map/ppermute | solution.py:351
  45.0 4.4 %collective-permute-start.15 = (bf16[8,32,128]{2,1,0:T(8,128)(2,1)S(1)}, bf16[8,32,128]{2,1,0:T(8,128)(2,1)S(1)}, u32[]{:S(2)}, u32[]{:S(2)}) collective-permute-start(bf16[8,32,128]{2,1,0:T(8,128)(2,1)S(1)} %get-tuple-element.60), channel_id=1, source_target_pairs={{0,4},{1,5},{2,6},{3,7},{4,0},{5,1},{6,2},{7,3},{8,12},{9,13},{10,... | collective-permute-start | bytes 196616 | tf_op jit(solution)/shard_map/ppermute | solution.py:351
  46.8 2.7 %collective-permute-start.16 = (bf16[8,32,128]{2,1,0:T(8,128)(2,1)S(1)}, bf16[8,32,128]{2,1,0:T(8,128)(2,1)S(1)}, u32[]{:S(2)}, u32[]{:S(2)}) collective-permute-start(bf16[8,32,128]{2,1,0:T(8,128)(2,1)S(1)} %get-tuple-element.61), channel_id=1, source_target_pairs={{0,1},{1,0},{2,3},{3,2},{4,5},{5,4},{6,7},{7,6},{8,9},{9,8},{10,11... | collective-permute-start | bytes 196616 | tf_op jit(solution)/shard_map/ppermute | solution.py:351
